TPU v7x, 32 devices: a whole 2x2x4 slice. The times are simulated.
32 devices in a mesh: dp: 4 (over z), expert: 8 (over y, x, core).
Axes of the slice: x: 2, y: 2, z: 4, core: 2. Of those that a mesh axis runs over, the one named last changes fastest.
Arguments:
- tokens: bfloat16 [16384, 512], P(('dp', 'expert')), may hold values from -6 to 6
- cotangent: bfloat16 [16384, 512], P(('dp', 'expert')), may hold values from -9 to 9
- routes: int32 [16384, 8], P(('dp', 'expert')), may hold values from 0 to 23, all different within a row; in each aligned block of 512 rows (0 to 511, 512 to 1023, ...) at most 336 rows name the same one
- group_batch: int32 [4], replicated, may hold values from 2 to 4, as said below
- seq_lengths: int32 [4, 4], replicated, may hold values from 0 to 2048, as said below
- gains: float32 [2, 512], replicated, may hold values from 0.3 to 3.5
- gains_first: float32 [2, 512], replicated, may hold values from -0.00048828125 to 0.00048828125
- gains_second: float32 [2, 512], replicated, may hold values from 4.6670895e-10 to 1.8668358e-09
- router_weight: float32 [512, 24], replicated, may hold values from -0.109375 to 0.109375
- router_first: float32 [512, 24], replicated, may hold values from -0.0024414062 to 0.0024414062
- router_second: float32 [512, 24], replicated, may hold values from 1.3275276e-08 to 5.3101104e-08
- keyval_weight: float32 [512, 128], P('dp'), may hold values from -0.25 to 0.25
- keyval_first: float32 [512, 128], P('dp'), may hold values from -0.0014648438 to 0.0014648438
- keyval_second: float32 [512, 128], P('dp'), may hold values from 5.1856546e-09 to 2.0742618e-08
- query_weight: float32 [24, 512, 64], P('expert'), may hold values from -0.25 to 0.25
- query_first: float32 [24, 512, 64], P('expert'), may hold values from -0.0004272461 to 0.0004272461
- query_second: float32 [24, 512, 64], P('expert'), may hold values from 3.7751566e-10 to 1.5100626e-09
- output_weight: float32 [24, 64, 512], P('expert'), may hold values from -12.613446 to 12.613446
- output_first: float32 [24, 64, 512], P('expert'), may hold values from -5.722046e-06 to 5.722046e-06
- output_second: float32 [24, 64, 512], P('expert'), may hold values from 8.2970475e-14 to 3.318819e-13
- up_weight: float32 [512, 2048], P('dp'), may hold values from -0.25 to 0.25
- up_first: float32 [512, 2048], P('dp'), may hold values from -0.00012207031 to 0.00012207031
- up_second: float32 [512, 2048], P('dp'), may hold values from 3.3188192e-11 to 1.3275277e-10
- down_weight: float32 [2048, 512], P(None, 'dp'), may hold values from -0.125 to 0.125
- down_first: float32 [2048, 512], P(None, 'dp'), may hold values from -0.00021362305 to 0.00021362305
- down_second: float32 [2048, 512], P(None, 'dp'), may hold values from 1.01638836e-10 to 4.0655534e-10
Outputs:
- layer_out: bfloat16 [16384, 512], P(('dp', 'expert'))
- tokens_grad: float32 [16384, 512], P(('dp', 'expert'))
- expert_counts: int32 [24], replicated
- grad_norm: float32 [], replicated
- new_gains: float32 [2, 512], replicated
- gains_moment: float32 [2, 512], replicated
- gains_power: float32 [2, 512], replicated
- new_router: float32 [512, 24], replicated
- router_moment: float32 [512, 24], replicated
- router_power: float32 [512, 24], replicated
- new_keyval: float32 [512, 128], P('dp')
- keyval_moment: float32 [512, 128], P('dp')
- keyval_power: float32 [512, 128], P('dp')
- new_query: float32 [24, 512, 64], P('expert')
- query_moment: float32 [24, 512, 64], P('expert')
- query_power: float32 [24, 512, 64], P('expert')
- new_output: float32 [24, 64, 512], P('expert')
- output_moment: float32 [24, 64, 512], P('expert')
- output_power: float32 [24, 64, 512], P('expert')
- new_up: float32 [512, 2048], P('dp')
- up_moment: float32 [512, 2048], P('dp')
- up_power: float32 [512, 2048], P('dp')
- new_down: float32 [2048, 512], P(None, 'dp')
- down_moment: float32 [2048, 512], P(None, 'dp')
- down_power: float32 [2048, 512], P(None, 'dp')
Inputs may be any that keep to these rules, and one draw needn't show every extreme that they name: `routes`: within the rows of one device, no head expert is named by more than 336 rows. `group_batch`: each entry is 2 or 4; both values occur. `seq_lengths`: for a group with b sequences, entries 0 to b - 1 lie between 1 and 4096 div b and one of them equals 4096 div b; the entries from b on are 0.
All inputs are finite; a program needn't handle non-finite values.
Results may differ from a plain program's by a relative error of at most 0.018.
Values may be sent and summed in bfloat16 or wider, within the bound.
A program may use at most 192 MiB of HBM per device.

v0:
```python
import jax
import jax.numpy as jnp
from jax import lax
from jax.sharding import PartitionSpec as P

ADAM_STEP = 10


NORM_EPS = 1e-06
BETA_FIRST = 0.9
BETA_SECOND = 0.999
ADAM_EPS = 1e-08
CLIP_LIMIT = 1.0
MASKED = -1e30
HIGHEST = lax.Precision.HIGHEST


def seq_layout(row_ids, seq_batch, lengths):
    sequence = row_ids % seq_batch
    position = row_ids // seq_batch
    slot_ids = jnp.arange(lengths.shape[0], dtype=jnp.int32)
    row_limit = jnp.sum(
        jnp.where(sequence[:, None] == slot_ids[None, :], lengths[None, :], 0), axis=1
    )
    return (sequence, position, row_limit)


def rms_forward(values, gain_vec):
    inverse = lax.rsqrt(jnp.mean(values * values, axis=-1, keepdims=True) + NORM_EPS)
    unit_rows = values * inverse
    return (unit_rows * gain_vec, unit_rows, inverse)


def rms_backward(d_normed, gain_vec, unit_rows, inverse):
    scaled = d_normed * gain_vec
    d_values = inverse * (scaled - unit_rows * jnp.mean(scaled * unit_rows, axis=-1, keepdims=True))
    return (d_values, jnp.sum(d_normed * unit_rows, axis=0))


def adam_update(weight, gradient, first_moment, second, clip_scale, step_rate, decay_rate):
    step_grad = gradient * clip_scale
    new_first = BETA_FIRST * first_moment + (1.0 - BETA_FIRST) * step_grad
    new_second = BETA_SECOND * second + (1.0 - BETA_SECOND) * step_grad * step_grad
    first_hat = new_first / (1.0 - BETA_FIRST**ADAM_STEP)
    second_hat = new_second / (1.0 - BETA_SECOND**ADAM_STEP)
    new_weight = weight - step_rate * (
        first_hat / (jnp.sqrt(second_hat) + ADAM_EPS) + decay_rate * weight
    )
    return (new_weight, new_first, new_second)


def on_device(
    tokens,
    cotangent,
    routes,
    group_batch,
    seq_lengths,
    gains,
    gains_first,
    gains_second,
    router_weight,
    router_first,
    router_second,
    keyval_weight,
    keyval_first,
    keyval_second,
    query_weight,
    query_first,
    query_second,
    output_weight,
    output_first,
    output_second,
    up_weight,
    up_first,
    up_second,
    down_weight,
    down_first,
    down_second,
):
    tok_count = tokens.shape[0]
    model_width = tokens.shape[1]
    experts = router_weight.shape[1]
    top_count = routes.shape[1]
    head_size = query_weight.shape[2]
    capacity = 2 * tok_count * top_count // experts // 8 * 8
    expert_devs = lax.axis_size("expert")
    local_experts = experts // expert_devs
    group_rows = tok_count * expert_devs
    dp_index = lax.axis_index("dp")
    expert_index = lax.axis_index("expert")
    seq_batch = lax.dynamic_index_in_dim(group_batch, dp_index, 0, keepdims=False)
    lengths = lax.dynamic_index_in_dim(seq_lengths, dp_index, 0, keepdims=False)
    seq_span = group_rows // seq_batch
    slot_ids = jnp.arange(lengths.shape[0], dtype=jnp.int32)
    keyval_full, up_full, down_full = (
        lax.all_gather(keyval_weight.astype(jnp.bfloat16), "dp", axis=0, tiled=True),
        lax.all_gather(up_weight.astype(jnp.bfloat16), "dp", axis=0, tiled=True),
        lax.all_gather(down_weight.astype(jnp.bfloat16), "dp", axis=1, tiled=True),
    )
    router_low = router_weight.astype(jnp.bfloat16)
    query_low = query_weight.astype(jnp.bfloat16)
    output_low = output_weight.astype(jnp.bfloat16)
    tokens_wide = tokens.astype(jnp.float32)
    normed, unit_attn, inverse_attn = rms_forward(tokens_wide, gains[0])
    normed_low = normed.astype(jnp.bfloat16)
    logits = jnp.dot(normed_low, router_low, preferred_element_type=jnp.float32)
    expert_ids = jnp.arange(experts, dtype=jnp.int32)
    onehot = (routes[:, :, None] == expert_ids[None, None, :]).astype(jnp.float32)
    chosen = jnp.sum(onehot * logits[:, None, :], axis=2)
    gate_probs = jax.nn.softmax(chosen, axis=1)
    own_rows = expert_index * tok_count + jnp.arange(tok_count, dtype=jnp.int32)
    own_seq, own_pos, own_limit = seq_layout(own_rows, seq_batch, lengths)
    live_rows = (own_pos < own_limit).astype(jnp.float32)
    counts_local = jnp.sum(onehot * live_rows[:, None, None], axis=(0, 1))
    keyval_local = jnp.dot(normed_low, keyval_full, preferred_element_type=jnp.float32).astype(
        jnp.bfloat16
    )
    keyval_group = lax.all_gather(keyval_local, "expert", axis=0, tiled=True)
    key_rows = jnp.arange(group_rows, dtype=jnp.int32)
    major_to_row = key_rows % seq_span * seq_batch + key_rows // seq_span
    row_to_major = key_rows % seq_batch * seq_span + key_rows // seq_batch
    keyval_major = keyval_group[major_to_row]
    keys_major = keyval_major[:, :head_size]
    values_major = keyval_major[:, head_size:]
    key_tile = min(512, group_rows)
    slot_total = tok_count * top_count
    flat_routes = routes.reshape(slot_total)
    flat_hot = (flat_routes[:, None] == expert_ids[None, :]).astype(jnp.int32)
    slot_rank = jnp.sum((jnp.cumsum(flat_hot, axis=0) - 1) * flat_hot, axis=1)
    slot_index = flat_routes * capacity + slot_rank
    source = (
        jnp.full((experts * capacity,), slot_total, jnp.int32)
        .at[slot_index]
        .set(jnp.arange(slot_total, dtype=jnp.int32))
    )
    source_token = source // top_count
    padded_normed = jnp.concatenate([normed_low, jnp.zeros((1, model_width), jnp.bfloat16)], axis=0)
    send_tokens = padded_normed[source_token].reshape(
        expert_devs, local_experts, capacity, model_width
    )
    send_rows = jnp.where(source < slot_total, expert_index * tok_count + source_token, 0).reshape(
        expert_devs, local_experts, capacity
    )
    slot_in = send_tokens.reshape(1, experts, capacity, model_width)
    slot_rows = send_rows.reshape(1, experts, capacity)
    query_use, output_use = (
        lax.all_gather(query_low, "expert", axis=0, tiled=True),
        lax.all_gather(output_low, "expert", axis=0, tiled=True),
    )
    queries = jnp.einsum(
        "sxcd,xdh->sxch", slot_in, query_use, preferred_element_type=jnp.float32
    ).astype(jnp.bfloat16)
    flat_count = queries.shape[0] * queries.shape[1] * queries.shape[2]
    block_rows = min(512, flat_count)
    padded_count = -(-flat_count // block_rows) * block_rows
    block_count = padded_count // block_rows
    extra_rows = padded_count - flat_count
    query_flat = jnp.concatenate(
        [queries.reshape(flat_count, head_size), jnp.zeros((extra_rows, head_size), jnp.bfloat16)],
        axis=0,
    )
    rows_flat = jnp.concatenate(
        [slot_rows.reshape(flat_count), jnp.zeros((extra_rows,), jnp.int32)], axis=0
    )
    major_index = rows_flat % seq_batch * seq_span + rows_flat // seq_batch
    order = jnp.argsort(major_index, stable=True)
    index_blocks = major_index[order].reshape(block_count, block_rows)
    query_blocks = query_flat[order].reshape(block_count, block_rows, head_size)

    def unsort(sorted_rows):
        return jnp.zeros_like(sorted_rows).at[order].set(sorted_rows)[:flat_count]

    def tile_range(index_blk):
        lower = index_blk[0] // seq_span * seq_span // key_tile
        upper = index_blk[block_rows - 1] // key_tile + 1
        return (lower, upper)

    def tile_scores(query_blk, index_blk, tile):
        start = tile * key_tile
        keys_tile = lax.dynamic_slice_in_dim(keys_major, start, key_tile, 0)
        values_tile = lax.dynamic_slice_in_dim(values_major, start, key_tile, 0)
        key_index = start + jnp.arange(key_tile, dtype=jnp.int32)
        query_seq = index_blk // seq_span
        query_pos = index_blk % seq_span
        row_limit = jnp.sum(
            jnp.where(query_seq[:, None] == slot_ids[None, :], lengths[None, :], 0), axis=1
        )
        key_seq = key_index // seq_span
        key_pos = key_index % seq_span
        visible = (
            (key_seq[None, :] == query_seq[:, None])
            & (key_pos[None, :] <= query_pos[:, None])
            & (key_pos[None, :] < row_limit[:, None])
        )
        scores = jnp.where(
            visible,
            jnp.einsum("rh,uh->ru", query_blk, keys_tile, preferred_element_type=jnp.float32)
            * 0.125,
            MASKED,
        )
        return (scores, visible, keys_tile, values_tile, start)

    def forward_block(inputs):
        query_blk, index_blk = inputs
        lower, upper = tile_range(index_blk)

        def peak_step(tile, carry):
            row_peak, row_sum = carry
            scores, visible, keys_tile, values_tile, start = tile_scores(query_blk, index_blk, tile)
            new_peak = jnp.maximum(row_peak, jnp.max(scores, axis=1))
            terms = jnp.where(visible, jnp.exp(scores - new_peak[:, None]), 0.0)
            return (new_peak, row_sum * jnp.exp(row_peak - new_peak) + jnp.sum(terms, axis=1))

        start_carry = (
            jnp.full((block_rows,), MASKED, jnp.float32),
            jnp.zeros((block_rows,), jnp.float32),
        )
        row_peak, row_sum = lax.fori_loop(lower, upper, peak_step, start_carry)
        log_total = row_peak + jnp.log(row_sum)

        def value_step(tile, acc):
            scores, visible, keys_tile, values_tile, start = tile_scores(query_blk, index_blk, tile)
            prob_low = jnp.where(visible, jnp.exp(scores - log_total[:, None]), 0.0).astype(
                jnp.bfloat16
            )
            return acc + jnp.dot(prob_low, values_tile, preferred_element_type=jnp.float32)

        attended_blk = lax.fori_loop(
            lower, upper, value_step, jnp.zeros((block_rows, head_size), jnp.float32)
        )
        return (attended_blk.astype(jnp.bfloat16), log_total)

    attended_sorted, log_totals = lax.map(forward_block, (query_blocks, index_blocks))
    attended = unsort(attended_sorted.reshape(padded_count, head_size)).reshape(queries.shape)
    branch = jnp.einsum(
        "sxch,xhd->sxcd", attended, output_use, preferred_element_type=jnp.float32
    ).astype(jnp.bfloat16)
    branch_slot = branch.reshape(experts * capacity, model_width)[slot_index].reshape(
        tok_count, top_count, model_width
    )
    attn_out = jnp.einsum(
        "tk,tkd->td", gate_probs, branch_slot, precision=HIGHEST, preferred_element_type=jnp.float32
    )
    mixed_rows = tokens_wide + attn_out
    normed_ffn, unit_ffn, inverse_ffn = rms_forward(mixed_rows, gains[1])
    ffn_low = normed_ffn.astype(jnp.bfloat16)
    up_proj = jnp.dot(ffn_low, up_full, preferred_element_type=jnp.float32)
    hidden_wide, gelu_back = jax.vjp(jax.nn.gelu, up_proj)
    hidden_low = hidden_wide.astype(jnp.bfloat16)
    result = (
        mixed_rows + jnp.dot(hidden_low, down_full, preferred_element_type=jnp.float32)
    ).astype(jnp.bfloat16)
    d_hidden = jnp.einsum("td,fd->tf", cotangent, down_full, preferred_element_type=jnp.float32)
    d_up = gelu_back(d_hidden)[0].astype(jnp.bfloat16)
    grad_down = jnp.einsum("tf,td->fd", hidden_low, cotangent, preferred_element_type=jnp.float32)
    grad_up = jnp.einsum("td,tf->df", ffn_low, d_up, preferred_element_type=jnp.float32)
    d_ffn = jnp.einsum("tf,df->td", d_up, up_full, preferred_element_type=jnp.float32)
    ffn_back, gain_ffn = rms_backward(d_ffn, gains[1], unit_ffn, inverse_ffn)
    d_mixed = cotangent.astype(jnp.float32) + ffn_back
    d_gate = jnp.einsum(
        "tkd,td->tk", branch_slot, d_mixed, precision=HIGHEST, preferred_element_type=jnp.float32
    )
    d_branch = (
        (gate_probs[:, :, None] * d_mixed[:, None, :])
        .astype(jnp.bfloat16)
        .reshape(slot_total, model_width)
    )
    padded_branch = jnp.concatenate([d_branch, jnp.zeros((1, model_width), jnp.bfloat16)], axis=0)
    d_send = padded_branch[source].reshape(expert_devs, local_experts, capacity, model_width)
    d_incoming = d_send.reshape(1, experts, capacity, model_width)
    d_attended = jnp.einsum(
        "sxcd,xhd->sxch", d_incoming, output_use, preferred_element_type=jnp.float32
    ).astype(jnp.bfloat16)
    output_part = jnp.einsum(
        "sxch,sxcd->xhd", attended, d_incoming, preferred_element_type=jnp.float32
    )
    d_att_flat = jnp.concatenate(
        [
            d_attended.reshape(flat_count, head_size),
            jnp.zeros((extra_rows, head_size), jnp.bfloat16),
        ],
        axis=0,
    )
    d_att_blocks = d_att_flat[order].reshape(block_count, block_rows, head_size)

    def backward_block(running, inputs):
        query_blk, index_blk, log_blk, d_att_blk = inputs
        lower, upper = tile_range(index_blk)

        def delta_step(tile, acc):
            scores, visible, keys_tile, values_tile, start = tile_scores(query_blk, index_blk, tile)
            prob_wide = jnp.where(visible, jnp.exp(scores - log_blk[:, None]), 0.0)
            d_probs = jnp.einsum(
                "rh,uh->ru", d_att_blk, values_tile, preferred_element_type=jnp.float32
            )
            return acc + jnp.sum(prob_wide * d_probs, axis=1)

        row_delta = lax.fori_loop(lower, upper, delta_step, jnp.zeros((block_rows,), jnp.float32))

        def grad_step(tile, carry):
            d_keys, d_values, d_query = carry
            scores, visible, keys_tile, values_tile, start = tile_scores(query_blk, index_blk, tile)
            prob_wide = jnp.where(visible, jnp.exp(scores - log_blk[:, None]), 0.0)
            d_probs = jnp.einsum(
                "rh,uh->ru", d_att_blk, values_tile, preferred_element_type=jnp.float32
            )
            d_scores = (prob_wide * (d_probs - row_delta[:, None])).astype(jnp.bfloat16)
            d_query = d_query + jnp.dot(d_scores, keys_tile, preferred_element_type=jnp.float32)
            key_part = (
                jnp.einsum("ru,rh->uh", d_scores, query_blk, preferred_element_type=jnp.float32)
                * 0.125
            )
            value_part = jnp.einsum(
                "ru,rh->uh",
                prob_wide.astype(jnp.bfloat16),
                d_att_blk,
                preferred_element_type=jnp.float32,
            )
            d_keys = lax.dynamic_update_slice_in_dim(
                d_keys, lax.dynamic_slice_in_dim(d_keys, start, key_tile, 0) + key_part, start, 0
            )
            d_values = lax.dynamic_update_slice_in_dim(
                d_values,
                lax.dynamic_slice_in_dim(d_values, start, key_tile, 0) + value_part,
                start,
                0,
            )
            return (d_keys, d_values, d_query)

        d_keys, d_values, d_query = lax.fori_loop(
            lower,
            upper,
            grad_step,
            (running[0], running[1], jnp.zeros((block_rows, head_size), jnp.float32)),
        )
        return ((d_keys, d_values), (d_query * 0.125).astype(jnp.bfloat16))

    zero_rows = jnp.zeros((group_rows, head_size), jnp.float32)
    (keys_grad, values_grad), d_query_sorted = lax.scan(
        backward_block,
        (zero_rows, zero_rows),
        (query_blocks, index_blocks, log_totals, d_att_blocks),
    )
    d_queries = unsort(d_query_sorted.reshape(padded_count, head_size)).reshape(queries.shape)
    query_part = jnp.einsum(
        "sxcd,sxch->xdh", slot_in, d_queries, preferred_element_type=jnp.float32
    )
    d_slot_out = jnp.einsum(
        "sxch,xdh->sxcd", d_queries, query_use, preferred_element_type=jnp.float32
    ).astype(jnp.bfloat16)
    slot_grads = d_slot_out.reshape(experts * capacity, model_width)[slot_index].reshape(
        tok_count, top_count, model_width
    )
    slot_sum = jnp.sum(slot_grads, axis=1, dtype=jnp.float32)
    keyval_grad_rows = jnp.concatenate([keys_grad, values_grad], axis=1)[row_to_major]
    keyval_sum = lax.psum_scatter(
        keyval_grad_rows.astype(jnp.bfloat16), "expert", scatter_dimension=0, tiled=True
    )
    d_chosen = gate_probs * (d_gate - jnp.sum(gate_probs * d_gate, axis=1, keepdims=True))
    d_logits = jnp.sum(onehot * d_chosen[:, :, None], axis=1).astype(jnp.bfloat16)
    d_normed = (
        slot_sum
        + jnp.einsum("tc,dc->td", keyval_sum, keyval_full, preferred_element_type=jnp.float32)
        + jnp.einsum("te,de->td", d_logits, router_low, preferred_element_type=jnp.float32)
    )
    grad_keyval = jnp.einsum(
        "td,tc->dc", normed_low, keyval_sum, preferred_element_type=jnp.float32
    )
    grad_router = jnp.einsum("td,te->de", normed_low, d_logits, preferred_element_type=jnp.float32)
    attn_back, gain_attn = rms_backward(d_normed, gains[0], unit_attn, inverse_attn)
    tokens_grad = d_mixed + attn_back
    keyval_part, up_part, down_part = (
        lax.psum_scatter(
            grad_keyval.astype(jnp.bfloat16), "dp", scatter_dimension=0, tiled=True
        ).astype(jnp.float32),
        lax.psum_scatter(
            grad_up.astype(jnp.bfloat16), "dp", scatter_dimension=0, tiled=True
        ).astype(jnp.float32),
        lax.psum_scatter(
            grad_down.astype(jnp.bfloat16), "dp", scatter_dimension=1, tiled=True
        ).astype(jnp.float32),
    )
    keyval_total, up_total, down_total = (
        lax.psum(keyval_part.astype(jnp.bfloat16), "expert").astype(jnp.float32),
        lax.psum(up_part.astype(jnp.bfloat16), "expert").astype(jnp.float32),
        lax.psum(down_part.astype(jnp.bfloat16), "expert").astype(jnp.float32),
    )
    query_owned, output_owned = (
        lax.psum_scatter(query_part, "expert", scatter_dimension=0, tiled=True),
        lax.psum_scatter(output_part, "expert", scatter_dimension=0, tiled=True),
    )
    query_total, output_total = (
        lax.psum(query_owned.astype(jnp.bfloat16), "dp").astype(jnp.float32),
        lax.psum(output_owned.astype(jnp.bfloat16), "dp").astype(jnp.float32),
    )
    router_total, gains_total, counts_all = lax.psum(
        (grad_router, jnp.stack([gain_attn, gain_ffn]), counts_local), ("dp", "expert")
    )
    dense_squares = (
        jnp.sum(keyval_total * keyval_total)
        + jnp.sum(up_total * up_total)
        + jnp.sum(down_total * down_total)
    ) / expert_devs
    expert_squares = (
        jnp.sum(query_total * query_total) + jnp.sum(output_total * output_total)
    ) / lax.axis_size("dp")
    total_squares = (
        lax.psum(dense_squares + expert_squares, ("dp", "expert"))
        + jnp.sum(router_total * router_total)
        + jnp.sum(gains_total * gains_total)
    )
    grad_norm = jnp.sqrt(total_squares)
    clip_scale = CLIP_LIMIT / jnp.maximum(grad_norm, CLIP_LIMIT)
    gains_out = adam_update(gains, gains_total, gains_first, gains_second, clip_scale, 0.7, 0.0)
    router_out = adam_update(
        router_weight, router_total, router_first, router_second, clip_scale, 0.03, 0.1
    )
    keyval_out = adam_update(
        keyval_weight, keyval_total, keyval_first, keyval_second, clip_scale, 0.06, 0.1
    )
    query_out = adam_update(
        query_weight, query_total, query_first, query_second, clip_scale, 0.06, 0.1
    )
    output_out = adam_update(
        output_weight, output_total, output_first, output_second, clip_scale, 2.0, 0.1
    )
    up_out = adam_update(up_weight, up_total, up_first, up_second, clip_scale, 0.06, 0.1)
    down_out = adam_update(down_weight, down_total, down_first, down_second, clip_scale, 0.03, 0.1)
    return (
        result,
        tokens_grad,
        counts_all.astype(jnp.int32),
        grad_norm,
        gains_out[0],
        gains_out[1],
        gains_out[2],
        router_out[0],
        router_out[1],
        router_out[2],
        keyval_out[0],
        keyval_out[1],
        keyval_out[2],
        query_out[0],
        query_out[1],
        query_out[2],
        output_out[0],
        output_out[1],
        output_out[2],
        up_out[0],
        up_out[1],
        up_out[2],
        down_out[0],
        down_out[1],
        down_out[2],
    )


def solution(mesh):
    return jax.shard_map(
        on_device,
        mesh=mesh,
        in_specs=(
            P(("dp", "expert"), None),
            P(("dp", "expert"), None),
            P(("dp", "expert"), None),
            P(),
            P(),
            P(),
            P(),
            P(),
            P(),
            P(),
            P(),
            P("dp", None),
            P("dp", None),
            P("dp", None),
            P("expert", None, None),
            P("expert", None, None),
            P("expert", None, None),
            P("expert", None, None),
            P("expert", None, None),
            P("expert", None, None),
            P("dp", None),
            P("dp", None),
            P("dp", None),
            P(None, "dp"),
            P(None, "dp"),
            P(None, "dp"),
        ),
        out_specs=(
            P(("dp", "expert"), None),
            P(("dp", "expert"), None),
            P(),
            P(),
            P(),
            P(),
            P(),
            P(),
            P(),
            P(),
            P("dp", None),
            P("dp", None),
            P("dp", None),
            P("expert", None, None),
            P("expert", None, None),
            P("expert", None, None),
            P("expert", None, None),
            P("expert", None, None),
            P("expert", None, None),
            P("dp", None),
            P("dp", None),
            P("dp", None),
            P(None, "dp"),
            P(None, "dp"),
            P(None, "dp"),
        ),
        check_vma=False,
    )
```

profile of v0, /device:TPU:0, one launch (start us, length us, event | category | flops | bytes accessed | tf_op | source)
XLA Modules:
  0.0 1526.0 jit_solution(8735590643908346715)
XLA Ops:
  10.3 15.0 all_gather.19
  38.0 5.6 compare_select_fusion
  44.6 6.9 reduce-window.6
  52.8 15.8 %scatter_custom_fusion = s32[8064]{0:T(1024)S(1)} fusion(s32[4096]{0:T(1024)S(1)} %bitcast.290, s32[4096]{0:T(1024)S(1)} %iota.101, s32[]{:T(128)} %constant.583.clone.1), kind=kCustom, calls=%fused_computation.318 | custom fusion | bytes 32260 | tf_op jit(solution)/shard_map/scatter | solution.py:134
  70.0 6.8 sort.17
  77.4 45.5 %gather_fusion = s32[8192]{0:T(1024)S(1)} fusion(s32[8192]{0:T(1024)S(1)} %get-tuple-element.1711, s32[8192]{0:T(1024)S(1)} %get-tuple-element.1703), kind=kCustom, calls=%fused_computation | custom fusion | bytes 98304 | tf_op jit(solution)/shard_map/gather | solution.py:167
  123.5 23.6 %gather_fusion.1 = bf16[8064,512]{1,0:T(8,128)(2,1)} fusion(bf16[513,512]{1,0:T(8,128)(2,1)S(1)} %concatenate.19, s32[8192]{0:T(1024)S(1)} %pad_clamp_fusion.1), kind=kCustom, calls=%fused_computation.1 | custom fusion | bytes 16547328 | tf_op jit(solution)/shard_map/gather | solution.py:138
  147.0 12.4 gather_fusion.3
  160.8 6.1 fusion.113
  171.2 29.4 %gather_fusion.2 = bf16[8192,64]{1,0:T(8,128)(2,1)} fusion(bf16[8192,64]{1,0:T(8,128)(2,1)S(1)} %concatenate.20, s32[8192]{0:T(1024)S(1)} %get-tuple-element.1703), kind=kCustom, calls=%fused_computation.2 | custom fusion | bytes 2129920 | tf_op jit(solution)/shard_map/gather | solution.py:168
  200.8 190.9 %while.155 = (s32[]{:T(128)}, bf16[16,512,64]{1,2,0:T(8,128)(2,1)S(1)}, f32[16,512]{1,0:T(8,128)}, s32[16,512]{1,0:T(8,128)S(1)}, s32[]{:T(128)}, /*index=5*/s32...) while((s32[]{:T(128)}, ...), condition=%wide.region_18.19_spmd.clone.clone, body=%wide.region_9.18_spmd.clone.clone.sunk | while | flops 107589688 | bytes 3525179 | solution.py:233
  393.5 32.6 %scatter_custom_fusion.1 = bf16[8192,64]{1,0:T(8,128)(2,1)} fusion(s32[8192]{0:T(1024)} %get-tuple-element.1704, bf16[8192,64]{1,0:T(8,128)(2,1)} %bitcast.285, bf16[]{:T(256)} %constant.582.clone.1), kind=kCustom, calls=%fused_computation.240 | custom fusion | bytes 1049088 | tf_op jit(solution)/shard_map/scatter | solution.py:171
  427.9 7.6 convolution_convert_fusion.1
  435.5 21.9 %gather_fusion.4 = bf16[4096,512]{1,0:T(8,128)(2,1)} fusion(bf16[8064,512]{1,0:T(8,128)(2,1)} %bitcast.267, s32[4096]{0:T(1024)S(1)} %broadcast_clamp_fusion.1), kind=kCustom, calls=%fused_computation.4 | custom fusion | bytes 8404992 | tf_op jit(solution)/shard_map/gather | solution.py:238
  457.4 5.9 fusion.107
  469.0 7.5 fusion.104
  482.7 27.2 %gather_fusion.5 = bf16[8064,512]{1,0:T(8,128)(2,1)} fusion(bf16[4097,512]{1,0:T(8,128)(2,1)} %concatenate.21, s32[8192]{0:T(1024)S(1)} %get-tuple-element.1712), kind=kCustom, calls=%fused_computation.5 | custom fusion | bytes 16547328 | tf_op jit(solution)/shard_map/gather | solution.py:269
  509.9 6.7 fusion.114
  522.2 29.3 %gather_fusion.6 = bf16[8192,64]{1,0:T(8,128)(2,1)} fusion(bf16[8192,64]{1,0:T(8,128)(2,1)S(1)} %concatenate.22, s32[8192]{0:T(1024)S(1)} %get-tuple-element.1703), kind=kCustom, calls=%fused_computation.6 | custom fusion | bytes 2129920 | tf_op jit(solution)/shard_map/gather | solution.py:284
  553.7 244.8 %while.158 = (s32[]{:T(128)}, f32[4096,64]{0,1:T(8,128)S(1)}, f32[4096,64]{0,1:T(8,128)}, bf16[16,512,64]{1,2,0:T(8,128)(2,1)}, s32[16,512]{1,0:T(8,128)S(1)}, /...) while((s32[]{:T(128)}, f32[4096,64]{0,1:T(8,128)S(1)}, ...), condition=%wide.region_30.31_spmd.clone.clone, body=%wide.region_22.30_spmd.clone.clone.sunk | while | flops 241412640 | bytes 9520831 | solution.py:339
  562.8 5.5 while.162
  578.1 5.5 while.162
  593.4 5.5 while.162
  608.7 5.5 while.162
  624.0 5.5 while.162
  639.3 5.5 while.162
  654.6 5.5 while.162
  669.9 5.5 while.162
  685.2 5.5 while.162
  700.5 5.5 while.162
  731.2 5.5 while.162
  761.8 5.5 while.162
  777.1 5.5 while.162
  803.4 15.0 gather_fusion.8
  832.8 310.9 %reduce-scatter.9.cloned.1.call-done = bf16[512,128]{1,0:T(8,128)(2,1)} async-done(((bf16[4096,128]{1,0:T(8,128)(2,1)}), bf16[512,128]{1,0:T(8,128)(2,1)}) %reduce-scatter.9.cloned.1.call-update) | async-done | bytes 131088 | tf_op jit(solution)/shard_map/reduce_scatter | solution.py:356
  1145.7 6.9 fusion.198
  1155.6 22.9 %scatter_custom_fusion.2 = bf16[8192,64]{1,0:T(8,128)(2,1)} fusion(s32[8192]{0:T(1024)} %get-tuple-element.1704, bf16[8192,64]{1,0:T(8,128)(2,1)} %bitcast.284, bf16[]{:T(256)} %constant.582.clone.1), kind=kCustom, calls=%fused_computation.238 | custom fusion | bytes 1049088 | tf_op jit(solution)/shard_map/scatter | solution.py:171
  1180.3 7.0 fusion.199
  1188.3 10.0 fusion.105
  1198.4 6.9 convolution_convert_fusion
  1205.3 22.1 %gather_fusion.7 = bf16[4096,512]{1,0:T(8,128)(2,1)} fusion(bf16[8064,512]{1,0:T(8,128)(2,1)} %bitcast.266, s32[4096]{0:T(1024)S(1)} %copy-done.39), kind=kCustom, calls=%fused_computation.7 | custom fusion | bytes 8404992 | tf_op jit(solution)/shard_map/gather | solution.py:351
  1242.6 14.4 reduce-scatter.11.cloned.1.call-done
  1257.0 22.9 %psum.64 = bf16[128,128]{1,0:T(8,128)(2,1)S(1)} all-reduce(bf16[128,128]{1,0:T(8,128)(2,1)} %reduce-scatter.11.cloned.1.call-done), channel_id=1, replica_groups=mesh['dp'=4,'expert'=8] {'expert'}, use_global_device_ids=true, to_apply=%region_41.42 | all-reduce | flops 16384 | bytes 65536 | tf_op jit(solution)/shard_map/psum | solution.py:384
  1279.9 25.2 %reduce-scatter.17.cloned.1.call-done = f32[3,64,512]{2,1,0:T(8,128)} async-done(((f32[24,64,512]{2,1,0:T(8,128)}), f32[3,64,512]{2,1,0:T(8,128)}) %reduce-scatter.17.cloned.1.call-update) | async-done | bytes 393232 | tf_op jit(solution)/shard_map/reduce_scatter | solution.py:390
  1306.7 48.0 %reduce-scatter.15.cloned.1.call-done = f32[3,512,64]{1,2,0:T(8,128)} async-done(((f32[24,512,64]{1,2,0:T(8,128)}), f32[3,512,64]{1,2,0:T(8,128)}) %reduce-scatter.15.cloned.1.call-update) | async-done | bytes 393232 | tf_op jit(solution)/shard_map/reduce_scatter | solution.py:389
  1357.0 58.4 %all-reduce.11.cloned.1.call-done = (bf16[128,2048]{1,0:T(8,128)(2,1)}, bf16[2048,128]{1,0:T(8,128)(2,1)}) async-done(((bf16[128,2048]{1,0:T(8,128)(2,1)}, bf16[2048,128]{1,0:T(8,128)(2,1)}), (bf16[128,2048]{1,0:T(8,128)(2,1)}, bf16[2048,128]{1,0:T(8,128)(2,1)})) %all-reduce.11.cloned.1.call-update) | async-done | bytes 1048592 | tf_op jit(solution)/shard_map/psum | solution.py:385
  1421.2 33.4 %all-reduce.13.cloned.1.call-done = (bf16[3,512,64]{1,2,0:T(8,128)(2,1)}, bf16[3,64,512]{2,1,0:T(8,128)(2,1)}) async-done(((bf16[3,512,64]{1,2,0:T(8,128)(2,1)}, bf16[3,64,512]{2,1,0:T(8,128)(2,1)}), (bf16[3,512,64]{1,2,0:T(8,128)(2,1)}, bf16[3,64,512]{2,1,0:T(8,128)(2,1)})) %all-reduce.13.cloned.1.call-update) | async-done | bytes 393232 | tf_op jit(solution)/shard_map/psum | solution.py:393
  1459.2 40.6 %all-reduce.5 = (f32[24]{0:T(128)S(1)}, f32[]{:T(128)}, f32[512,24]{0,1:T(8,128)S(1)}, f32[2,512]{1,0:T(2,128)S(1)}) all-reduce(f32[24]{0:T(128)S(1)} %get-tuple-element.1459, f32[]{:T(128)S(6)} %add.785, f32[512,24]{0,1:T(8,128)} %fusion.200, f32[2,512]{1,0:T(2,128)S(1)} %pad_maximum_fusion.1), channel_id=1, replica_groups=mesh['dp'=4,'expert'=8] {'dp','expert'}, use_global_device_ids=true, to_apply=%region_39.40 | all-reduce | flops 13337 | bytes 106696 | tf_op jit(solution)/shard_map/psum | solution.py:396
  (1070 shorter events, 519.9 us)
Async XLA Ops:
  7.2 30.8 %copy-start = (s32[4,4]{1,0:T(4,128)S(1)}, s32[4,4]{1,0:T(4,128)}, u32[]{:S(2)}) copy-start(s32[4,4]{1,0:T(4,128)} %param.42) | copy-start | bytes 196
  7.2 24.0 %copy-start.11 = (f32[2048,128]{1,0:T(8,128)S(1)}, f32[2048,128]{1,0:T(8,128)}, u32[]{:S(2)}) copy-start(f32[2048,128]{1,0:T(8,128)} %param.61) | copy-start | bytes 3145732
  7.2 24.9 %copy-start.13 = (f32[128,2048]{1,0:T(8,128)S(1)}, f32[128,2048]{1,0:T(8,128)}, u32[]{:S(2)}) copy-start(f32[128,2048]{1,0:T(8,128)} %param.58) | copy-start | bytes 3145732
  7.2 25.9 %copy-start.54 = (s32[4]{0:T(128)S(1)}, s32[4]{0:T(128)}, u32[]{:S(2)}) copy-start(s32[4]{0:T(128)} %param.41) | copy-start | bytes 52
  7.3 29.1 %copy-start.35 = (s32[512,8]{0,1:T(8,128)S(1)}, s32[512,8]{0,1:T(8,128)}, u32[]{:S(2)}) copy-start(s32[512,8]{0,1:T(8,128)} %param.40) | copy-start | bytes 49156
  7.3 139.7 %all-gather.8.cloned.1.call-start = ((), (), s32[]{:S(2)}) async-start(), calls=%async_computation.7 | async-start | bytes 1179648 | tf_op jit(solution)/shard_map/all_gather | solution.py:118
  8.7 28.0 %copy-start.45 = (f32[512]{0:T(512)}, f32[512]{0:T(512)S(1)}, u32[]{:S(2)}) copy-start(f32[512]{0:T(512)S(1)} %add_rsqrt_fusion.1) | copy-start | bytes 6148
  9.5 27.2 %copy-start.47 = (f32[1,512]{1,0:T(1,128)}, f32[1,512]{1,0:T(1,128)S(1)}, u32[]{:S(2)}) copy-start(f32[1,512]{1,0:T(1,128)S(1)} %get-tuple-element.1706) | copy-start | bytes 6148
  25.4 11.5 copy-start.31
  26.7 96.7 %copy-start.4 = (bf16[512,512]{1,0:T(8,128)(2,1)}, bf16[512,512]{1,0:T(8,128)(2,1)S(1)}, u32[]{:S(2)}) copy-start(bf16[512,512]{1,0:T(8,128)(2,1)S(1)} %fusion.122) | copy-start | bytes 1572868
  27.6 133.1 %all-gather.6.cloned.1.call-start = ((), (), s32[]{:S(2)}) async-start(), calls=%async_computation.6 | async-start | bytes 1769472 | tf_op jit(solution)/shard_map/all_gather | solution.py:147
  29.4 398.4 %all-gather.10.cloned.1.call-start = ((), (), s32[]{:S(2)}) async-start(), calls=%async_computation.8 | async-start | bytes 1769472 | tf_op jit(solution)/shard_map/all_gather | solution.py:148
  31.2 432.4 %all-gather.14.cloned.1.call-start = ((), (), s32[]{:S(2)}) async-start(), calls=%async_computation.10 | async-start | bytes 2621440 | tf_op jit(solution)/shard_map/all_gather | solution.py:98
  32.1 436.8 %all-gather.12.cloned.1.call-start = ((), (), s32[]{:S(2)}) async-start(), calls=%async_computation.9 | async-start | bytes 2621440 | tf_op jit(solution)/shard_map/all_gather | solution.py:97
  33.1 1110.7 %reduce-scatter.9.cloned.1.call-start = ((), (), s32[]{:S(2)}) async-start(), calls=%async_computation.11 | async-start | bytes 1179648 | tf_op jit(solution)/shard_map/reduce_scatter | solution.py:356
  37.2 7.1 copy-start.28
  37.2 7.0 copy-start.40
  52.8 382.7 %copy-start.38 = (s32[4096]{0:T(1024)}, s32[4096]{0:T(1024)S(1)}, u32[]{:S(2)}) copy-start(s32[4096]{0:T(1024)S(1)} %broadcast_clamp_fusion.1) | copy-start | bytes 49156
  427.8 7.7 copy-start.2
  463.5 14.9 copy-start.15
  469.0 7.5 copy-start.53
  482.7 27.2 %copy-start.10 = (bf16[24,64,512]{2,1,0:T(8,128)(2,1)S(1)}, bf16[24,64,512]{2,1,0:T(8,128)(2,1)}, u32[]{:S(2)}) copy-start(bf16[24,64,512]{2,1,0:T(8,128)(2,1)} %all-gather.10.cloned.1.call-done) | copy-start | bytes 4718596
  803.4 15.1 copy-start.18
  818.4 420.7 %reduce-scatter.19.cloned.1.call-start = ((), (), s32[]{:S(2)}) async-start(), calls=%async_computation.16 | async-start | bytes 2621440
  827.9 315.9 %copy-start.5 = (bf16[512,512]{1,0:T(8,128)(2,1)S(1)}, bf16[512,512]{1,0:T(8,128)(2,1)}, u32[]{:S(2)}) copy-start(bf16[512,512]{1,0:T(8,128)(2,1)} %copy-done.4) | copy-start | bytes 1572868
  827.9 317.9 %copy-start.3 = (bf16[8064,64]{1,0:T(8,128)(2,1)S(1)}, bf16[8064,64]{1,0:T(8,128)(2,1)}, u32[]{:S(2)}) copy-start(bf16[8064,64]{1,0:T(8,128)(2,1)} %copy-done.2) | copy-start | bytes 3096580
  827.9 413.3 %reduce-scatter.13.cloned.1.call-start = ((), (), s32[]{:S(2)}) async-start(), calls=%async_computation.13 | async-start | bytes 2621440 | tf_op jit(solution)/shard_map/reduce_scatter | solution.py:376
  832.7 424.2 %reduce-scatter.11.cloned.1.call-start = ((), (), s32[]{:S(2)}) async-start(), calls=%async_computation.12 | async-start | bytes 163840 | tf_op jit(solution)/shard_map/reduce_scatter | solution.py:373
  1145.7 159.3 %reduce-scatter.17.cloned.1.call-start = ((), (), s32[]{:S(2)}) async-start(), calls=%async_computation.15 | async-start | bytes 3538944 | tf_op jit(solution)/shard_map/reduce_scatter | solution.py:390
  1152.7 202.0 %reduce-scatter.15.cloned.1.call-start = ((), (), s32[]{:S(2)}) async-start(), calls=%async_computation.14 | async-start | bytes 3538944 | tf_op jit(solution)/shard_map/reduce_scatter | solution.py:389
  1187.3 228.1 %all-reduce.11.cloned.1.call-start = ((), (), s32[]{:S(2)}) async-start(), calls=%async_computation.17 | async-start | bytes 2097152 | tf_op jit(solution)/shard_map/psum | solution.py:385
  1198.4 6.9 copy-start.39
  1205.3 22.1 %copy-start.29 = (f32[512,8]{0,1:T(8,128)S(1)}, f32[512,8]{0,1:T(8,128)}, u32[]{:S(2)}) copy-start(f32[512,8]{0,1:T(8,128)} %copy-done.28) | copy-start | bytes 49156
  1205.3 22.1 %copy-start.41 = (f32[512]{0:T(512)S(1)}, f32[512]{0:T(512)}, u32[]{:S(2)}) copy-start(f32[512]{0:T(512)} %copy-done.40) | copy-start | bytes 6148
  1205.3 22.1 %copy-start.44 = (f32[512]{0:T(512)S(1)}, f32[512]{0:T(512)}, u32[]{:S(2)}) copy-start(f32[512]{0:T(512)} %copy-done.43) | copy-start | bytes 6148
  1205.3 22.2 %copy-start.36 = (s32[512,8]{0,1:T(8,128)S(1)}, s32[512,8]{0,1:T(8,128)}, u32[]{:S(2)}) copy-start(s32[512,8]{0,1:T(8,128)} %param.40) | copy-start | bytes 49156
  1241.2 262.5 %copy-start.49 = (f32[2,512]{1,0:T(2,128)S(1)}, f32[2,512]{1,0:T(2,128)}, u32[]{:S(2)}) copy-start(f32[2,512]{1,0:T(2,128)} %param.43) | copy-start | bytes 12292
  1241.2 262.5 %copy-start.50 = (f32[2,512]{1,0:T(2,128)S(1)}, f32[2,512]{1,0:T(2,128)}, u32[]{:S(2)}) copy-start(f32[2,512]{1,0:T(2,128)} %param.44) | copy-start | bytes 12292
  1241.2 262.5 %copy-start.51 = (f32[2,512]{1,0:T(2,128)S(1)}, f32[2,512]{1,0:T(2,128)}, u32[]{:S(2)}) copy-start(f32[2,512]{1,0:T(2,128)} %param.45) | copy-start | bytes 12292
  1241.2 264.6 %copy-start.37 = (f32[128,128]{1,0:T(8,128)S(1)}, f32[128,128]{1,0:T(8,128)}, u32[]{:S(2)}) copy-start(f32[128,128]{1,0:T(8,128)} %param.49) | copy-start | bytes 196612
  1241.2 266.1 %copy-start.22 = (f32[3,64,512]{2,1,0:T(8,128)S(1)}, f32[3,64,512]{2,1,0:T(8,128)}, u32[]{:S(2)}) copy-start(f32[3,64,512]{2,1,0:T(8,128)} %param.55) | copy-start | bytes 1179652
  1241.2 266.1 %copy-start.33 = (f32[3,64,512]{2,1,0:T(8,128)S(1)}, f32[3,64,512]{2,1,0:T(8,128)}, u32[]{:S(2)}) copy-start(f32[3,64,512]{2,1,0:T(8,128)} %param.56) | copy-start | bytes 1179652
  1241.2 213.4 %all-reduce.13.cloned.1.call-start = ((), (), s32[]{:S(2)}) async-start(), calls=%async_computation.18 | async-start | bytes 786432 | tf_op jit(solution)/shard_map/psum | solution.py:393
  1242.6 264.8 %copy-start.34 = (f32[3,64,512]{2,1,0:T(8,128)S(1)}, f32[3,64,512]{2,1,0:T(8,128)}, u32[]{:S(2)}) copy-start(f32[3,64,512]{2,1,0:T(8,128)} %param.57) | copy-start | bytes 1179652
  1242.6 266.9 %copy-start.23 = (f32[3,512,64]{1,2,0:T(8,128)S(1)}, f32[3,512,64]{1,2,0:T(8,128)}, u32[]{:S(2)}) copy-start(f32[3,512,64]{1,2,0:T(8,128)} %param.52) | copy-start | bytes 1179652
  1306.7 205.4 %copy-start.12 = (f32[2048,128]{1,0:T(8,128)S(1)}, f32[2048,128]{1,0:T(8,128)}, u32[]{:S(2)}) copy-start(f32[2048,128]{1,0:T(8,128)} %param.61) | copy-start | bytes 3145732
  1415.4 96.7 %copy-start.21 = (bf16[2048,128]{1,0:T(8,128)(2,1)S(1)}, bf16[2048,128]{1,0:T(8,128)(2,1)}, u32[]{:S(2)}) copy-start(bf16[2048,128]{1,0:T(8,128)(2,1)} %get-tuple-element.1648) | copy-start | bytes 1572868
  1509.5 6.4 copy-start.26
  (21 other events, 88.0 us)
Sparse Core Ops, SparseCore 0:
  27.8 24.8 all-gather.7
  55.2 27.2 all-gather.5
  84.9 25.6 all-gather.9
  112.6 46.2 all-gather.13
  160.9 44.1 all-gather.11
  818.6 325.1 reduce-scatter.8
  1146.0 43.8 reduce-scatter.18
  1192.3 43.2 reduce-scatter.12
  1238.4 18.5 reduce-scatter.10
  1260.6 44.4 reduce-scatter.16
  1308.4 46.2 reduce-scatter.14
  1358.6 56.7 all-reduce.10
  1418.5 36.1 all-reduce.12
where the time goes:
time: 1540 us; the launch traced here: 1530 us
  waiting for transfers between devices  491 us (32%)
  local copies, waits for them, and re-layouts  418 us (27%)
  matrix products  248 us (16%)
  loops' own time  152 us (10%)
  other arithmetic  113 us (7%)
  blocking collectives  78.6 us (5%)
  between operations  24.8 us (2%)
    reduce_scatter x1, waiting for transfers between devices, on_device(): lax.psum_scatter(keyval_grad_rows.astype(jnp.bfloat16), 'expert', scatter...  311 us
    another operation x1, loops' own time, on_device(): lax.map(forward_block, (query_blocks, index_blocks))  74.8 us
    another operation x1, loops' own time, on_device(): lax.scan(backward_block, (zero_rows, zero_rows), (query_blocks, index_blo...  74.1 us
    dot_general x48, matrix products, tile_scores(): jnp.einsum('rh,uh->ru', query_blk, keys_tile, preferred_element_type=jnp....  67.4 us
    psum x1, waiting for transfers between devices, on_device(): lax.psum(up_part.astype(jnp.bfloat16), 'expert').astype(jnp.float32)  58.4 us
    scatter x2, local copies, waits for them, and re-layouts, unsort(): return jnp.zeros_like(sorted_rows).at[order].set(sorted_rows)[:flat_count]  55.5 us
    reduce_scatter x1, waiting for transfers between devices, on_device(): lax.psum_scatter(query_part, 'expert', scatter_dimension=0, tiled=True)  48 us
    gather x1, local copies, waits for them, and re-layouts, on_device(): index_blocks = major_index[order].reshape(block_count, block_rows)  45.5 us
  transfers between devices with their start and end apart: 13, of which 6 were waited for; matrix products, arithmetic and copies ran while one was open for 32% of the time, Pallas kernels for 0%

commit v1 on v0

v1 whole, which is shorter than its diff:
```python
import math

import jax
import jax.numpy as jnp
from jax import lax
from jax.experimental import pallas as pl
from jax.experimental.pallas import tpu as pltpu
from jax.sharding import PartitionSpec as P

ADAM_STEP = 10
NORM_EPS = 1e-06
BETA_FIRST = 0.9
BETA_SECOND = 0.999
ADAM_EPS = 1e-08
CLIP_LIMIT = 1.0
MASKED = -1e30
LOG2E = math.log2(math.e)
LN2 = math.log(2.0)
MESH = pl.DeviceIdType.MESH
BF = jnp.bfloat16
F32 = jnp.float32

T = 512
D = 512
FF = 2048
HD = 64
K8 = 8
NE = 24
PL = 8
LE = NE // PL
ER = LE * HD
HB = FF // 2
R = 512
NR = K8 * 128 // R


def mm(a, b):
    return jnp.dot(a, b, preferred_element_type=F32)


def mm_nt(a, b):
    return lax.dot_general(a, b, (((1,), (1,)), ((), ())), preferred_element_type=F32)


def mm_tn(a, b):
    return lax.dot_general(a, b, (((0,), (0,)), ((), ())), preferred_element_type=F32)


def expert_at(place):
    slot = place // LE
    return LE * (2 * (slot % 4) + slot // 4) + place % LE


def piece_rows(dp):
    return -(-ER // (dp * 16)) * 16


def scratch_list(dp):
    shard = D // dp
    pr = piece_rows(dp)
    return dict(
        wkvf=((D, 2 * HD), BF),
        w2=((2, D, FF), BF),
        eq=((NE * HD, D), BF),
        eo=((NE * HD, D), BF),
        kvb=((PL, 2, 256, 128), BF),
        tokx=((256, D), BF),
        cotx=((256, D), BF),
        rtx=((8, 256), jnp.int32),
        tokd=((T, D), BF),
        cotd=((T, D), BF),
        cott=((D, T), BF),
        rtd=((8, T), jnp.int32),
        nd=((T, D), BF),
        gate=((8, T), F32),
        dgate=((8, T), F32),
        big=((PL * 256, T), F32),
        at=((NE * HD, T), BF),
        qx=((4, 128, 1024), BF),
        dox=((4, 128, 1024), BF),
        att=((4, HD, 1024), F32),
        linv=((4, 8, 1024), F32),
        kx=((2, 8, 256, 128), BF),
        vx=((2, 8, 256, 128), BF),
        kt=((2, 8, HD, 256), BF),
        vt=((2, 8, HD + 16, 256), BF),
        pst=((2, 9, 256, 1024), BF),
        dkv=((2, 8, 256, 128), F32),
        mixed=((T, D), F32),
        ffn=((T, D), BF),
        ffnt=((D, T), BF),
        dmb=((T, D), BF),
        acc1=((T, D), F32),
        acc2=((T, D), F32),
        gf=((2, D, FF), BF),
        rf1=((2, D, HB), BF),
        rf2=((dp - 1, 2, shard, HB), BF),
        rs=((2, shard, HB), BF),
        rf3=((3, 2, shard, HB // 4), BF),
        f2=((2, shard, FF), BF),
        go=((NE * HD, D), BF),
        rq1=((NE * HD // 2, D), BF),
        ro1=((NE * HD // 2, D), BF),
        rq2=((3, ER, D), BF),
        ro2=((3, ER, D), BF),
        xq=((dp * pr, D), BF),
        xo=((dp * pr, D), BF),
        rq3=((dp - 1, pr, D), BF),
        ro3=((dp - 1, pr, D), BF),
        fq=((dp * pr, D), BF),
        fo=((dp * pr, D), BF),
        rk1=((4, 2, 256, 128), BF),
        rk2=((3, 2, 256, 128), BF),
        dkvd=((T, 128), BF),
        tbf=((128, 640), F32),
        tb=((128, 640), BF),
        rt1=((64, 640), BF),
        tsm=((64, 640), BF),
        rt2=((3, 16, 640), BF),
        rt3=((dp, 16, 640), BF),
        tf=((128, 640), BF),
        cnt=((32, 128), F32),
        mz=((dp, 32, 128), F32),
        mq=((PL, 32, 128), F32),
        layx=((256, D), BF),
        layr=((256, D), BF),
        tgx=((256, D), BF),
        tgr=((256, D), BF),
        gain=((8, D), F32),
        layo=((T, D), BF),
        osem=(8,),
        ssem=None,
        rsem=None,
    )


def copies_of(dp):
    return 64 + 8 * dp + 8


def layer_kernel(dp, *refs):
    shard = D // dp
    pr = piece_rows(dp)
    (tok, cot, rt, wkv, w2i, eqi, eoi, wrt, gains, info) = refs[:10]
    (lay, tg, msgo, f2o, fqo, foo, tbo) = refs[10:17]
    names = list(scratch_list(dp))
    s = type("Scratch", (), dict(zip(names, refs[17:])))

    z = lax.axis_index("dp")
    e = lax.axis_index("expert")
    c = e % 2
    q = e // 2
    qs = [q, q + 1 - 2 * (q % 2), (q + 2) % 4, 3 - q]
    sib = (z, e + 1 - 2 * c)
    chips = [None] + [(z, 2 * qs[m] + c) for m in (1, 2, 3)]
    swap = (z, 7 - e)
    zp = [None] + [((z + i) % dp, e) for i in range(1, dp)]
    zfrom = [None] + [(z + dp - i) % dp for i in range(1, dp)]
    slot = c * 4 + q
    plane = [sib] + [(z, (e + i) % PL) for i in range(1, PL)]

    count = [0]
    sends = []

    def rcopy(src, dst, peer):
        k = count[0]
        count[0] += 1
        d = pltpu.make_async_remote_copy(
            src_ref=src,
            dst_ref=dst,
            send_sem=s.ssem.at[k],
            recv_sem=s.rsem.at[k],
            device_id=peer,
            device_id_type=MESH,
        )
        d.start()
        sends.append(d)
        return (k, peer, d)

    def sent(handle):
        sends[:] = [d for d in sends if d is not handle[2]]
        handle[2].wait_send()

    def rwait(handle, dst):
        k, peer, _ = handle
        pltpu.make_async_remote_copy(
            src_ref=dst,
            dst_ref=dst,
            send_sem=s.ssem.at[k],
            recv_sem=s.rsem.at[k],
            device_id=peer,
            device_id_type=MESH,
        ).wait_recv()

    def lcopy(src, dst, k):
        d = pltpu.make_async_copy(src, dst, s.osem.at[k])
        d.start()
        return d

    bar = pltpu.get_barrier_semaphore()
    for peer in plane[1:] + zp[1:]:
        pl.semaphore_signal(bar, inc=1, device_id=peer, device_id_type=MESH)
    pl.semaphore_wait(bar, PL - 1 + dp - 1)

    def zrows(ref, i, n):
        return ref.at[pl.ds(pl.multiple_of(i * n, n), n)]

    h_wkv = [None] + [rcopy(wkv, zrows(s.wkvf, z, shard), zp[i]) for i in range(1, dp)]
    h_tok = rcopy(tok.at[pl.ds(256, 256)], s.tokx, swap)
    h_rt = rcopy(rt.at[:, pl.ds(256, 256)], s.rtx, swap)
    lo = pl.multiple_of(c * HB, HB)
    hi = pl.multiple_of((1 - c) * HB, HB)
    h_w2 = [None] + [
        rcopy(
            w2i.at[:, :, pl.ds(lo, HB)],
            s.w2.at[:, pl.ds(pl.multiple_of(z * shard, shard), shard), pl.ds(lo, HB)],
            zp[i],
        )
        for i in range(1, dp)
    ]
    h_eq = [None] + [rcopy(eqi, zrows(s.eq, slot, ER), chips[m]) for m in (1, 2, 3)]

    s.wkvf[pl.ds(pl.multiple_of(z * shard, shard), shard), :] = wkv[...]
    l_eq = lcopy(eqi, zrows(s.eq, slot, ER), 0)
    l_eo = lcopy(eoi, zrows(s.eo, slot, ER), 1)
    l_w2 = lcopy(
        w2i.at[:, :, pl.ds(lo, HB)],
        s.w2.at[:, pl.ds(pl.multiple_of(z * shard, shard), shard), pl.ds(lo, HB)],
        2,
    )

    ri = lax.broadcasted_iota(jnp.int32, (256, 256), 0)
    ci = lax.broadcasted_iota(jnp.int32, (256, 256), 1)
    split = jnp.where(ci == 2 * (ri % 128) + ri // 128, 1.0, 0.0).astype(BF)
    join = jnp.where(ri == 2 * (ci % 128) + ci // 128, 1.0, 0.0).astype(BF)
    g0 = gains[0:1, :]
    g1 = gains[1:2, :]

    def rms(x):
        inv = lax.rsqrt(jnp.mean(x * x, axis=-1, keepdims=True) + NORM_EPS)
        return x * inv, inv

    nat0 = mm(split, tok[0:256, :])
    nat1 = mm(split, tok[256:512, :])
    s.tokd[0:256, :] = nat0.astype(BF)
    n0 = (rms(nat0)[0] * g0).astype(BF)
    n1 = (rms(nat1)[0] * g0).astype(BF)
    s.nd[0:256, :] = n0
    cot0 = mm(split, cot[0:256, :])
    s.cotd[0:256, :] = cot0.astype(BF)

    for i in range(1, dp):
        rwait(h_wkv[i], zrows(s.wkvf, zfrom[i], shard))
    kv0 = mm(n0, s.wkvf[...]).astype(BF)
    kv1 = mm(n1, s.wkvf[...]).astype(BF)
    for p in range(2):
        s.kvb[slot, p, 0:128, :] = kv0[p * 128 : (p + 1) * 128]
        s.kvb[slot, p, 128:256, :] = kv1[p * 128 : (p + 1) * 128]
    h_kv = [None] + [rcopy(s.kvb.at[slot], s.kvb.at[slot], chips[m]) for m in (1, 2, 3)]
    h_cot = rcopy(cot.at[pl.ds(256, 256)], s.cotx, swap)
    h_eo = [None] + [rcopy(eoi, zrows(s.eo, slot, ER), chips[m]) for m in (1, 2, 3)]

    rwait(h_tok, s.tokx)
    rwait(h_rt, s.rtx)
    sw = mm(split, s.tokx[...])
    s.tokd[256:512, :] = sw.astype(BF)
    s.nd[256:512, :] = (rms(sw)[0] * g0).astype(BF)
    s.rtd[:, 0:256] = rt[:, 0:256]
    s.rtd[:, 256:512] = s.rtx[...]

    bm1 = info[0] - 1
    is2 = (4 - info[0]) // 2

    def seq_pos(r):
        return r & bm1, (r >> 1) * is2 + (r >> 2) * (1 - is2)

    def limit_of(index):
        out = jnp.zeros(index.shape, jnp.int32)
        for i in range(4):
            out = jnp.where(index == i, info[1 + i], out)
        return out

    block = [2 * e, 15 - 2 * e]
    lanes128 = lax.broadcasted_iota(jnp.int32, (16, 128), 1)
    row16 = lax.broadcasted_iota(jnp.int32, (16, 128), 0)
    row32 = lax.broadcasted_iota(jnp.int32, (32, 128), 0)

    logits = mm_nt(wrt[...], s.nd[...])
    row_e = lax.broadcasted_iota(jnp.int32, (32, T), 0)
    chosen = jnp.concatenate(
        [
            jnp.sum(jnp.where(row_e == s.rtd[k : k + 1, :], logits, 0.0), axis=0, keepdims=True)
            for k in range(K8)
        ],
        axis=0,
    )
    ex = jnp.exp(chosen - jnp.max(chosen, axis=0, keepdims=True))
    s.gate[...] = ex / jnp.sum(ex, axis=0, keepdims=True)

    counts = jnp.zeros((32, 128), F32)
    for g in range(4):
        b, p = g // 2, g % 2
        row = 2 * (block[b] * 128 + lanes128) + p
        seq, pos = seq_pos(row)
        live = (pos < limit_of(seq))[0:1, :].astype(F32)
        for k in range(K8):
            counts = counts + jnp.where(
                row32 == s.rtd[k : k + 1, g * 128 : (g + 1) * 128], live, 0.0
            )
        feat = jnp.where(seq == row16, 1.0, 0.0).astype(BF)
        s.qx[g, 64:80, :] = jnp.concatenate([feat] * K8, axis=1)
        s.qx[g, 80:128, :] = jnp.zeros((48, 1024), BF)
    s.cnt[...] = jnp.broadcast_to(jnp.sum(counts, axis=1, keepdims=True), (32, 128))

    for m in (1, 2, 3):
        rwait(h_eq[m], zrows(s.eq, c * 4 + qs[m], ER))
    half = NE * HD // 2
    l_eq.wait()
    h_eqs = rcopy(zrows(s.eq, c, half), zrows(s.eq, c, half), sib)
    for m in (1, 2, 3):
        rwait(h_kv[m], s.kvb.at[c * 4 + qs[m]])
    h_kvs = rcopy(s.kvb.at[pl.ds(c * 4, 4)], s.kvb.at[pl.ds(c * 4, 4)], sib)
    rwait(h_eqs, zrows(s.eq, 1 - c, half))

    def query_rows(i, _):
        rows = pl.ds(pl.multiple_of(i * 256, 256), 256)
        s.big[rows, :] = mm_nt(s.eq[rows, :], s.nd[...])
        return 0

    lax.fori_loop(0, NE * HD // 256, query_rows, 0)

    def pick(g, k):
        lanes = pl.ds(pl.multiple_of(g * 128, 128), 128)
        rk = s.rtd[k : k + 1, lanes]
        acc = jnp.zeros((HD, 128), F32)
        for place in range(NE):
            acc = jnp.where(rk == expert_at(place), s.big[place * HD : (place + 1) * HD, lanes], acc)
        return acc

    def choose(g, _):
        for k in range(K8):
            s.qx[g, 0:64, k * 128 : (k + 1) * 128] = (pick(g, k) * (0.125 * LOG2E)).astype(BF)
        return 0

    lax.fori_loop(0, 4, choose, 0)

    rwait(h_kvs, s.kvb.at[pl.ds((1 - c) * 4, 4)])
    krow = lax.broadcasted_iota(jnp.int32, (256, 128), 0)
    klane = lax.broadcasted_iota(jnp.int32, (256, 128), 1)
    for t in range(8):
        for p in range(2):
            kv = s.kvb[(t % 2) * 4 + t // 2, p].astype(F32)
            seq, pos = seq_pos(2 * (t * 256 + krow) + p)
            col = klane - 64
            shown = (seq == col) & (pos < limit_of(col))
            feat = jnp.where(shown | (col > 3), 0.0, MASKED)
            s.kx[p, t] = jnp.where(col < 0, kv, feat).astype(BF)
            s.vx[p, t] = jnp.where(col >= 0, kv, jnp.where(klane < 2, 1.0, 0.0)).astype(BF)
            kvt = kv.T
            s.kt[p, t] = kvt[0:64].astype(BF)
            s.vt[p, t, 0:64, :] = kvt[64:128].astype(BF)
            s.vt[p, t, 64:80, :] = jnp.ones((16, 256), BF)

    tiles = [e + 1, 8 - e]
    base = [0, e + 1]
    for g in range(4):
        b, p = g // 2, g % 2
        nt, first = tiles[b], base[b]
        visible = (
            lax.broadcasted_iota(jnp.int32, (256, 128), 0)
            <= lax.broadcasted_iota(jnp.int32, (256, 128), 1) + 128 * b
        )
        visible = jnp.concatenate([visible] * (R // 128), axis=1)
        for rc in range(NR):
            ls = slice(rc * R, (rc + 1) * R)

            def scores(t, peak):
                sc = mm(s.kx[p, t], s.qx[g, :, ls])
                s.big[pl.ds(pl.multiple_of(t * 256, 256), 256), :] = sc
                return jnp.maximum(peak, jnp.max(sc.reshape(32, 8, R), axis=0))

            peak = lax.fori_loop(0, nt - 1, scores, jnp.full((8, R), MASKED, F32))
            sc = jnp.where(visible, mm(s.kx[p, nt - 1], s.qx[g, :, ls]), MASKED)
            s.big[pl.ds(pl.multiple_of((nt - 1) * 256, 256), 256), :] = sc
            peak = jnp.maximum(peak, jnp.max(sc.reshape(32, 8, R), axis=0))
            peak = jnp.max(peak, axis=0, keepdims=True)

            def values(t, acc):
                pb = jnp.exp2(s.big[pl.ds(pl.multiple_of(t * 256, 256), 256), :] - peak).astype(BF)
                s.pst[p, first + t, :, ls] = pb
                return acc + mm(s.vt[p, t], pb)

            acc = lax.fori_loop(0, nt, values, jnp.zeros((HD + 16, R), F32))
            inv = 1.0 / acc[64:72]
            s.linv[g, :, ls] = inv
            s.att[g, :, ls] = acc[0:64] * inv[0:1]

    for m in (1, 2, 3):
        rwait(h_eo[m], zrows(s.eo, c * 4 + qs[m], ER))
    l_eo.wait()
    h_eos = rcopy(zrows(s.eo, c, half), zrows(s.eo, c, half), sib)
    for i in range(1, dp):
        rwait(
            h_w2[i],
            s.w2.at[:, pl.ds(pl.multiple_of(zfrom[i] * shard, shard), shard), pl.ds(lo, HB)],
        )
    l_w2.wait()
    h_w2s = rcopy(s.w2.at[:, :, pl.ds(lo, HB)], s.w2.at[:, :, pl.ds(lo, HB)], sib)

    def spread(dst, src, scale):
        def one(g, _):
            lanes = pl.ds(pl.multiple_of(g * 128, 128), 128)
            for k in range(K8):
                part = src[g, :, k * 128 : (k + 1) * 128]
                if scale is not None:
                    part = part * scale[k : k + 1, lanes]
                else:
                    part = part * 0.125
                s.acc1[k * HD : (k + 1) * HD, 0:128] = part
            for place in range(NE):
                acc = jnp.zeros((HD, 128), F32)
                for k in range(K8):
                    acc = jnp.where(
                        s.rtd[k : k + 1, lanes] == expert_at(place),
                        s.acc1[k * HD : (k + 1) * HD, 0:128],
                        acc,
                    )
                dst[place * HD : (place + 1) * HD, lanes] = acc.astype(BF)
            return 0

        lax.fori_loop(0, 4, one, 0)

    spread(s.at, s.att, s.gate)
    rwait(h_eos, zrows(s.eo, 1 - c, half))
    s.acc1[...] = s.tokd[...].astype(F32)

    def mix(i, _):
        rows = pl.ds(pl.multiple_of(i * 256, 256), 256)
        s.acc1[...] += mm_tn(s.at[rows, :], s.eo[rows, :])
        return 0

    lax.fori_loop(0, NE * HD // 256, mix, 0)
    mixed = s.acc1[...]
    s.mixed[...] = mixed
    ffn = rms(mixed)[0] * g1
    s.ffn[...] = ffn.astype(BF)
    s.ffnt[...] = ffn.T.astype(BF)
    rwait(h_cot, s.cotx)
    cot1 = mm(split, s.cotx[...])
    s.cotd[256:512, :] = cot1.astype(BF)
    s.cott[:, 0:256] = cot0.T.astype(BF)
    s.cott[:, 256:512] = cot1.T.astype(BF)
    s.acc2[...] = jnp.zeros((T, D), F32)
    rwait(h_w2s, s.w2.at[:, :, pl.ds(hi, HB)])

    FT = 256

    def feed(i, _):
        cols = pl.ds(pl.multiple_of(i * FT, FT), FT)
        up = mm(s.ffn[...], s.w2[0, :, cols])
        sq = up * up
        th = jnp.tanh(0.79788456 * up * (1.0 + 0.044715 * sq))
        hid = (0.5 * up * (1.0 + th)).astype(BF)
        slope = 0.5 * (1.0 + th) + 0.5 * up * (1.0 - th * th) * (
            0.79788456 * (1.0 + 3 * 0.044715 * sq)
        )
        s.acc1[...] += mm_nt(hid, s.w2[1, :, cols])
        dup = (mm(s.cotd[...], s.w2[1, :, cols]) * slope).astype(BF)
        s.gf[0, :, cols] = mm(s.ffnt[...], dup).astype(BF)
        s.gf[1, :, cols] = mm(s.cott[...], hid).astype(BF)
        s.acc2[...] += mm_nt(dup, s.w2[0, :, cols])
        return 0

    lax.fori_loop(0, FF // FT, feed, 0)
    h_f1 = rcopy(s.gf.at[:, :, pl.ds(hi, HB)], s.rf1, sib)

    out = s.acc1[...].astype(BF)
    s.layx[...] = mm(join, out[256:512]).astype(BF)
    h_lay = rcopy(s.layx, s.layr, swap)
    s.layo[0:256, :] = mm(join, out[0:256]).astype(BF)

    def rms_back(dn, gain, unit, inv):
        a = dn * gain
        return inv * (a - unit * jnp.mean(a * unit, axis=-1, keepdims=True)), jnp.sum(
            dn * unit, axis=0, keepdims=True
        )

    unit1, inv1 = rms(s.mixed[...])
    back, gain1 = rms_back(s.acc2[...], g1, unit1, inv1)
    s.gain[1:2, :] = gain1
    dmix = s.cotd[...].astype(F32) + back
    s.mixed[...] = dmix
    s.dmb[...] = dmix.astype(BF)

    def out_rows(i, _):
        rows = pl.ds(pl.multiple_of(i * 256, 256), 256)
        s.big[rows, :] = mm_nt(s.eo[rows, :], s.dmb[...])
        s.go[rows, :] = mm(s.at[rows, :], s.dmb[...]).astype(BF)
        return 0

    lax.fori_loop(0, NE * HD // 256, out_rows, 0)
    h_o1 = rcopy(zrows(s.go, 1 - c, half), s.ro1, sib)

    def heads_back(g, _):
        lanes = pl.ds(pl.multiple_of(g * 128, 128), 128)
        for k in range(K8):
            ks = slice(k * 128, (k + 1) * 128)
            da = pick(g, k)
            at = s.att[g, :, ks]
            s.dgate[k : k + 1, lanes] = jnp.sum(at * da, axis=0, keepdims=True)
            do = (da * (s.gate[k : k + 1, lanes] * s.linv[g, 0:1, ks])).astype(BF)
            s.dox[g, 64:128, ks] = do
            delta = -jnp.sum(do.astype(F32) * at, axis=0, keepdims=True)
            top = delta.astype(BF).astype(F32)
            s.dox[g, 0:16, ks] = jnp.where(
                row16 == 0, top, jnp.where(row16 == 1, delta - top, 0.0)
            ).astype(BF)
            s.dox[g, 16:64, ks] = jnp.zeros((48, 128), BF)
        return 0

    lax.fori_loop(0, 4, heads_back, 0)
    s.dkv[...] = jnp.zeros(s.dkv.shape, F32)

    left = lax.broadcasted_iota(jnp.int32, (256, 128), 1) < 64

    def attend_back(g):
        b, p = g // 2, g % 2
        nt, first = tiles[b], base[b]
        for rc in range(NR):
            ls = slice(rc * R, (rc + 1) * R)

            def tile(t, acc):
                prob = s.pst[p, first + t, :, ls]
                dprob = mm(s.vx[p, t], s.dox[g, :, ls])
                ds = (prob.astype(F32) * dprob).astype(BF)
                kpart = mm_nt(ds, s.qx[g, :, ls])
                vpart = mm_nt(prob, s.dox[g, :, ls])
                s.dkv[p, t] += jnp.where(left, kpart * LN2, vpart)
                return acc + mm(s.kt[p, t], ds)

            s.att[g, :, ls] = lax.fori_loop(0, nt, tile, jnp.zeros((HD, R), F32))

    def add_rows(n, step, fn):
        def one(i, _):
            fn(pl.ds(pl.multiple_of(i * step, step), step))
            return 0

        lax.fori_loop(0, n // step, one, 0)

    def both(a, b):
        return (a.astype(F32) + b.astype(F32)).astype(BF)

    attend_back(0)
    rwait(h_f1, s.rf1)

    def pair_ffn(rows):
        for w in range(2):
            s.rf1[w, rows, :] = both(s.gf[w, rows, pl.ds(lo, HB)], s.rf1[w, rows, :])

    add_rows(D, 64, pair_ffn)
    h_f2 = [None] + [
        rcopy(
            s.rf1.at[:, pl.ds(pl.multiple_of(zp[i][0] * shard, shard), shard), :],
            s.rf2.at[i - 1],
            zp[i],
        )
        for i in range(1, dp)
    ]
    rwait(h_o1, s.ro1)

    def pair_sum(own, got):
        def one(i, _):
            rows = pl.ds(pl.multiple_of(i * 64, 64), 64)
            mine = pl.ds(pl.multiple_of(c * half + i * 64, 64), 64)
            got[rows, :] = both(own[mine, :], got[rows, :])
            return 0

        lax.fori_loop(0, half // 64, one, 0)

    pair_sum(s.go, s.ro1)
    h_o2 = [None] + [rcopy(zrows(s.ro1, qs[m], ER), s.ro2.at[m - 1], chips[m]) for m in (1, 2, 3)]

    def chip_sum(dst, own, got):
        total = own[pl.ds(pl.multiple_of(q * ER, ER), ER), :].astype(F32)
        for m in (1, 2, 3):
            total = total + got[m - 1].astype(F32)
        dst[0:ER, :] = total.astype(BF)
        if dp * pr > ER:
            dst[ER:, :] = jnp.zeros((dp * pr - ER, D), BF)

    def z_scatter(own, got):
        return [None] + [rcopy(zrows(own, zp[i][0], pr), got.at[i - 1], zp[i]) for i in range(1, dp)]

    def z_sum(own, got, dst):
        total = own[pl.ds(pl.multiple_of(z * pr, pr), pr), :].astype(F32)
        for i in range(1, dp):
            total = total + got[i - 1].astype(F32)
        done = total.astype(BF)
        dst[pl.ds(pl.multiple_of(z * pr, pr), pr), :] = done
        wide = done.astype(F32)
        return [None] + [
            rcopy(zrows(dst, z, pr), zrows(dst, z, pr), zp[i]) for i in range(1, dp)
        ], wide * wide

    def fold(sq):
        sq = jnp.sum(sq, axis=0, keepdims=True)
        out = sq[:, 0:128]
        for j in range(1, sq.shape[1] // 128):
            out = out + sq[:, j * 128 : (j + 1) * 128]
        return out

    attend_back(1)
    for m in (1, 2, 3):
        rwait(h_o2[m], s.ro2.at[m - 1])
    chip_sum(s.xo, s.ro1, s.ro2)
    h_o3 = z_scatter(s.xo, s.ro3)

    attend_back(2)
    for i in range(1, dp):
        rwait(h_f2[i], s.rf2.at[i - 1])
    for w in range(2):
        total = s.rf1[w, pl.ds(pl.multiple_of(z * shard, shard), shard), :].astype(F32)
        for i in range(1, dp):
            total = total + s.rf2[i - 1, w].astype(F32)
        s.rs[w] = total.astype(BF)
    quart = HB // 4
    h_f3 = [None] + [
        rcopy(
            s.rs.at[:, :, pl.ds(pl.multiple_of(qs[m] * quart, quart), quart)],
            s.rf3.at[m - 1],
            chips[m],
        )
        for m in (1, 2, 3)
    ]
    for i in range(1, dp):
        rwait(h_o3[i], s.ro3.at[i - 1])
    h_o4, sq_o = z_sum(s.xo, s.ro3, s.fo)

    attend_back(3)
    sent(h_kvs)
    for m in (1, 2, 3):
        sent(h_kv[m])
    for dev in range(PL):
        sl = (dev % 2) * 4 + dev // 2
        for b, blk in enumerate((2 * dev, 15 - 2 * dev)):
            for p in range(2):
                s.kvb[sl, b, p * 128 : (p + 1) * 128, :] = s.dkv[p, blk // 2, (blk % 2) * 128 : (blk % 2) * 128 + 128, :].astype(BF)
    h_k1 = rcopy(s.kvb.at[pl.ds((1 - c) * 4, 4)], s.rk1, sib)
    spread(s.at, s.att, None)
    rwait(h_k1, s.rk1)
    for i in range(4):
        s.rk1[i] = both(s.kvb[c * 4 + i], s.rk1[i])
    h_k2 = [None] + [rcopy(s.rk1.at[qs[m]], s.rk2.at[m - 1], chips[m]) for m in (1, 2, 3)]

    sent(h_o1)

    def query_grad(i, _):
        rows = pl.ds(pl.multiple_of(i * 256, 256), 256)
        s.go[rows, :] = mm(s.at[rows, :], s.nd[...]).astype(BF)
        return 0

    lax.fori_loop(0, NE * HD // 256, query_grad, 0)
    h_q1 = rcopy(zrows(s.go, 1 - c, half), s.rq1, sib)
    s.acc2[...] = jnp.zeros((T, D), F32)

    def slot_sum(i, _):
        rows = pl.ds(pl.multiple_of(i * 256, 256), 256)
        s.acc2[...] += mm_tn(s.at[rows, :], s.eq[rows, :])
        return 0

    lax.fori_loop(0, NE * HD // 256, slot_sum, 0)
    gate = s.gate[...]
    dch = gate * (s.dgate[...] - jnp.sum(gate * s.dgate[...], axis=0, keepdims=True))
    dlog = jnp.zeros((32, T), F32)
    for k in range(K8):
        dlog = dlog + jnp.where(row_e == s.rtd[k : k + 1, :], dch[k : k + 1, :], 0.0)
    dlog = dlog.astype(BF)
    s.acc2[...] += mm_tn(dlog, wrt[...])
    grt = mm(dlog, s.nd[...])

    rwait(h_q1, s.rq1)
    pair_sum(s.go, s.rq1)
    for m in (1, 2, 3):
        rwait(h_k2[m], s.rk2.at[m - 1])
    for i in range(2):
        total = s.rk1[q, i].astype(F32)
        for m in (1, 2, 3):
            total = total + s.rk2[m - 1, i].astype(F32)
        s.dkvd[i * 256 : (i + 1) * 256, :] = total.astype(BF)
    dn = s.acc2[...] + mm_nt(s.dkvd[...], s.wkvf[...])
    unit0, inv0 = rms(s.tokd[...].astype(F32))
    back0, gain0 = rms_back(dn, g0, unit0, inv0)
    s.tbf[:, 0:512] = mm_tn(s.dkvd[...], s.nd[...])
    for j in range(4):
        js = slice(j * 128, (j + 1) * 128)
        s.tbf[j * 24 : (j + 1) * 24, 512:640] = grt[0:24, js]
        s.tbf[96 + j : 97 + j, 512:640] = gain0[:, js]
        s.tbf[100 + j : 101 + j, 512:640] = s.gain[1:2, js]
    s.tbf[104:128, 512:640] = jnp.zeros((24, 128), F32)
    s.tb[...] = s.tbf[...].astype(BF)
    h_t1 = rcopy(zrows(s.tb, 1 - c, 64), s.rt1, sib)
    h_q2 = [None] + [rcopy(zrows(s.rq1, qs[m], ER), s.rq2.at[m - 1], chips[m]) for m in (1, 2, 3)]

    grad = s.mixed[...] + back0
    s.tgx[...] = mm(join, grad[256:512].astype(BF)).astype(BF)
    rwait(h_t1, s.rt1)
    s.tsm[...] = both(s.tb[pl.ds(pl.multiple_of(c * 64, 64), 64), :], s.rt1[...])
    h_t2 = [None] + [rcopy(zrows(s.tsm, qs[m], 16), s.rt2.at[m - 1], chips[m]) for m in (1, 2, 3)]
    h_tg = rcopy(s.tgx, s.tgr, swap)
    top = grad[0:256].astype(BF)
    rest = (grad[0:256] - top.astype(F32)).astype(BF)
    s.acc1[0:256, :] = mm(join, top) + mm(join, rest)

    for m in (1, 2, 3):
        rwait(h_f3[m], s.rf3.at[m - 1])
    mine = pl.ds(pl.multiple_of(q * quart, quart), quart)
    sq_f = jnp.zeros((1, 128), F32)
    wide = pl.ds(pl.multiple_of(c * HB + q * quart, quart), quart)
    for w in range(2):
        total = s.rs[w, :, mine].astype(F32)
        for m in (1, 2, 3):
            total = total + s.rf3[m - 1, w].astype(F32)
        done = total.astype(BF)
        s.f2[w, :, wide] = done
        sq_f = sq_f + fold(done.astype(F32) * done.astype(F32))
    h_f4 = [None] + [
        rcopy(s.f2.at[:, :, wide], s.f2.at[:, :, wide], chips[m]) for m in (1, 2, 3)
    ]

    for m in (1, 2, 3):
        rwait(h_t2[m], s.rt2.at[m - 1])
    total = s.tsm[pl.ds(pl.multiple_of(q * 16, 16), 16), :].astype(F32)
    for m in (1, 2, 3):
        total = total + s.rt2[m - 1].astype(F32)
    s.rt3[z] = total.astype(BF)
    h_t3 = [None] + [rcopy(s.rt3.at[z], s.rt3.at[z], zp[i]) for i in range(1, dp)]
    for m in (1, 2, 3):
        rwait(h_q2[m], s.rq2.at[m - 1])
    chip_sum(s.xq, s.rq1, s.rq2)
    h_q3 = z_scatter(s.xq, s.rq3)

    for i in range(1, dp):
        rwait(h_t3[i], s.rt3.at[zfrom[i]])
    total = s.rt3[0].astype(F32)
    for i in range(1, dp):
        total = total + s.rt3[i].astype(F32)
    done = total.astype(BF)
    s.tf[pl.ds(pl.multiple_of(slot * 16, 16), 16), :] = done
    h_t4 = [None] + [
        rcopy(zrows(s.tf, slot, 16), zrows(s.tf, slot, 16), chips[m]) for m in (1, 2, 3)
    ]
    sq_t = fold(done.astype(F32) * done.astype(F32)) * (1.0 / dp)

    for i in range(1, dp):
        rwait(h_q3[i], s.rq3.at[i - 1])
    h_q4, sq_q = z_sum(s.xq, s.rq3, s.fq)

    squares = sq_f + sq_t + fold(sq_o) + fold(sq_q)
    s.mz[z] = jnp.where(row32 < 24, s.cnt[...], jnp.where(row32 == 24, squares, 0.0))
    h_m1 = [None] + [rcopy(s.mz.at[z], s.mz.at[z], zp[i]) for i in range(1, dp)]

    for m in (1, 2, 3):
        rwait(
            h_f4[m],
            s.f2.at[:, :, pl.ds(pl.multiple_of(c * HB + qs[m] * quart, quart), quart)],
        )
    h_f5 = rcopy(s.f2.at[:, :, pl.ds(lo, HB)], s.f2.at[:, :, pl.ds(lo, HB)], sib)
    for m in (1, 2, 3):
        rwait(h_t4[m], zrows(s.tf, c * 4 + qs[m], 16))
    h_t5 = rcopy(zrows(s.tf, c, 64), zrows(s.tf, c, 64), sib)

    for i in range(1, dp):
        rwait(h_m1[i], s.mz.at[zfrom[i]])
    total = s.mz[0]
    for i in range(1, dp):
        total = total + s.mz[i]
    s.mq[e] = total
    h_m2 = [None] + [rcopy(s.mq.at[e], s.mq.at[e], plane[i]) for i in range(1, PL)]

    rwait(h_lay, s.layr)
    s.layo[256:512, :] = s.layr[...]
    done = [lcopy(s.layo, lay, 0)]
    rwait(h_tg, s.tgr)
    s.acc1[256:512, :] = s.tgr[...].astype(F32)
    done.append(lcopy(s.acc1, tg, 1))
    rwait(h_f5, s.f2.at[:, :, pl.ds(hi, HB)])
    done.append(lcopy(s.f2, f2o, 2))
    rwait(h_t5, zrows(s.tf, 1 - c, 64))
    done.append(lcopy(s.tf, tbo, 3))
    for i in range(1, dp):
        rwait(h_o4[i], zrows(s.fo, zfrom[i], pr))
        rwait(h_q4[i], zrows(s.fq, zfrom[i], pr))
    done.append(lcopy(s.fo.at[pl.ds(0, ER)], foo, 4))
    done.append(lcopy(s.fq.at[pl.ds(0, ER)], fqo, 5))
    for i in range(1, PL):
        rwait(h_m2[i], s.mq.at[(e + PL - i) % PL])
    total = s.mq[0]
    for i in range(1, PL):
        total = total + s.mq[i]
    s.cnt[...] = total
    done.append(lcopy(s.cnt, msgo, 6))
    for d in done:
        d.wait()
    for d in sends:
        d.wait_send()
    assert count[0] <= copies_of(dp)


def adam_update(weight, gradient, first_moment, second, clip_scale, step_rate, decay_rate):
    step_grad = gradient * clip_scale
    new_first = BETA_FIRST * first_moment + (1.0 - BETA_FIRST) * step_grad
    new_second = BETA_SECOND * second + (1.0 - BETA_SECOND) * step_grad * step_grad
    first_hat = new_first / (1.0 - BETA_FIRST**ADAM_STEP)
    second_hat = new_second / (1.0 - BETA_SECOND**ADAM_STEP)
    new_weight = weight - step_rate * (
        first_hat / (jnp.sqrt(second_hat) + ADAM_EPS) + decay_rate * weight
    )
    return (new_weight, new_first, new_second)


def on_device(
    tokens, cotangent, routes, group_batch, seq_lengths,
    gains, gains_first, gains_second,
    router_weight, router_first, router_second,
    keyval_weight, keyval_first, keyval_second,
    query_weight, query_first, query_second,
    output_weight, output_first, output_second,
    up_weight, up_first, up_second,
    down_weight, down_first, down_second,
):
    dp = lax.axis_size("dp")
    z = lax.axis_index("dp")
    shard = D // dp
    pr = piece_rows(dp)
    batch = lax.dynamic_index_in_dim(group_batch, z, 0, keepdims=True)
    lengths = lax.dynamic_index_in_dim(seq_lengths, z, 0, keepdims=False)
    info = jnp.concatenate([batch, lengths])
    rt = routes.reshape(2, 128, 2, K8).transpose(3, 0, 2, 1).reshape(K8, T)
    w2i = jnp.stack([up_weight, down_weight.T]).astype(BF)
    eqi = query_weight.transpose(0, 2, 1).reshape(ER, D).astype(BF)
    eoi = output_weight.reshape(ER, D).astype(BF)
    wrt = jnp.pad(router_weight.T, ((0, 32 - NE), (0, 0))).astype(BF)

    scr = []
    for name, item in scratch_list(dp).items():
        if item is None:
            scr.append(pltpu.SemaphoreType.DMA((copies_of(dp),)))
        elif len(item) == 1:
            scr.append(pltpu.SemaphoreType.DMA(item))
        else:
            scr.append(pltpu.VMEM(item[0], item[1]))
    vm = pl.BlockSpec(memory_space=pltpu.VMEM)
    hbm = pl.BlockSpec(memory_space=pl.ANY)
    outs = [
        jax.ShapeDtypeStruct((T, D), BF),
        jax.ShapeDtypeStruct((T, D), F32),
        jax.ShapeDtypeStruct((32, 128), F32),
        jax.ShapeDtypeStruct((2, shard, FF), BF),
        jax.ShapeDtypeStruct((ER, D), BF),
        jax.ShapeDtypeStruct((ER, D), BF),
        jax.ShapeDtypeStruct((128, 640), BF),
    ]

    def kernel(*refs):
        layer_kernel(dp, *refs)

    lay, tg, msg, f2, fq, fo, tb = pl.pallas_call(
        kernel,
        out_shape=outs,
        in_specs=[vm] * 4 + [hbm] * 3 + [vm] * 2 + [pl.BlockSpec(memory_space=pltpu.SMEM)],
        out_specs=[hbm] * len(outs),
        scratch_shapes=scr,
        compiler_params=pltpu.CompilerParams(
            collective_id=0, has_side_effects=True, vmem_limit_bytes=64 * 2**20 - 2**17
        ),
        name="layer",
    )(tokens, cotangent, rt, keyval_weight.astype(BF), w2i, eqi, eoi, wrt, gains, info)

    counts = msg[0:NE, 0].astype(jnp.int32)
    grad_norm = jnp.sqrt(jnp.sum(msg[24]))
    clip = CLIP_LIMIT / jnp.maximum(grad_norm, CLIP_LIMIT)
    up_g = f2[0].astype(F32)
    down_g = f2[1].T.astype(F32)
    q_g = fq.reshape(LE, HD, D).transpose(0, 2, 1).astype(F32)
    o_g = fo.reshape(LE, HD, D).astype(F32)
    kv_g = lax.dynamic_slice_in_dim(tb[:, 0:512], z * shard, shard, 1).T.astype(F32)
    side = tb[:, 512:640].astype(F32)
    r_g = side[0:96].reshape(4, NE, 128).transpose(1, 0, 2).reshape(NE, D).T
    gain_g = side[96:104].reshape(2, D)
    gains_out = adam_update(gains, gain_g, gains_first, gains_second, clip, 0.7, 0.0)
    router_out = adam_update(router_weight, r_g, router_first, router_second, clip, 0.03, 0.1)
    keyval_out = adam_update(keyval_weight, kv_g, keyval_first, keyval_second, clip, 0.06, 0.1)
    query_out = adam_update(query_weight, q_g, query_first, query_second, clip, 0.06, 0.1)
    output_out = adam_update(output_weight, o_g, output_first, output_second, clip, 2.0, 0.1)
    up_out = adam_update(up_weight, up_g, up_first, up_second, clip, 0.06, 0.1)
    down_out = adam_update(down_weight, down_g, down_first, down_second, clip, 0.03, 0.1)
    return (
        lay, tg, counts, grad_norm,
        *gains_out, *router_out, *keyval_out, *query_out, *output_out, *up_out, *down_out,
    )


def solution(mesh):
    tok = P(("dp", "expert"), None)
    dp0 = P("dp", None)
    ex0 = P("expert", None, None)
    dp1 = P(None, "dp")
    return jax.shard_map(
        on_device,
        mesh=mesh,
        in_specs=(tok,) * 3 + (P(),) * 8 + (dp0,) * 3 + (ex0,) * 6 + (dp0,) * 3 + (dp1,) * 3,
        out_specs=(tok,) * 2 + (P(),) * 8 + (dp0,) * 3 + (ex0,) * 6 + (dp0,) * 3 + (dp1,) * 3,
        check_vma=False,
    )
```

time: 1540 us -> 236 us (0.15)
  waiting for transfers between devices: 491 us -> 0 us
  local copies, waits for them, and re-layouts: 418 us -> 23.5 us
  matrix products: 248 us -> 0 us
  Pallas kernels: 0 us -> 190 us
  loops' own time: 152 us -> 0 us
  other arithmetic: 113 us -> 18.5 us
  blocking collectives: 78.6 us -> 0 us
  between operations: 24.8 us -> 2.74 us
    reduce_scatter x5 -> x0, waiting for transfers between devices: 398 us -> none  [the longest x1 311 us: on_device(): lax.psum_scatter(keyval_grad_rows.astype(jnp.bfloat16), 'expert', scatter...]
    dot_general x164 -> x0, matrix products: 248 us -> none  [the longest x48 67.4 us: tile_scores(): jnp.einsum('rh,uh->ru', query_blk, keys_tile, preferred_element_type=jnp....]
    gather x9 -> x0, local copies, waits for them, and re-layouts: 226 us -> none  [the longest x1 45.5 us: on_device(): index_blocks = major_index[order].reshape(block_count, block_rows)]
    pallas_call x0 -> x1, Pallas kernels: none -> 190 us  [on_device(): pl.pallas_call(kernel, out_shape=outs, in_specs=[vm] * 4 + [hbm] * 3 + [v...]
    another operation x66 -> x0, loops' own time: 152 us -> none  [the longest x1 74.8 us: on_device(): lax.map(forward_block, (query_blocks, index_blocks))]
    psum x2 -> x0, waiting for transfers between devices: 91.8 us -> none  [the longest x1 58.4 us: on_device(): lax.psum(up_part.astype(jnp.bfloat16), 'expert').astype(jnp.float32)]
    scatter x3 -> x0, local copies, waits for them, and re-layouts: 71.3 us -> none  [the longest x2 55.5 us: unsort(): return jnp.zeros_like(sorted_rows).at[order].set(sorted_rows)[:flat_count]]
    psum x2 -> x0, blocking collectives: 63.5 us -> none  [the longest x1 40.6 us: on_device(): lax.psum((grad_router, jnp.stack([gain_attn, gain_ffn]), counts_local), (...]
  transfers between devices with their start and end apart: 13 -> 0, of which waited for: 6 -> 0; matrix products, arithmetic and copies ran while one was open for 32% -> 0% of each run, Pallas kernels for 0% -> 0%
where the time goes in v1:
time: 236 us; the launch traced here: 235 us
  Pallas kernels  190 us (81%)
  local copies, waits for them, and re-layouts  23.5 us (10%)
  other arithmetic  18.5 us (8%)
  between operations  2.74 us (1%)
    pallas_call x1, Pallas kernels, on_device(): pl.pallas_call(kernel, out_shape=outs, in_specs=[vm] * 4 + [hbm] * 3 + [v...  190 us
    unnamed x81, local copies, waits for them, and re-layouts  20.9 us
    sub x7, other arithmetic, adam_update(): weight - step_rate * (first_hat / (jnp.sqrt(second_hat) + ADAM_EPS) + dec...  10.4 us

profile of v1, /device:TPU:0, one launch (start us, length us, event | category | flops | bytes accessed | tf_op | source)
XLA Modules:
  0.0 234.8 jit_solution(798277352908373564)
XLA Ops:
  0.7 1.3 dynamic_slice.11
  2.0 1.2 pad_add_fusion.refs_9_
  3.2 0.8 convert_bitcast_fusion.2
  4.0 0.6 pad.5.refs_7_
  4.7 1.5 convert_element_type.50.refs_3_
  6.2 1.7 copy.72
  7.8 1.6 copy.73
  9.4 0.7 copy.75
  10.1 0.7 convert_element_type.51
  10.8 0.7 convert_element_type.54
  11.5 0.1 copy.68
  11.7 0.7 copy.69
  12.5 0.3 copy-done.8
  12.8 0.3 copy.70
  13.1 0.1 convert_bitcast_fusion
  13.2 1.1 pad_maximum_fusion.refs_4_
  14.3 0.2 copy-done.1
  14.4 0.7 copy-done.9
  15.1 1.3 copy.76
  16.4 1.3 copy.77
  17.7 190.1 %layer.1 = (bf16[512,512]{1,0:T(8,128)(2,1)}, f32[512,512]{1,0:T(8,128)}, f32[32,128]{1,0:T(8,128)}, bf16[2,128,2048]{2,1,0:T(8,128)(2,1)}, bf16[192,512]{1,0:T(...) custom-call(bf16[512,512]{1,0:T(8,128)(2,1)} %refs_0_.1, bf16[512,512]{1,0:T(8,128)(2,1)} %refs_1_.1, ...), custom_call_target="tpu_custom_call" | custom-call | tf_op jit(solution)/shard_map/layer/pallas_call | solution.py:867
  207.8 1.3 slice_reduce_fusion
  209.8 2.9 %multiply_subtract_fusion = (f32[2048,128]{0,1:T(8,128)S(1)}, f32[2048,128]{0,1:T(8,128)S(1)}, f32[2048,128]{0,1:T(8,128)S(1)}) fusion(f32[2048,128]{0,1:T(8,128)} %copy-done.1, f32[]{:T(128)S(6)} %div.108, bf16[2,128,2048]{2,1,0:T(8,128)(2,1)} %get-tuple-element.38, f32[2048,128]{0,1:T(8,128)} %copy.76, f32[2048,128]{0,1:T(8,128)} %copy.77), kind=kLoop, calls=%fused_computation.9 | loop fusion | flops 4456448 | bytes 6815748 | tf_op jit(solution)/shard_map/sub | solution.py:815
  212.7 1.3 copy.83
  214.0 0.6 convert_reduce_fusion
  214.7 0.8 copy-done.19
  215.6 0.1 multiply_subtract_fusion.4
  215.7 0.7 copy.80
  216.5 0.7 copy-done.28
  217.1 0.6 multiply_subtract_fusion.6
  217.8 0.7 copy.81
  218.5 0.7 copy.82
  219.3 0.7 multiply_subtract_fusion.5
  220.0 0.3 copy-done.23
  220.3 0.1 convert_multiply_fusion.2
  220.4 0.9 copy-done.5
  221.3 0.1 copy-done.14
  221.4 0.1 copy-done.15
  221.5 1.2 multiply_subtract_fusion.3
  222.8 0.4 copy-done.17
  223.2 1.2 multiply_subtract_fusion.2
  224.4 1.3 copy.84
  225.7 1.3 copy.85
  227.0 0.6 copy-done.12
  227.6 3.7 %multiply_subtract_fusion.1 = (f32[128,2048]{1,0:T(8,128)}, f32[128,2048]{1,0:T(8,128)}, f32[128,2048]{1,0:T(8,128)}) fusion(f32[128,2048]{1,0:T(8,128)S(1)} %copy-done.3, f32[]{:T(128)S(6)} %div.108, bf16[2,128,2048]{2,1,0:T(8,128)(2,1)} %get-tuple-element.38, f32[128,2048]{1,0:T(8,128)S(1)} %copy-done.12, f32[128,2048]{1,0:T(8,128)} %param.48), kind=kLoop, calls=%fused_computation.11 | loop fusion | flops 4456448 | bytes 6815748 | tf_op jit(solution)/shard_map/sub | solution.py:815
  231.3 0.8 copy.93
  232.1 0.6 copy-done.11
  232.7 1.0 copy.94
  (61 shorter events, 0.4 us)
Async XLA Ops:
  0.7 1.3 copy-start
  0.7 9.4 %copy-start.4 = (f32[3,512,64]{1,2,0:T(8,128)S(1)}, f32[3,512,64]{1,2,0:T(8,128)}, u32[]{:S(2)}) copy-start(f32[3,512,64]{1,2,0:T(8,128)} %param.40) | copy-start | bytes 1179652
  4.0 5.4 %copy-start.18 = (f32[128,128]{1,0:T(8,128)S(1)}, f32[128,128]{1,0:T(8,128)}, u32[]{:S(2)}) copy-start(f32[128,128]{1,0:T(8,128)} %param.37) | copy-start | bytes 196612
  4.7 6.2 %copy-start.6 = (f32[3,64,512]{2,1,0:T(8,128)S(1)}, f32[3,64,512]{2,1,0:T(8,128)}, u32[]{:S(2)}) copy-start(f32[3,64,512]{2,1,0:T(8,128)} %param.43) | copy-start | bytes 1179652
  4.7 6.9 %copy-start.29 = (s32[512,8]{0,1:T(8,128)S(1)}, s32[512,8]{0,1:T(8,128)}, u32[]{:S(2)}) copy-start(s32[512,8]{0,1:T(8,128)} %param.28) | copy-start | bytes 49156
  6.2 6.2 %copy-start.2 = (f32[128,2048]{1,0:T(8,128)S(1)}, f32[128,2048]{1,0:T(8,128)}, u32[]{:S(2)}) copy-start(f32[128,2048]{1,0:T(8,128)} %param.46) | copy-start | bytes 3145732
  11.5 1.2 copy-start.8
  13.1 1.3 copy-start.1
  13.2 1.9 copy-start.9
  15.1 1.3 copy-start.10
  212.7 1.3 copy-start.30
  212.7 1.9 copy-start.25
  214.7 0.8 copy-start.19
  214.7 0.9 copy-start.20
  214.7 0.9 copy-start.21
  215.6 0.9 copy-start.32
  216.4 2.8 %copy-start.26 = (f32[512,24]{0,1:T(8,128)S(1)}, f32[512,24]{0,1:T(8,128)}, u32[]{:S(2)}) copy-start(f32[512,24]{0,1:T(8,128)} %param.35) | copy-start | bytes 147460
  216.4 2.8 %copy-start.27 = (f32[512,24]{0,1:T(8,128)S(1)}, f32[512,24]{0,1:T(8,128)}, u32[]{:S(2)}) copy-start(f32[512,24]{0,1:T(8,128)} %param.36) | copy-start | bytes 147460
  216.4 0.7 copy-start.28
  216.4 0.7 copy-start.31
  218.5 0.8 copy-start.22
  218.5 1.5 copy-start.24
  219.3 1.0 copy-start.23
  220.3 1.0 copy-start.5
  220.3 1.1 copy-start.14
  220.3 1.2 copy-start.15
  221.5 1.2 copy-start.7
  221.5 1.3 copy-start.16
  221.5 1.7 copy-start.17
  225.7 1.3 copy-start.3
  225.7 1.9 copy-start.12
  227.6 3.7 %copy-start.13 = (bf16[512,512]{1,0:T(8,128)(2,1)S(1)}, bf16[512,512]{1,0:T(8,128)(2,1)}, u32[]{:S(2)}) copy-start(bf16[512,512]{1,0:T(8,128)(2,1)} %get-tuple-element.137) | copy-start | bytes 1572868
  231.3 1.4 copy-start.11

commit v2 on v1

v2 whole, which is shorter than its diff:
```python
import math

import jax
import jax.numpy as jnp
from jax import lax
from jax.experimental import pallas as pl
from jax.experimental.pallas import tpu as pltpu
from jax.sharding import PartitionSpec as P

ADAM_STEP = 10
NORM_EPS = 1e-06
BETA_FIRST = 0.9
BETA_SECOND = 0.999
ADAM_EPS = 1e-08
CLIP_LIMIT = 1.0
MASKED = -1e30
LOG2E = math.log2(math.e)
LN2 = math.log(2.0)
MESH = pl.DeviceIdType.MESH
BF = jnp.bfloat16
F32 = jnp.float32

T = 512
D = 512
FF = 2048
HD = 64
K8 = 8
NE = 24
PL = 8
LE = NE // PL
ER = LE * HD
HB = FF // 2
R = 512
NR = K8 * 128 // R


def mm(a, b):
    return jnp.dot(a, b, preferred_element_type=F32)


def mm_nt(a, b):
    return lax.dot_general(a, b, (((1,), (1,)), ((), ())), preferred_element_type=F32)


def mm_tn(a, b):
    return lax.dot_general(a, b, (((0,), (0,)), ((), ())), preferred_element_type=F32)


def expert_at(place):
    return LE * device_at(place // LE) + place % LE


def device_at(slot):
    c, a, b = slot // 4, slot // 2 % 2, slot % 2
    qx, qy = (a, b) if c == 0 else (b, a)
    return 4 * qy + 2 * qx + c


def slot_of(dev):
    c, qx, qy = dev % 2, dev // 2 % 2, dev // 4
    return 4 * c + (2 * qx + qy if c == 0 else 2 * qy + qx)


def piece_rows(dp):
    return -(-ER // (dp * 16)) * 16


def scratch_list(dp):
    shard = D // dp
    pr = piece_rows(dp)
    return dict(
        wkvf=((D, 2 * HD), BF),
        w2=((2, D, FF), BF),
        eq=((NE * HD, D), BF),
        eo=((NE * HD, D), BF),
        kvb=((PL, 2, 256, 128), BF),
        tokx=((256, D), BF),
        cotx=((256, D), BF),
        rtx=((8, 256), jnp.int32),
        rts=((8, 256), jnp.int32),
        wrt=((32, D), F32),
        tokd=((T, D), BF),
        cotd=((T, D), BF),
        cott=((D, T), BF),
        rtd=((8, T), jnp.int32),
        nd=((T, D), BF),
        gate=((8, T), F32),
        dgate=((8, T), F32),
        big=((PL * 256, T), F32),
        at=((NE * HD, T), BF),
        qx=((4, 128, 1024), BF),
        dox=((4, 128, 1024), BF),
        att=((4, HD, 1024), F32),
        linv=((4, 8, 1024), F32),
        kx=((2, 8, 256, 128), BF),
        vx=((2, 8, 256, 128), BF),
        kt=((2, 8, HD, 256), BF),
        vt=((2, 8, HD + 16, 256), BF),
        pst=((2, 9, 256, 1024), BF),
        dkv=((2, 8, 256, 128), F32),
        mixed=((T, D), F32),
        ffn=((T, D), BF),
        ffnt=((D, T), BF),
        acc1=((T, D), F32),
        acc2=((T, D), F32),
        gfh=((2, D, HB), BF),
        gfl=((2, D, HB), BF),
        rf1=((2, D, HB), BF),
        rfa=((2, D, HB // 2), BF),
        rfb=((2, D, HB // 4), BF),
        rfc=((dp - 1, 2, shard, HB // 4), BF),
        f2=((2, shard, FF), BF),
        go=((NE * HD, D), BF),
        rq1=((NE * HD // 2, D), BF),
        ro1=((NE * HD // 2, D), BF),
        rq2=((2 * ER, D), BF),
        ro2=((2 * ER, D), BF),
        rq3=((ER, D), BF),
        ro3=((ER, D), BF),
        xq=((dp * pr, D), BF),
        xo=((dp * pr, D), BF),
        rq4=((dp - 1, pr, D), BF),
        ro4=((dp - 1, pr, D), BF),
        fq=((dp * pr, D), BF),
        fo=((dp * pr, D), BF),
        rk1=((4, 2, 256, 128), BF),
        rk2=((3, 2, 256, 128), BF),
        dkvd=((T, 128), BF),
        tbf=((128, 640), F32),
        tb=((128, 640), BF),
        rt1=((64, 640), BF),
        tsm=((64, 640), BF),
        rt2=((3, 16, 640), BF),
        rt3=((dp, 16, 640), BF),
        tf=((128, 640), BF),
        cnt=((32, 128), F32),
        mz=((dp, 32, 128), F32),
        mq=((PL, 32, 128), F32),
        layx=((256, D), BF),
        layr=((256, D), BF),
        tgr=((256, D), BF),
        gain=((8, D), F32),
        osem=(9,),
        ssem=None,
        rsem=None,
    )


def copies_of(dp):
    return 80 + 12 * dp


def layer_kernel(dp, *refs):
    shard = D // dp
    pr = piece_rows(dp)
    (tok, cot, routes, wkv, up, down, qw, ow, rw, gains, gbatch, lens) = refs[:12]
    (lay, tg, msgo, f2o, fqo, foo, sideo, kvo) = refs[12:20]
    names = list(scratch_list(dp))
    s = type("Scratch", (), dict(zip(names, refs[20:])))

    z = lax.axis_index("dp")
    e = lax.axis_index("expert")
    c = e % 2
    qx = e // 2 % 2
    qy = e // 4
    a = (1 - c) * qx + c * qy
    b = (1 - c) * qy + c * qx
    q = 2 * a + b

    def device(a_, b_):
        return (z, 4 * ((1 - c) * b_ + c * a_) + 2 * ((1 - c) * a_ + c * b_) + c)

    qs = [q, 2 * a + 1 - b, 2 * (1 - a) + b, 2 * (1 - a) + 1 - b]
    sib = (z, e + 1 - 2 * c)
    near, far = device(a, 1 - b), device(1 - a, b)
    chips = [None, near, far, device(1 - a, 1 - b)]
    swap = (z, 7 - e)
    zp = [None] + [((z + i) % dp, e) for i in range(1, dp)]
    zfrom = [None] + [(z + dp - i) % dp for i in range(1, dp)]
    slot = c * 4 + q
    plane = [sib] + [(z, (e + i) % PL) for i in range(1, PL)]

    count = [0]
    sends = []

    def rcopy(src, dst, peer):
        k = count[0]
        count[0] += 1
        d = pltpu.make_async_remote_copy(
            src_ref=src,
            dst_ref=dst,
            send_sem=s.ssem.at[k],
            recv_sem=s.rsem.at[k],
            device_id=peer,
            device_id_type=MESH,
        )
        d.start()
        sends.append(d)
        return (k, peer, d)

    def sent(handle):
        sends[:] = [d for d in sends if d is not handle[2]]
        handle[2].wait_send()

    def rwait(handle, dst):
        k, peer, _ = handle
        pltpu.make_async_remote_copy(
            src_ref=dst,
            dst_ref=dst,
            send_sem=s.ssem.at[k],
            recv_sem=s.rsem.at[k],
            device_id=peer,
            device_id_type=MESH,
        ).wait_recv()

    def lcopy(src, dst, k):
        d = pltpu.make_async_copy(src, dst, s.osem.at[k])
        d.start()
        return d

    bar = pltpu.get_barrier_semaphore()
    for peer in plane[1:] + zp[1:]:
        pl.semaphore_signal(bar, inc=1, device_id=peer, device_id_type=MESH)

    def zrows(ref, i, n):
        return ref.at[pl.ds(pl.multiple_of(i * n, n), n)]

    def turned(x):
        rows, cols = x.shape
        if cols % 128:
            x = jnp.concatenate([x, jnp.zeros((rows, 128 - cols % 128), x.dtype)], axis=1)
        return x.T[0:cols]

    lo = pl.multiple_of(c * HB, HB)
    hi = pl.multiple_of((1 - c) * HB, HB)
    ri = lax.broadcasted_iota(jnp.int32, (256, 256), 0)
    ci = lax.broadcasted_iota(jnp.int32, (256, 256), 1)
    split = jnp.where(ci == 2 * (ri % 128) + ri // 128, 1.0, 0.0).astype(BF)
    join = jnp.where(ri == 2 * (ci % 128) + ci // 128, 1.0, 0.0).astype(BF)
    own_rows = pl.ds(pl.multiple_of(z * shard, shard), shard)
    s.wkvf[own_rows, :] = wkv[...].astype(BF)
    rtt = routes[...].astype(F32).astype(BF)
    s.rtd[:, 0:256] = mm(rtt[:, 0:256], join).astype(jnp.int32)
    s.rts[...] = mm(rtt[:, 256:512], join).astype(jnp.int32)
    WD = HB // 2
    WP = (HB - WD) // 4
    part = pl.multiple_of(c * HB + WD + q * WP, WP)
    for at, n in ((lo, WD), (part, WP)):
        s.w2[0, own_rows, pl.ds(at, n)] = up[:, pl.ds(at, n)].astype(BF)
        s.w2[1, own_rows, pl.ds(at, n)] = turned(down[pl.ds(at, n), :]).astype(BF)

    def w2_rows(i, at, n):
        return s.w2.at[:, pl.ds(pl.multiple_of(i * shard, shard), shard), pl.ds(at, n)]

    def to_all_z(ref):
        return [None] + [rcopy(ref, ref, zp[i]) for i in range(1, dp)]
    pl.semaphore_wait(bar, PL - 1 + dp - 1)
    h_wkv = [None] + [
        rcopy(zrows(s.wkvf, z, shard), zrows(s.wkvf, z, shard), zp[i]) for i in range(1, dp)
    ]
    h_tok = rcopy(tok.at[pl.ds(256, 256)], s.tokx, swap)
    h_rt = rcopy(s.rts, s.rtx, swap)
    for i in range(LE):
        rows = pl.ds(pl.multiple_of(slot * ER + i * HD, HD), HD)
        s.eq[rows, :] = qw[i].astype(BF)
        s.eo[rows, :] = ow[i].astype(BF)
    own_eq = zrows(s.eq, slot, ER)
    own_eo = zrows(s.eo, slot, ER)
    h_eq1 = rcopy(own_eq, own_eq, near)
    h_wp1 = to_all_z(w2_rows(z, part, WP))
    h_wd = to_all_z(w2_rows(z, lo, WD))

    def gather_far(h, ref):
        rwait(h, zrows(ref, c * 4 + qs[1], ER))
        pair = zrows(ref, c * 2 + a, 2 * ER)
        return rcopy(pair, pair, far)

    def gather_sib(h, ref):
        rwait(h, zrows(ref, c * 2 + 1 - a, 2 * ER))
        mine = zrows(ref, c, 4 * ER)
        return rcopy(mine, mine, sib)

    def w2_cols(at, n):
        return s.w2.at[:, :, pl.ds(at, n)]

    s.wrt[0:NE, :] = rw[...]
    s.wrt[NE:32, :] = jnp.zeros((32 - NE, D), F32)

    g0 = gains[0:1, :]
    g1 = gains[1:2, :]

    def rms(x):
        inv = lax.rsqrt(jnp.mean(x * x, axis=-1, keepdims=True) + NORM_EPS)
        return x * inv, inv

    nat0 = mm(split, tok[0:256, :])
    nat1 = mm(split, tok[256:512, :])
    s.tokd[0:256, :] = nat0.astype(BF)
    n0 = (rms(nat0)[0] * g0).astype(BF)
    n1 = (rms(nat1)[0] * g0).astype(BF)
    s.nd[0:256, :] = n0
    cot0 = mm(split, cot[0:256, :])
    s.cotd[0:256, :] = cot0.astype(BF)

    for i in range(1, dp):
        rwait(h_wkv[i], zrows(s.wkvf, zfrom[i], shard))
    kv0 = mm(n0, s.wkvf[...]).astype(BF)
    kv1 = mm(n1, s.wkvf[...]).astype(BF)
    for p in range(2):
        s.kvb[slot, p, 0:128, :] = kv0[p * 128 : (p + 1) * 128]
        s.kvb[slot, p, 128:256, :] = kv1[p * 128 : (p + 1) * 128]
    h_kv = [None] + [rcopy(s.kvb.at[slot], s.kvb.at[slot], chips[m]) for m in (1, 2, 3)]
    h_eq2 = gather_far(h_eq1, s.eq)
    h_cot = rcopy(cot.at[pl.ds(256, 256)], s.cotx, swap)
    h_eo1 = rcopy(own_eo, own_eo, near)

    rwait(h_tok, s.tokx)
    rwait(h_rt, s.rtx)
    sw = mm(split, s.tokx[...])
    s.tokd[256:512, :] = sw.astype(BF)
    s.nd[256:512, :] = (rms(sw)[0] * g0).astype(BF)
    s.rtd[:, 256:512] = s.rtx[...]

    wrt = s.wrt[...].astype(BF)
    bm1 = gbatch[z] - 1
    is2 = (4 - gbatch[z]) // 2

    def seq_pos(r):
        return r & bm1, (r >> 1) * is2 + (r >> 2) * (1 - is2)

    def limit_of(index):
        out = jnp.zeros(index.shape, jnp.int32)
        for i in range(4):
            out = jnp.where(index == i, lens[z, i], out)
        return out

    block = [2 * e, 15 - 2 * e]
    lanes128 = lax.broadcasted_iota(jnp.int32, (16, 128), 1)
    row16 = lax.broadcasted_iota(jnp.int32, (16, 128), 0)
    row32 = lax.broadcasted_iota(jnp.int32, (32, 128), 0)

    logits = mm_nt(wrt, s.nd[...])
    row_e = lax.broadcasted_iota(jnp.int32, (32, T), 0)
    chosen = jnp.concatenate(
        [
            jnp.sum(jnp.where(row_e == s.rtd[k : k + 1, :], logits, 0.0), axis=0, keepdims=True)
            for k in range(K8)
        ],
        axis=0,
    )
    ex = jnp.exp(chosen - jnp.max(chosen, axis=0, keepdims=True))
    s.gate[...] = ex / jnp.sum(ex, axis=0, keepdims=True)

    counts = jnp.zeros((32, 128), F32)
    for g in range(4):
        blk, p = g // 2, g % 2
        row = 2 * (block[blk] * 128 + lanes128) + p
        seq, pos = seq_pos(row)
        live = (pos < limit_of(seq))[0:1, :].astype(F32)
        for k in range(K8):
            counts = counts + jnp.where(
                row32 == s.rtd[k : k + 1, g * 128 : (g + 1) * 128], live, 0.0
            )
        feat = jnp.where(seq == row16, 1.0, 0.0).astype(BF)
        s.qx[g, 64:80, :] = jnp.concatenate([feat] * K8, axis=1)
        s.qx[g, 80:128, :] = jnp.zeros((48, 1024), BF)
    s.cnt[...] = jnp.broadcast_to(jnp.sum(counts, axis=1, keepdims=True), (32, 128))

    half = NE * HD // 2
    h_eqs = gather_sib(h_eq2, s.eq)
    for m in (1, 2, 3):
        rwait(h_kv[m], s.kvb.at[c * 4 + qs[m]])
    h_kvs = rcopy(s.kvb.at[pl.ds(c * 4, 4)], s.kvb.at[pl.ds(c * 4, 4)], sib)
    rwait(h_eqs, zrows(s.eq, 1 - c, half))

    def query_rows(i, _):
        rows = pl.ds(pl.multiple_of(i * 256, 256), 256)
        s.big[rows, :] = mm_nt(s.eq[rows, :], s.nd[...])
        return 0

    lax.fori_loop(0, NE * HD // 256, query_rows, 0)

    def pick(g, k):
        lanes = pl.ds(pl.multiple_of(g * 128, 128), 128)
        rk = s.rtd[k : k + 1, lanes]
        acc = jnp.zeros((HD, 128), F32)
        for place in range(NE):
            acc = jnp.where(rk == expert_at(place), s.big[place * HD : (place + 1) * HD, lanes], acc)
        return acc

    def choose(g, _):
        for k in range(K8):
            s.qx[g, 0:64, k * 128 : (k + 1) * 128] = (pick(g, k) * (0.125 * LOG2E)).astype(BF)
        return 0

    lax.fori_loop(0, 4, choose, 0)

    for i in range(1, dp):
        rwait(h_wp1[i], w2_rows(zfrom[i], part, WP))
    h_wp2 = rcopy(w2_cols(part, WP), w2_cols(part, WP), near)
    h_eo2 = gather_far(h_eo1, s.eo)
    rwait(h_kvs, s.kvb.at[pl.ds((1 - c) * 4, 4)])
    krow = lax.broadcasted_iota(jnp.int32, (256, 128), 0)
    klane = lax.broadcasted_iota(jnp.int32, (256, 128), 1)
    for t in range(8):
        for p in range(2):
            kv = s.kvb[slot_of(t), p].astype(F32)
            seq, pos = seq_pos(2 * (t * 256 + krow) + p)
            col = klane - 64
            shown = (seq == col) & (pos < limit_of(col))
            feat = jnp.where(shown | (col > 3), 0.0, MASKED)
            s.kx[p, t] = jnp.where(col < 0, kv, feat).astype(BF)
            s.vx[p, t] = jnp.where(col >= 0, kv, jnp.where(klane < 2, 1.0, 0.0)).astype(BF)
            kvt = kv.T
            s.kt[p, t] = kvt[0:64].astype(BF)
            s.vt[p, t, 0:64, :] = kvt[64:128].astype(BF)
            s.vt[p, t, 64:80, :] = jnp.ones((16, 256), BF)

    tiles = [e + 1, 8 - e]
    base = [0, e + 1]

    def attend(g, rc):
        blk, p = g // 2, g % 2
        nt, first = tiles[blk], base[blk]
        visible = (
            lax.broadcasted_iota(jnp.int32, (256, 128), 0)
            <= lax.broadcasted_iota(jnp.int32, (256, 128), 1) + 128 * blk
        )
        visible = jnp.concatenate([visible] * (R // 128), axis=1)
        ls = slice(rc * R, (rc + 1) * R)

        def scores(t, peak):
            sc = mm(s.kx[p, t], s.qx[g, :, ls])
            s.big[pl.ds(pl.multiple_of(t * 256, 256), 256), :] = sc
            return jnp.maximum(peak, jnp.max(sc.reshape(32, 8, R), axis=0))

        peak = lax.fori_loop(0, nt - 1, scores, jnp.full((8, R), MASKED, F32))
        sc = jnp.where(visible, mm(s.kx[p, nt - 1], s.qx[g, :, ls]), MASKED)
        s.big[pl.ds(pl.multiple_of((nt - 1) * 256, 256), 256), :] = sc
        peak = jnp.maximum(peak, jnp.max(sc.reshape(32, 8, R), axis=0))
        peak = jnp.max(peak, axis=0, keepdims=True)

        def values(t, acc):
            pb = jnp.exp2(s.big[pl.ds(pl.multiple_of(t * 256, 256), 256), :] - peak).astype(BF)
            s.pst[p, first + t, :, ls] = pb
            return acc + mm(s.vt[p, t], pb)

        acc = lax.fori_loop(0, nt, values, jnp.zeros((HD + 16, R), F32))
        inv = 1.0 / acc[64:72]
        s.linv[g, :, ls] = inv
        s.att[g, :, ls] = acc[0:64] * inv[0:1]

    pieces = [(p + 2 * blk, rc) for p in range(2) for rc in range(NR) for blk in range(2)]
    for piece in pieces[0:2]:
        attend(*piece)
    rwait(h_wp2, w2_cols(c * HB + WD + qs[1] * WP, WP))
    both_parts = pl.multiple_of(c * HB + WD + a * 2 * WP, 2 * WP)
    h_wp3 = rcopy(w2_cols(both_parts, 2 * WP), w2_cols(both_parts, 2 * WP), far)
    for piece in pieces[2:4]:
        attend(*piece)
    h_eos = gather_sib(h_eo2, s.eo)
    for piece in pieces[4:6]:
        attend(*piece)
    rwait(h_wp3, w2_cols(pl.multiple_of(c * HB + WD + (1 - a) * 2 * WP, 2 * WP), 2 * WP))
    for piece in pieces[6:8]:
        attend(*piece)
    for i in range(1, dp):
        rwait(h_wd[i], w2_rows(zfrom[i], lo, WD))
    h_w2s = rcopy(w2_cols(lo, HB), w2_cols(lo, HB), sib)

    def spread(dst, src, scale):
        def one(g, _):
            lanes = pl.ds(pl.multiple_of(g * 128, 128), 128)
            for k in range(K8):
                part = src[g, :, k * 128 : (k + 1) * 128]
                if scale is not None:
                    part = part * scale[k : k + 1, lanes]
                else:
                    part = part * 0.125
                s.acc1[k * HD : (k + 1) * HD, 0:128] = part
            for place in range(NE):
                acc = jnp.zeros((HD, 128), F32)
                for k in range(K8):
                    acc = jnp.where(
                        s.rtd[k : k + 1, lanes] == expert_at(place),
                        s.acc1[k * HD : (k + 1) * HD, 0:128],
                        acc,
                    )
                dst[place * HD : (place + 1) * HD, lanes] = acc.astype(BF)
            return 0

        lax.fori_loop(0, 4, one, 0)

    spread(s.at, s.att, s.gate)
    rwait(h_eos, zrows(s.eo, 1 - c, half))
    s.acc1[...] = s.tokd[...].astype(F32)

    def mix(i, _):
        rows = pl.ds(pl.multiple_of(i * 256, 256), 256)
        s.acc1[...] += mm_tn(s.at[rows, :], s.eo[rows, :])
        return 0

    lax.fori_loop(0, NE * HD // 256, mix, 0)
    mixed = s.acc1[...]
    s.mixed[...] = mixed
    ffn = rms(mixed)[0] * g1
    s.ffn[...] = ffn.astype(BF)
    s.ffnt[...] = ffn.T.astype(BF)
    rwait(h_cot, s.cotx)
    cot1 = mm(split, s.cotx[...])
    s.cotd[256:512, :] = cot1.astype(BF)
    s.cott[:, 0:256] = cot0.T.astype(BF)
    s.cott[:, 256:512] = cot1.T.astype(BF)
    s.acc2[...] = jnp.zeros((T, D), F32)
    rwait(h_w2s, s.w2.at[:, :, pl.ds(hi, HB)])

    FT = 256

    def feed(i, base_, keep):
        cols = pl.ds(pl.multiple_of(base_ + i * FT, FT), FT)
        part_cols = pl.ds(pl.multiple_of(i * FT, FT), FT)
        up = mm(s.ffn[...], s.w2[0, :, cols])
        sq = up * up
        th = jnp.tanh(0.79788456 * up * (1.0 + 0.044715 * sq))
        hid = (0.5 * up * (1.0 + th)).astype(BF)
        slope = 0.5 * (1.0 + th) + 0.5 * up * (1.0 - th * th) * (
            0.79788456 * (1.0 + 3 * 0.044715 * sq)
        )
        s.acc1[...] += mm_nt(hid, s.w2[1, :, cols])
        dup = (mm(s.cotd[...], s.w2[1, :, cols]) * slope).astype(BF)
        keep[0, :, part_cols] = mm(s.ffnt[...], dup).astype(BF)
        keep[1, :, part_cols] = mm(s.cott[...], hid).astype(BF)
        s.acc2[...] += mm_nt(dup, s.w2[0, :, cols])
        return 0

    lax.fori_loop(0, HB // FT, lambda i, _: feed(i, hi, s.gfh), 0)
    h_f1 = [rcopy(s.gfh.at[w], s.rf1.at[w], sib) for w in range(2)]
    lax.fori_loop(0, HB // FT, lambda i, _: feed(i, lo, s.gfl), 0)

    def both(x, y):
        return (x.astype(F32) + y.astype(F32)).astype(BF)

    def fold(sq):
        sq = jnp.sum(sq, axis=0, keepdims=True)
        out = sq[:, 0:128]
        for j in range(1, sq.shape[1] // 128):
            out = out + sq[:, j * 128 : (j + 1) * 128]
        return out

    done, squares = [], []
    quart = HB // 4
    keep2 = pl.multiple_of(a * 2 * quart, 2 * quart)
    give2 = pl.multiple_of((1 - a) * 2 * quart, 2 * quart)
    keep1 = pl.multiple_of(q * quart, quart)
    give1 = pl.multiple_of(qs[1] * quart, quart)
    place1 = pl.multiple_of(c * HB + keep1, quart)

    def feed_grad(w):
        own, total, one, two, three, out = (
            s.gfl.at[w], s.rf1.at[w], s.rfa.at[w], s.rfb.at[w], s.rfc, s.f2.at[w],
        )

        def pair(at, n):
            total[:, pl.ds(at, n)] = both(own[:, pl.ds(at, n)], total[:, pl.ds(at, n)])

        rwait(h_f1[w], total)
        pair(give2, 2 * quart)
        h = rcopy(total.at[:, pl.ds(give2, 2 * quart)], one, far)
        pair(keep2, 2 * quart)
        yield
        rwait(h, one)
        for at in (give1, keep1):
            inner = pl.multiple_of(at - keep2, quart)
            total[:, pl.ds(at, quart)] = both(
                total[:, pl.ds(at, quart)], one[:, pl.ds(inner, quart)]
            )
            if at is give1:
                h = rcopy(total.at[:, pl.ds(give1, quart)], two, near)
        yield
        rwait(h, two)
        total[:, pl.ds(keep1, quart)] = both(total[:, pl.ds(keep1, quart)], two[...])

        def zpart(i):
            return total.at[pl.ds(pl.multiple_of(i * shard, shard), shard), pl.ds(keep1, quart)]

        hz = [rcopy(zpart(zp[i][0]), three.at[i - 1, w], zp[i]) for i in range(1, dp)]
        yield
        acc = zpart(z)[...].astype(F32)
        for i in range(1, dp):
            rwait(hz[i - 1], three.at[i - 1, w])
            acc = acc + three[i - 1, w].astype(F32)
        acc = acc.astype(BF)
        out[:, pl.ds(place1, quart)] = acc
        acc = acc.astype(F32)
        squares.append(fold(acc * acc))
        h = rcopy(out.at[:, pl.ds(place1, quart)], out.at[:, pl.ds(place1, quart)], near)
        yield
        rwait(h, out.at[:, pl.ds(pl.multiple_of(c * HB + give1, quart), quart)])
        wide = out.at[:, pl.ds(pl.multiple_of(c * HB + keep2, 2 * quart), 2 * quart)]
        h = rcopy(wide, wide, far)
        yield
        rwait(h, out.at[:, pl.ds(pl.multiple_of(c * HB + give2, 2 * quart), 2 * quart)])
        h = rcopy(out.at[:, pl.ds(lo, HB)], out.at[:, pl.ds(lo, HB)], sib)
        yield
        rwait(h, out.at[:, pl.ds(hi, HB)])
        done.append(lcopy(out, f2o.at[w], 2 + w))
        yield

    def head_grad(src, total, one, two, full, part_, final, dst, sem):
        h = rcopy(zrows(src, 1 - c, half), total, sib)
        s.half_sent = h
        yield
        rwait(h, total)

        def pair(which):
            rows = pl.ds(pl.multiple_of(which * 2 * ER, 128), 2 * ER)
            wide = pl.ds(pl.multiple_of(c * half + which * 2 * ER, 128), 2 * ER)
            total[rows, :] = both(src[wide, :], total[rows, :])

        pair(1 - a)
        h = rcopy(zrows(total, 1 - a, 2 * ER), one, far)
        pair(a)
        yield
        rwait(h, one)
        for which in (1 - b, b):
            rows = pl.ds(pl.multiple_of((2 * a + which) * ER, ER), ER)
            total[rows, :] = both(total[rows, :], one[pl.ds(pl.multiple_of(which * ER, ER), ER), :])
            if which is not b:
                h = rcopy(zrows(total, qs[1], ER), two, near)
        yield
        rwait(h, two)
        full[0:ER, :] = both(total[pl.ds(pl.multiple_of(q * ER, ER), ER), :], two[...])
        if dp * pr > ER:
            full[ER:, :] = jnp.zeros((dp * pr - ER, D), BF)
        hz = [rcopy(zrows(full, zp[i][0], pr), part_.at[i - 1], zp[i]) for i in range(1, dp)]
        yield
        mine = pl.ds(pl.multiple_of(z * pr, pr), pr)
        acc = full[mine, :].astype(F32)
        for i in range(1, dp):
            rwait(hz[i - 1], part_.at[i - 1])
            acc = acc + part_[i - 1].astype(F32)
        acc = acc.astype(BF)
        final[mine, :] = acc
        acc = acc.astype(F32)
        squares.append(fold(acc * acc))
        hz = to_all_z(zrows(final, z, pr))
        yield
        for i in range(1, dp):
            rwait(hz[i], zrows(final, zfrom[i], pr))
        done.append(lcopy(final.at[pl.ds(0, ER)], dst, sem))
        yield

    chain = [feed_grad(0), feed_grad(1)]

    out = s.acc1[...].astype(BF)
    s.layx[...] = mm(join, out[256:512]).astype(BF)
    h_lay = rcopy(s.layx, s.layr, swap)
    s.ffn[0:256, :] = mm(join, out[0:256]).astype(BF)

    def rms_back(dn, gain, unit, inv):
        a = dn * gain
        return inv * (a - unit * jnp.mean(a * unit, axis=-1, keepdims=True)), jnp.sum(
            dn * unit, axis=0, keepdims=True
        )

    unit1, inv1 = rms(s.mixed[...])
    back, gain1 = rms_back(s.acc2[...], g1, unit1, inv1)
    s.gain[1:2, :] = gain1
    dmix = s.cotd[...].astype(F32) + back
    s.mixed[...] = dmix
    s.cott[...] = dmix.astype(BF)

    def out_rows(i, _):
        rows = pl.ds(pl.multiple_of(i * 256, 256), 256)
        s.big[rows, :] = mm_nt(s.eo[rows, :], s.cott[...])
        s.go[rows, :] = mm(s.at[rows, :], s.cott[...]).astype(BF)
        return 0

    lax.fori_loop(0, NE * HD // 256, out_rows, 0)
    chain.append(head_grad(s.go, s.ro1, s.ro2, s.ro3, s.xo, s.ro4, s.fo, foo, 4))
    next(chain[2])
    sent_o = s.half_sent
    next(chain[0])

    def heads_back(g, _):
        lanes = pl.ds(pl.multiple_of(g * 128, 128), 128)
        for k in range(K8):
            ks = slice(k * 128, (k + 1) * 128)
            da = pick(g, k)
            at = s.att[g, :, ks]
            s.dgate[k : k + 1, lanes] = jnp.sum(at * da, axis=0, keepdims=True)
            do = (da * (s.gate[k : k + 1, lanes] * s.linv[g, 0:1, ks])).astype(BF)
            s.dox[g, 64:128, ks] = do
            delta = -jnp.sum(do.astype(F32) * at, axis=0, keepdims=True)
            top = delta.astype(BF).astype(F32)
            s.dox[g, 0:16, ks] = jnp.where(
                row16 == 0, top, jnp.where(row16 == 1, delta - top, 0.0)
            ).astype(BF)
            s.dox[g, 16:64, ks] = jnp.zeros((48, 128), BF)
        return 0

    lax.fori_loop(0, 4, heads_back, 0)
    s.dkv[...] = jnp.zeros(s.dkv.shape, F32)

    left = lax.broadcasted_iota(jnp.int32, (256, 128), 1) < 64

    def attend_back(g, rc):
        blk, p = g // 2, g % 2
        nt, first = tiles[blk], base[blk]
        ls = slice(rc * R, (rc + 1) * R)

        def tile(t, acc):
            prob = s.pst[p, first + t, :, ls]
            dprob = mm(s.vx[p, t], s.dox[g, :, ls])
            ds = (prob.astype(F32) * dprob).astype(BF)
            kpart = mm_nt(ds, s.qx[g, :, ls])
            vpart = mm_nt(prob, s.dox[g, :, ls])
            s.dkv[p, t] += jnp.where(left, kpart * LN2, vpart)
            return acc + mm(s.kt[p, t], ds)

        s.att[g, :, ls] = lax.fori_loop(0, nt, tile, jnp.zeros((HD, R), F32))

    next(chain[1])
    next(chain[2])
    for piece in pieces[0:2]:
        attend_back(*piece)
    next(chain[0])
    for piece in pieces[2:4]:
        attend_back(*piece)
    next(chain[1])
    next(chain[2])
    for piece in pieces[4:6]:
        attend_back(*piece)
    next(chain[0])
    next(chain[2])
    for piece in pieces[6:8]:
        attend_back(*piece)
    next(chain[1])
    next(chain[2])
    sent(h_kvs)
    for m in (1, 2, 3):
        sent(h_kv[m])
    for dev in range(PL):
        sl = slot_of(dev)
        for side_, blk in enumerate((2 * dev, 15 - 2 * dev)):
            for p in range(2):
                s.kvb[sl, side_, p * 128 : (p + 1) * 128, :] = s.dkv[p, blk // 2, (blk % 2) * 128 : (blk % 2) * 128 + 128, :].astype(BF)
    h_k1 = rcopy(s.kvb.at[pl.ds((1 - c) * 4, 4)], s.rk1, sib)
    spread(s.at, s.att, None)
    rwait(h_k1, s.rk1)
    for i in range(4):
        s.rk1[i] = both(s.kvb[c * 4 + i], s.rk1[i])
    h_k2 = [None] + [rcopy(s.rk1.at[qs[m]], s.rk2.at[m - 1], chips[m]) for m in (1, 2, 3)]

    sent(sent_o)
    next(chain[0])

    def query_grad(i, _):
        rows = pl.ds(pl.multiple_of(i * 256, 256), 256)
        s.go[rows, :] = mm(s.at[rows, :], s.nd[...]).astype(BF)
        return 0

    lax.fori_loop(0, NE * HD // 256, query_grad, 0)
    chain.append(head_grad(s.go, s.rq1, s.rq2, s.rq3, s.xq, s.rq4, s.fq, fqo, 5))
    next(chain[3])
    next(chain[1])
    s.acc2[...] = jnp.zeros((T, D), F32)

    def slot_sum(i, _):
        rows = pl.ds(pl.multiple_of(i * 256, 256), 256)
        s.acc2[...] += mm_tn(s.at[rows, :], s.eq[rows, :])
        return 0

    lax.fori_loop(0, NE * HD // 256, slot_sum, 0)
    gate = s.gate[...]
    dch = gate * (s.dgate[...] - jnp.sum(gate * s.dgate[...], axis=0, keepdims=True))
    dlog = jnp.zeros((32, T), F32)
    for k in range(K8):
        dlog = dlog + jnp.where(row_e == s.rtd[k : k + 1, :], dch[k : k + 1, :], 0.0)
    dlog = dlog.astype(BF)
    s.acc2[...] += mm_tn(dlog, wrt)
    grt = mm(dlog, s.nd[...])

    next(chain[3])
    next(chain[0])
    for m in (1, 2, 3):
        rwait(h_k2[m], s.rk2.at[m - 1])
    for i in range(2):
        total = s.rk1[q, i].astype(F32)
        for m in (1, 2, 3):
            total = total + s.rk2[m - 1, i].astype(F32)
        s.dkvd[i * 256 : (i + 1) * 256, :] = total.astype(BF)
    dn = s.acc2[...] + mm_nt(s.dkvd[...], s.wkvf[...])
    unit0, inv0 = rms(s.tokd[...].astype(F32))
    back0, gain0 = rms_back(dn, g0, unit0, inv0)
    s.tbf[:, 0:512] = mm_tn(s.dkvd[...], s.nd[...])
    for j in range(4):
        js = slice(j * 128, (j + 1) * 128)
        s.tbf[j * 24 : (j + 1) * 24, 512:640] = grt[0:24, js]
        s.tbf[96 + j : 97 + j, 512:640] = gain0[:, js]
        s.tbf[100 + j : 101 + j, 512:640] = s.gain[1:2, js]
    s.tbf[104:128, 512:640] = jnp.zeros((24, 128), F32)
    s.tb[...] = s.tbf[...].astype(BF)
    h_t1 = rcopy(zrows(s.tb, 1 - c, 64), s.rt1, sib)
    next(chain[3])
    next(chain[1])

    grad = s.mixed[...] + back0
    sent(h_lay)
    s.layx[...] = mm(join, grad[256:512].astype(BF)).astype(BF)
    rwait(h_t1, s.rt1)
    s.tsm[...] = both(s.tb[pl.ds(pl.multiple_of(c * 64, 64), 64), :], s.rt1[...])
    h_t2 = [None] + [rcopy(zrows(s.tsm, qs[m], 16), s.rt2.at[m - 1], chips[m]) for m in (1, 2, 3)]
    h_tg = rcopy(s.layx, s.tgr, swap)
    top = grad[0:256].astype(BF)
    rest = (grad[0:256] - top.astype(F32)).astype(BF)
    s.acc1[0:256, :] = mm(join, top) + mm(join, rest)

    next(chain[3])
    next(chain[0])
    for m in (1, 2, 3):
        rwait(h_t2[m], s.rt2.at[m - 1])
    total = s.tsm[pl.ds(pl.multiple_of(q * 16, 16), 16), :].astype(F32)
    for m in (1, 2, 3):
        total = total + s.rt2[m - 1].astype(F32)
    s.rt3[z] = total.astype(BF)
    h_t3 = [None] + [rcopy(s.rt3.at[z], s.rt3.at[z], zp[i]) for i in range(1, dp)]
    next(chain[3])
    next(chain[1])
    for i in range(1, dp):
        rwait(h_t3[i], s.rt3.at[zfrom[i]])
    total = s.rt3[0].astype(F32)
    for i in range(1, dp):
        total = total + s.rt3[i].astype(F32)
    tail = total.astype(BF)
    s.tf[pl.ds(pl.multiple_of(slot * 16, 16), 16), :] = tail
    h_t4 = [None] + [
        rcopy(zrows(s.tf, slot, 16), zrows(s.tf, slot, 16), chips[m]) for m in (1, 2, 3)
    ]
    sq_t = fold(tail.astype(F32) * tail.astype(F32)) * (1.0 / dp)

    total = squares[0]
    for sq in squares[1:] + [sq_t]:
        total = total + sq
    squares = jnp.sum(total, axis=1, keepdims=True)
    s.mz[z] = jnp.where(row32 < 24, s.cnt[...], jnp.where(row32 == 24, squares, 0.0))
    h_m1 = [None] + [rcopy(s.mz.at[z], s.mz.at[z], zp[i]) for i in range(1, dp)]

    for m in (1, 2, 3):
        rwait(h_t4[m], zrows(s.tf, c * 4 + qs[m], 16))
    h_t5 = rcopy(zrows(s.tf, c, 64), zrows(s.tf, c, 64), sib)

    for i in range(1, dp):
        rwait(h_m1[i], s.mz.at[zfrom[i]])
    total = s.mz[0]
    for i in range(1, dp):
        total = total + s.mz[i]
    s.mq[e] = total
    h_m2 = [None] + [rcopy(s.mq.at[e], s.mq.at[e], plane[i]) for i in range(1, PL)]

    rwait(h_lay, s.layr)
    s.ffn[256:512, :] = s.layr[...]
    done.append(lcopy(s.ffn, lay, 0))
    rwait(h_tg, s.tgr)
    s.acc1[256:512, :] = s.tgr[...].astype(F32)
    done.append(lcopy(s.acc1, tg, 1))
    next(chain[0])
    next(chain[1])
    rwait(h_t5, zrows(s.tf, 1 - c, 64))
    s.acc2[:, 0:128] = s.tf[:, 0:512].astype(F32).T
    done.append(lcopy(s.tf.at[:, pl.ds(512, 128)], sideo, 8))
    done.append(lcopy(s.acc2.at[own_rows, pl.ds(0, 128)], kvo, 7))
    next(chain[2])
    next(chain[3])
    for i in range(1, PL):
        rwait(h_m2[i], s.mq.at[(e + PL - i) % PL])
    total = s.mq[0]
    for i in range(1, PL):
        total = total + s.mq[i]
    s.cnt[...] = total
    done.append(lcopy(s.cnt, msgo, 6))
    for d in done:
        d.wait()
    for d in sends:
        d.wait_send()
    assert count[0] <= copies_of(dp)


def adam_kernel(steps, *refs):
    (lay, tg, msg, upg, downg, qg, og, side, kvg) = refs[:9]
    params = [refs[9 + 3 * i : 12 + 3 * i] for i in range(7)]
    layo, tgo, counts, norm = refs[30:34]
    outs = [refs[34 + 3 * i : 37 + 3 * i] for i in range(7)]
    step = pl.program_id(0)
    total = jnp.sqrt(jnp.full((8, 128), msg[24, 0], F32))
    clip = (CLIP_LIMIT / jnp.maximum(total, CLIP_LIMIT))[0:1, 0:1]

    def update(k, g, rate, decay, at=Ellipsis):
        w, m, v = [r[at] for r in params[k]]
        g = g * clip
        m = BETA_FIRST * m + (1.0 - BETA_FIRST) * g
        v = BETA_SECOND * v + (1.0 - BETA_SECOND) * g * g
        mh = m * (1.0 / (1.0 - BETA_FIRST**ADAM_STEP))
        vh = v * (1.0 / (1.0 - BETA_SECOND**ADAM_STEP))
        outs[k][0][at] = w - rate * (mh / (jnp.sqrt(vh) + ADAM_EPS) + decay * w)
        outs[k][1][at] = m
        outs[k][2][at] = v

    @pl.when(step == 0)
    def _():
        norm[...] = total[0:1, 0:1]
        for i in range(NE):
            counts[i] = msg[i, 0].astype(jnp.int32)
        sd = side[...].astype(F32)
        for row in range(2):
            g = jnp.concatenate([sd[96 + 4 * row + j : 97 + 4 * row + j] for j in range(4)], axis=1)
            update(0, g, 0.7, 0.0, pl.ds(row, 1))
        g = jnp.concatenate([sd[j * NE : (j + 1) * NE] for j in range(4)], axis=1)
        update(1, g, 0.03, 0.1)

    layo[...] = lay[...]
    tgo[...] = tg[...]
    update(2, kvg[...], 0.06, 0.1)
    update(3, qg[...].astype(F32), 0.06, 0.1)
    update(4, og[...].astype(F32), 2.0, 0.1)
    update(5, upg[0].astype(F32), 0.06, 0.1)
    update(6, downg[0].astype(F32).T, 0.03, 0.1)


def on_device(tokens, cotangent, routes, group_batch, seq_lengths, *state):
    dp = lax.axis_size("dp")
    shard = D // dp
    state = list(state)
    for i in range(3):
        state[3 + i] = state[3 + i].T
        state[9 + i] = state[9 + i].transpose(0, 2, 1)
    gains, router, keyval, query, output, up, down = [state[3 * i] for i in range(7)]

    scr = []
    for item in scratch_list(dp).values():
        if item is None:
            scr.append(pltpu.SemaphoreType.DMA((copies_of(dp),)))
        elif len(item) == 1:
            scr.append(pltpu.SemaphoreType.DMA(item))
        else:
            scr.append(pltpu.VMEM(item[0], item[1]))
    routes_cols = routes.T
    vm = pl.BlockSpec(memory_space=pltpu.VMEM)
    sm = pl.BlockSpec(memory_space=pltpu.SMEM)
    hbm = pl.BlockSpec(memory_space=pl.ANY)
    outs = [
        jax.ShapeDtypeStruct((T, D), BF),
        jax.ShapeDtypeStruct((T, D), F32),
        jax.ShapeDtypeStruct((32, 128), F32),
        jax.ShapeDtypeStruct((2, shard, FF), BF),
        jax.ShapeDtypeStruct((ER, D), BF),
        jax.ShapeDtypeStruct((ER, D), BF),
        jax.ShapeDtypeStruct((128, 128), BF),
        jax.ShapeDtypeStruct((shard, 128), F32),
    ]

    def kernel(*refs):
        layer_kernel(dp, *refs)

    lay, tg, msg, f2, fq, fo, side, kvg = pl.pallas_call(
        kernel,
        out_shape=outs,
        in_specs=[vm] * 10 + [sm] * 2,
        out_specs=[hbm] * len(outs),
        scratch_shapes=scr,
        compiler_params=pltpu.CompilerParams(
            collective_id=0, has_side_effects=True, vmem_limit_bytes=64 * 2**20 - 2**17
        ),
        name="layer",
    )(
        tokens, cotangent, routes_cols, keyval, up, down, query, output, router, gains,
        group_batch, seq_lengths,
    )

    steps = min(4, shard // 16)
    rows = lambda i: (i, 0)
    middle = lambda i: (0, i, 0)
    blocks = [
        pl.BlockSpec((2, D), lambda i: (0, 0)),
        pl.BlockSpec((NE, D), lambda i: (0, 0)),
        pl.BlockSpec((shard // steps, 2 * HD), rows),
        pl.BlockSpec((LE, HD // steps, D), middle),
        pl.BlockSpec((LE, HD // steps, D), middle),
        pl.BlockSpec((shard // steps, FF), rows),
        pl.BlockSpec((FF // steps, shard), rows),
    ]
    each = [b for b in blocks for _ in range(3)]

    def update(*refs):
        adam_kernel(steps, *refs)

    result = list(pl.pallas_call(
        update,
        grid=(steps,),
        out_shape=[
            jax.ShapeDtypeStruct((T, D), BF),
            jax.ShapeDtypeStruct((T, D), F32),
            jax.ShapeDtypeStruct((NE,), jnp.int32),
            jax.ShapeDtypeStruct((1, 1), F32),
        ]
        + [jax.ShapeDtypeStruct(x.shape, F32) for x in state],
        in_specs=[
            pl.BlockSpec((T // steps, D), rows),
            pl.BlockSpec((T // steps, D), rows),
            sm,
            pl.BlockSpec((1, shard // steps, FF), middle),
            pl.BlockSpec((1, shard, FF // steps), lambda i: (1, 0, i)),
            pl.BlockSpec((LE, HD // steps, D), middle),
            pl.BlockSpec((LE, HD // steps, D), middle),
            pl.BlockSpec((128, 128), lambda i: (0, 0)),
            pl.BlockSpec((shard // steps, 2 * HD), rows),
        ]
        + each,
        out_specs=[pl.BlockSpec((T // steps, D), rows), pl.BlockSpec((T // steps, D), rows), sm, pl.BlockSpec((1, 1), lambda i: (0, 0))] + each,
        compiler_params=pltpu.CompilerParams(vmem_limit_bytes=63 * 2**20),
        name="adamw",
    )(lay, tg, msg, f2, f2, fq.reshape(LE, HD, D), fo.reshape(LE, HD, D), side, kvg, *state))
    result[3] = result[3].reshape(())
    for i in range(3):
        result[7 + i] = result[7 + i].T
        result[13 + i] = result[13 + i].transpose(0, 2, 1)
    return tuple(result)


def solution(mesh):
    tok = P(("dp", "expert"), None)
    dp0 = P("dp", None)
    ex0 = P("expert", None, None)
    dp1 = P(None, "dp")
    return jax.shard_map(
        on_device,
        mesh=mesh,
        in_specs=(tok,) * 3 + (P(),) * 8 + (dp0,) * 3 + (ex0,) * 6 + (dp0,) * 3 + (dp1,) * 3,
        out_specs=(tok,) * 2 + (P(),) * 8 + (dp0,) * 3 + (ex0,) * 6 + (dp0,) * 3 + (dp1,) * 3,
        check_vma=False,
    )
```

time: 236 us -> 179 us (0.76)
  local copies, waits for them, and re-layouts: 23.5 us -> 0 us
  other arithmetic: 18.5 us -> 0 us
  Pallas kernels: 190 us -> 178 us
    unnamed x81 -> x0, local copies, waits for them, and re-layouts: 20.9 us -> none
    pallas_call x1 -> x2, Pallas kernels: 190 us -> 178 us  [the longest x1 168 us: on_device(): pl.pallas_call(kernel, out_shape=outs, in_specs=[vm] * 10 + [sm] * 2, out...]
    sub x7 -> x0, other arithmetic: 10.4 us -> none  [adam_update(): weight - step_rate * (first_hat / (jnp.sqrt(second_hat) + ADAM_EPS) + dec...]
    convert_element_type x5 -> x0, other arithmetic: 3.54 us -> none  [the longest x1 1.51 us: on_device(): keyval_weight.astype(BF)]
where the time goes in v2:
time: 179 us
  Pallas kernels  178 us (99%)
    pallas_call x1, Pallas kernels, on_device(): pl.pallas_call(kernel, out_shape=outs, in_specs=[vm] * 10 + [sm] * 2, out...  168 us
    pallas_call x1, Pallas kernels, on_device(): pl.pallas_call(update, grid=(steps,), out_shape=[jax.ShapeDtypeStruct((T,...  10.2 us

profile of v2, /device:TPU:0, one launch (start us, length us, event | category | flops | bytes accessed | tf_op | source)
XLA Modules:
  0.0 178.6 jit_solution(11460623031783360897)
XLA Ops:
  0.7 167.5 %layer.1 = (bf16[512,512]{1,0:T(8,128)(2,1)}, f32[512,512]{1,0:T(8,128)}, f32[32,128]{1,0:T(8,128)}, bf16[2,128,2048]{2,1,0:T(8,128)(2,1)}, bf16[192,512]{1,0:T(...) custom-call(bf16[512,512]{1,0:T(8,128)(2,1)} %refs_0_.1, ...), custom_call_target="tpu_custom_call" | custom-call | tf_op jit(solution)/shard_map/layer/pallas_call | solution.py:965
  168.2 10.2 %adamw.1 = (bf16[512,512]{1,0:T(8,128)(2,1)}, f32[512,512]{1,0:T(8,128)}, s32[24]{0:T(128)}, f32[1,1]{1,0:T(1,128)}, f32[2,512]{1,0:T(2,128)}, /*index=5*/f32[2,...) custom-call(bf16[512,512]{1,0:T(8,128)(2,1)} %get-tuple-element.58.r, ...), custom_call_target="tpu_custom_call" | custom-call | tf_op jit(solution)/shard_map/adamw/pallas_call | solution.py:997

commit v3 on v2

--- a/solution.py
+++ b/solution.py
@@ -30,8 +30,6 @@
 LE = NE // PL
 ER = LE * HD
 HB = FF // 2
-R = 512
-NR = K8 * 128 // R
 
 
 def mm(a, b):
@@ -86,11 +84,13 @@
         nd=((T, D), BF),
         gate=((8, T), F32),
         dgate=((8, T), F32),
-        big=((PL * 256, T), F32),
+        big=((NE * HD, T), F32),
+        peak=((2, 9, 8, 1024), F32),
         at=((NE * HD, T), BF),
         qx=((4, 128, 1024), BF),
         dox=((4, 128, 1024), BF),
-        att=((4, HD, 1024), F32),
+        att=((4, HD + 16, 1024), F32),
+        top=((4, 8, 1024), F32),
         linv=((4, 8, 1024), F32),
         kx=((2, 8, 256, 128), BF),
         vx=((2, 8, 256, 128), BF),
@@ -311,8 +311,6 @@
         s.kvb[slot, p, 128:256, :] = kv1[p * 128 : (p + 1) * 128]
     h_kv = [None] + [rcopy(s.kvb.at[slot], s.kvb.at[slot], chips[m]) for m in (1, 2, 3)]
     h_eq2 = gather_far(h_eq1, s.eq)
-    h_cot = rcopy(cot.at[pl.ds(256, 256)], s.cotx, swap)
-    h_eo1 = rcopy(own_eo, own_eo, near)
 
     rwait(h_tok, s.tokx)
     rwait(h_rt, s.rtx)
@@ -395,10 +393,7 @@
 
     lax.fori_loop(0, 4, choose, 0)
 
-    for i in range(1, dp):
-        rwait(h_wp1[i], w2_rows(zfrom[i], part, WP))
-    h_wp2 = rcopy(w2_cols(part, WP), w2_cols(part, WP), near)
-    h_eo2 = gather_far(h_eo1, s.eo)
+    h_eo1 = rcopy(own_eo, own_eo, near)
     rwait(h_kvs, s.kvb.at[pl.ds((1 - c) * 4, 4)])
     krow = lax.broadcasted_iota(jnp.int32, (256, 128), 0)
     klane = lax.broadcasted_iota(jnp.int32, (256, 128), 1)
@@ -416,63 +411,63 @@
             s.vt[p, t, 0:64, :] = kvt[64:128].astype(BF)
             s.vt[p, t, 64:80, :] = jnp.ones((16, 256), BF)
 
-    tiles = [e + 1, 8 - e]
-    base = [0, e + 1]
-
-    def attend(g, rc):
-        blk, p = g // 2, g % 2
-        nt, first = tiles[blk], base[blk]
-        visible = (
-            lax.broadcasted_iota(jnp.int32, (256, 128), 0)
-            <= lax.broadcasted_iota(jnp.int32, (256, 128), 1) + 128 * blk
-        )
-        visible = jnp.concatenate([visible] * (R // 128), axis=1)
-        ls = slice(rc * R, (rc + 1) * R)
-
-        def scores(t, peak):
-            sc = mm(s.kx[p, t], s.qx[g, :, ls])
-            s.big[pl.ds(pl.multiple_of(t * 256, 256), 256), :] = sc
-            return jnp.maximum(peak, jnp.max(sc.reshape(32, 8, R), axis=0))
-
-        peak = lax.fori_loop(0, nt - 1, scores, jnp.full((8, R), MASKED, F32))
-        sc = jnp.where(visible, mm(s.kx[p, nt - 1], s.qx[g, :, ls]), MASKED)
-        s.big[pl.ds(pl.multiple_of((nt - 1) * 256, 256), 256), :] = sc
-        peak = jnp.maximum(peak, jnp.max(sc.reshape(32, 8, R), axis=0))
-        peak = jnp.max(peak, axis=0, keepdims=True)
-
-        def values(t, acc):
-            pb = jnp.exp2(s.big[pl.ds(pl.multiple_of(t * 256, 256), 256), :] - peak).astype(BF)
-            s.pst[p, first + t, :, ls] = pb
-            return acc + mm(s.vt[p, t], pb)
-
-        acc = lax.fori_loop(0, nt, values, jnp.zeros((HD + 16, R), F32))
-        inv = 1.0 / acc[64:72]
-        s.linv[g, :, ls] = inv
-        s.att[g, :, ls] = acc[0:64] * inv[0:1]
-
-    pieces = [(p + 2 * blk, rc) for p in range(2) for rc in range(NR) for blk in range(2)]
-    for piece in pieces[0:2]:
-        attend(*piece)
+    turn = e + 1
+    below = lax.broadcasted_iota(jnp.int32, (256, 128), 0) - lax.broadcasted_iota(
+        jnp.int32, (256, 128), 1
+    )
+    s.att[...] = jnp.zeros(s.att.shape, F32)
+    s.top[...] = jnp.full(s.top.shape, MASKED, F32)
+
+    def place_of(i):
+        blk = jnp.where(i >= turn, 1, 0)
+        return blk * 2, i - blk * turn
+
+    def attend(i, _):
+        g0_, t = place_of(i)
+        visible = below <= jnp.where(i == turn - 1, 0, jnp.where(i == 8, 128, 256))
+        visible = jnp.concatenate([visible] * K8, axis=1)
+        both_p = range(2)
+        scs = [jnp.where(visible, mm(s.kx[p, t], s.qx[g0_ + p]), MASKED) for p in both_p]
+        tops = [jnp.max(jnp.max(x.reshape(32, 8, 1024), axis=0), axis=0, keepdims=True) for x in scs]
+        olds = [s.top[g0_ + p, 0:1, :] for p in both_p]
+        news = [jnp.maximum(old, jnp.ceil(x)) for old, x in zip(olds, tops)]
+        pbs = [jnp.exp2(sc - new).astype(BF) for sc, new in zip(scs, news)]
+        outs = [mm(s.vt[p, t], pbs[p]) for p in both_p]
+        for p in both_p:
+            s.att[g0_ + p] = s.att[g0_ + p] * jnp.exp2(olds[p] - news[p]) + outs[p]
+            s.pst[p, i] = pbs[p]
+            s.peak[p, i] = jnp.broadcast_to(news[p], (8, 1024))
+            s.top[g0_ + p] = jnp.broadcast_to(news[p], (8, 1024))
+        return 0
+
+    lax.fori_loop(0, 3, attend, 0)
+    h_eo2 = gather_far(h_eo1, s.eo)
+    for i in range(1, dp):
+        rwait(h_wp1[i], w2_rows(zfrom[i], part, WP))
+    h_wp2 = rcopy(w2_cols(part, WP), w2_cols(part, WP), near)
+    lax.fori_loop(3, 5, attend, 0)
     rwait(h_wp2, w2_cols(c * HB + WD + qs[1] * WP, WP))
     both_parts = pl.multiple_of(c * HB + WD + a * 2 * WP, 2 * WP)
     h_wp3 = rcopy(w2_cols(both_parts, 2 * WP), w2_cols(both_parts, 2 * WP), far)
-    for piece in pieces[2:4]:
-        attend(*piece)
+    h_cot = rcopy(cot.at[pl.ds(256, 256)], s.cotx, swap)
+    lax.fori_loop(5, 7, attend, 0)
     h_eos = gather_sib(h_eo2, s.eo)
-    for piece in pieces[4:6]:
-        attend(*piece)
-    rwait(h_wp3, w2_cols(pl.multiple_of(c * HB + WD + (1 - a) * 2 * WP, 2 * WP), 2 * WP))
-    for piece in pieces[6:8]:
-        attend(*piece)
+    lax.fori_loop(7, 9, attend, 0)
+    for g in range(4):
+        inv = 1.0 / s.att[g, 64:72, :]
+        s.linv[g] = inv
+        s.att[g, 0:64, :] = s.att[g, 0:64, :] * inv[0:1]
     for i in range(1, dp):
         rwait(h_wd[i], w2_rows(zfrom[i], lo, WD))
-    h_w2s = rcopy(w2_cols(lo, HB), w2_cols(lo, HB), sib)
-
+    h_w2s = [rcopy(w2_cols(lo, WD), w2_cols(lo, WD), sib)]
+    rwait(h_wp3, w2_cols(pl.multiple_of(c * HB + WD + (1 - a) * 2 * WP, 2 * WP), 2 * WP))
+    rest = pl.multiple_of(lo + WD, WD)
+    h_w2s.append(rcopy(w2_cols(rest, HB - WD), w2_cols(rest, HB - WD), sib))
     def spread(dst, src, scale):
         def one(g, _):
             lanes = pl.ds(pl.multiple_of(g * 128, 128), 128)
             for k in range(K8):
-                part = src[g, :, k * 128 : (k + 1) * 128]
+                part = src[g, 0:HD, k * 128 : (k + 1) * 128]
                 if scale is not None:
                     part = part * scale[k : k + 1, lanes]
                 else:
@@ -512,7 +507,8 @@
     s.cott[:, 0:256] = cot0.T.astype(BF)
     s.cott[:, 256:512] = cot1.T.astype(BF)
     s.acc2[...] = jnp.zeros((T, D), F32)
-    rwait(h_w2s, s.w2.at[:, :, pl.ds(hi, HB)])
+    rwait(h_w2s[0], w2_cols(hi, WD))
+    rwait(h_w2s[1], w2_cols(pl.multiple_of(hi + WD, WD), HB - WD))
 
     FT = 256
 
@@ -651,10 +647,11 @@
         yield
 
     chain = [feed_grad(0), feed_grad(1)]
+    next(chain[0])
+    next(chain[1])
 
     out = s.acc1[...].astype(BF)
     s.layx[...] = mm(join, out[256:512]).astype(BF)
-    h_lay = rcopy(s.layx, s.layr, swap)
     s.ffn[0:256, :] = mm(join, out[0:256]).astype(BF)
 
     def rms_back(dn, gain, unit, inv):
@@ -680,14 +677,13 @@
     chain.append(head_grad(s.go, s.ro1, s.ro2, s.ro3, s.xo, s.ro4, s.fo, foo, 4))
     next(chain[2])
     sent_o = s.half_sent
-    next(chain[0])
 
     def heads_back(g, _):
         lanes = pl.ds(pl.multiple_of(g * 128, 128), 128)
         for k in range(K8):
             ks = slice(k * 128, (k + 1) * 128)
             da = pick(g, k)
-            at = s.att[g, :, ks]
+            at = s.att[g, 0:HD, ks]
             s.dgate[k : k + 1, lanes] = jnp.sum(at * da, axis=0, keepdims=True)
             do = (da * (s.gate[k : k + 1, lanes] * s.linv[g, 0:1, ks])).astype(BF)
             s.dox[g, 64:128, ks] = do
@@ -704,39 +700,34 @@
 
     left = lax.broadcasted_iota(jnp.int32, (256, 128), 1) < 64
 
-    def attend_back(g, rc):
-        blk, p = g // 2, g % 2
-        nt, first = tiles[blk], base[blk]
-        ls = slice(rc * R, (rc + 1) * R)
-
-        def tile(t, acc):
-            prob = s.pst[p, first + t, :, ls]
-            dprob = mm(s.vx[p, t], s.dox[g, :, ls])
-            ds = (prob.astype(F32) * dprob).astype(BF)
-            kpart = mm_nt(ds, s.qx[g, :, ls])
-            vpart = mm_nt(prob, s.dox[g, :, ls])
-            s.dkv[p, t] += jnp.where(left, kpart * LN2, vpart)
-            return acc + mm(s.kt[p, t], ds)
-
-        s.att[g, :, ls] = lax.fori_loop(0, nt, tile, jnp.zeros((HD, R), F32))
-
+    s.att[...] = jnp.zeros(s.att.shape, F32)
+
+    def attend_back(i, _):
+        g0_, t = place_of(i)
+        both_p = range(2)
+        scales = [jnp.exp2(s.peak[p, i, 0:1, :] - s.top[g0_ + p, 0:1, :]) for p in both_p]
+        doxs = [(s.dox[g0_ + p].astype(F32) * scales[p]).astype(BF) for p in both_p]
+        dprobs = [mm(s.vx[p, t], doxs[p]) for p in both_p]
+        vparts = [mm_nt(s.pst[p, i], doxs[p]) for p in both_p]
+        dss = [(s.pst[p, i].astype(F32) * dprobs[p]).astype(BF) for p in both_p]
+        kparts = [mm_nt(dss[p], s.qx[g0_ + p]) for p in both_p]
+        dqs = [mm(s.kt[p, t], dss[p]) for p in both_p]
+        for p in both_p:
+            s.dkv[p, t] += jnp.where(left, kparts[p] * LN2, vparts[p])
+            s.att[g0_ + p, 0:HD, :] += dqs[p]
+        return 0
+
+    next(chain[2])
+    lax.fori_loop(0, 3, attend_back, 0)
+    next(chain[0])
+    lax.fori_loop(3, 5, attend_back, 0)
     next(chain[1])
+    lax.fori_loop(5, 7, attend_back, 0)
     next(chain[2])
-    for piece in pieces[0:2]:
-        attend_back(*piece)
     next(chain[0])
-    for piece in pieces[2:4]:
-        attend_back(*piece)
+    lax.fori_loop(7, 9, attend_back, 0)
     next(chain[1])
-    next(chain[2])
-    for piece in pieces[4:6]:
-        attend_back(*piece)
-    next(chain[0])
-    next(chain[2])
-    for piece in pieces[6:8]:
-        attend_back(*piece)
-    next(chain[1])
-    next(chain[2])
+    h_lay = rcopy(s.layx, s.layr, swap)
     sent(h_kvs)
     for m in (1, 2, 3):
         sent(h_kv[m])
@@ -747,23 +738,24 @@
                 s.kvb[sl, side_, p * 128 : (p + 1) * 128, :] = s.dkv[p, blk // 2, (blk % 2) * 128 : (blk % 2) * 128 + 128, :].astype(BF)
     h_k1 = rcopy(s.kvb.at[pl.ds((1 - c) * 4, 4)], s.rk1, sib)
     spread(s.at, s.att, None)
+    next(chain[0])
     rwait(h_k1, s.rk1)
     for i in range(4):
         s.rk1[i] = both(s.kvb[c * 4 + i], s.rk1[i])
     h_k2 = [None] + [rcopy(s.rk1.at[qs[m]], s.rk2.at[m - 1], chips[m]) for m in (1, 2, 3)]
 
+    next(chain[2])
     sent(sent_o)
-    next(chain[0])
-
-    def query_grad(i, _):
-        rows = pl.ds(pl.multiple_of(i * 256, 256), 256)
+
+    def query_grad(i, start):
+        rows = pl.ds(pl.multiple_of(start + i * 256, 256), 256)
         s.go[rows, :] = mm(s.at[rows, :], s.nd[...]).astype(BF)
-        return 0
-
-    lax.fori_loop(0, NE * HD // 256, query_grad, 0)
+        return start
+
+    lax.fori_loop(0, half // 256, query_grad, (1 - c) * half)
     chain.append(head_grad(s.go, s.rq1, s.rq2, s.rq3, s.xq, s.rq4, s.fq, fqo, 5))
     next(chain[3])
-    next(chain[1])
+    lax.fori_loop(0, half // 256, lambda i, _: query_grad(i, c * half) * 0, 0)
     s.acc2[...] = jnp.zeros((T, D), F32)
 
     def slot_sum(i, _):
@@ -783,6 +775,7 @@
 
     next(chain[3])
     next(chain[0])
+    next(chain[1])
     for m in (1, 2, 3):
         rwait(h_k2[m], s.rk2.at[m - 1])
     for i in range(2):
@@ -802,22 +795,20 @@
     s.tbf[104:128, 512:640] = jnp.zeros((24, 128), F32)
     s.tb[...] = s.tbf[...].astype(BF)
     h_t1 = rcopy(zrows(s.tb, 1 - c, 64), s.rt1, sib)
+    next(chain[0])
+    next(chain[2])
     next(chain[3])
-    next(chain[1])
-
+    rwait(h_t1, s.rt1)
+    s.tsm[...] = both(s.tb[pl.ds(pl.multiple_of(c * 64, 64), 64), :], s.rt1[...])
+    h_t2 = [None] + [rcopy(zrows(s.tsm, qs[m], 16), s.rt2.at[m - 1], chips[m]) for m in (1, 2, 3)]
     grad = s.mixed[...] + back0
     sent(h_lay)
     s.layx[...] = mm(join, grad[256:512].astype(BF)).astype(BF)
-    rwait(h_t1, s.rt1)
-    s.tsm[...] = both(s.tb[pl.ds(pl.multiple_of(c * 64, 64), 64), :], s.rt1[...])
-    h_t2 = [None] + [rcopy(zrows(s.tsm, qs[m], 16), s.rt2.at[m - 1], chips[m]) for m in (1, 2, 3)]
-    h_tg = rcopy(s.layx, s.tgr, swap)
     top = grad[0:256].astype(BF)
     rest = (grad[0:256] - top.astype(F32)).astype(BF)
     s.acc1[0:256, :] = mm(join, top) + mm(join, rest)
-
+    next(chain[1])
     next(chain[3])
-    next(chain[0])
     for m in (1, 2, 3):
         rwait(h_t2[m], s.rt2.at[m - 1])
     total = s.tsm[pl.ds(pl.multiple_of(q * 16, 16), 16), :].astype(F32)
@@ -825,7 +816,7 @@
         total = total + s.rt2[m - 1].astype(F32)
     s.rt3[z] = total.astype(BF)
     h_t3 = [None] + [rcopy(s.rt3.at[z], s.rt3.at[z], zp[i]) for i in range(1, dp)]
-    next(chain[3])
+    h_tg = rcopy(s.layx, s.tgr, swap)
     next(chain[1])
     for i in range(1, dp):
         rwait(h_t3[i], s.rt3.at[zfrom[i]])
@@ -837,6 +828,7 @@
     h_t4 = [None] + [
         rcopy(zrows(s.tf, slot, 16), zrows(s.tf, slot, 16), chips[m]) for m in (1, 2, 3)
     ]
+    next(chain[3])
     sq_t = fold(tail.astype(F32) * tail.astype(F32)) * (1.0 / dp)
 
     total = squares[0]

time: 179 us -> 157 us (0.88)
  Pallas kernels: 178 us -> 156 us
    pallas_call x1, Pallas kernels: 168 us -> 146 us  [on_device(): pl.pallas_call(kernel, out_shape=outs, in_specs=[vm] * 10 + [sm] * 2, out...]
where the time goes in v3:
time: 157 us
  Pallas kernels  156 us (99%)
    pallas_call x1, Pallas kernels, on_device(): pl.pallas_call(kernel, out_shape=outs, in_specs=[vm] * 10 + [sm] * 2, out...  146 us
    pallas_call x1, Pallas kernels, on_device(): pl.pallas_call(update, grid=(steps,), out_shape=[jax.ShapeDtypeStruct((T,...  10.2 us

profile of v3, /device:TPU:0, one launch (start us, length us, event | category | flops | bytes accessed | tf_op | source)
XLA Modules:
  0.0 156.5 jit_solution(16536176841368045988)
XLA Ops:
  0.7 145.5 %layer.1 = (bf16[512,512]{1,0:T(8,128)(2,1)}, f32[512,512]{1,0:T(8,128)}, f32[32,128]{1,0:T(8,128)}, bf16[2,128,2048]{2,1,0:T(8,128)(2,1)}, bf16[192,512]{1,0:T(...) custom-call(bf16[512,512]{1,0:T(8,128)(2,1)} %refs_0_.1, ...), custom_call_target="tpu_custom_call" | custom-call | tf_op jit(solution)/shard_map/layer/pallas_call | solution.py:957
  146.2 10.2 %adamw.1 = (bf16[512,512]{1,0:T(8,128)(2,1)}, f32[512,512]{1,0:T(8,128)}, s32[24]{0:T(128)}, f32[1,1]{1,0:T(1,128)}, f32[2,512]{1,0:T(2,128)}, /*index=5*/f32[2,...) custom-call(bf16[512,512]{1,0:T(8,128)(2,1)} %get-tuple-element.58.r, ...), custom_call_target="tpu_custom_call" | custom-call | tf_op jit(solution)/shard_map/adamw/pallas_call | solution.py:989

commit v4 on v3

--- a/solution.py
+++ b/solution.py
@@ -106,9 +106,13 @@
         gfh=((2, D, HB), BF),
         gfl=((2, D, HB), BF),
         rf1=((2, D, HB), BF),
-        rfa=((2, D, HB // 2), BF),
-        rfb=((2, D, HB // 4), BF),
-        rfc=((dp - 1, 2, shard, HB // 4), BF),
+        rfa=((D, HB // 2), BF),
+        rfb=((D, HB // 4), BF),
+        rfc=((dp - 1, shard, HB // 4), BF),
+        rga=((shard, HB // 2), BF),
+        rgb=((shard, HB // 4), BF),
+        rgc=((dp - 1, shard, HB), BF),
+        rgs=((shard, HB), BF),
         f2=((2, shard, FF), BF),
         go=((NE * HD, D), BF),
         rq1=((NE * HD // 2, D), BF),
@@ -126,7 +130,6 @@
         rk1=((4, 2, 256, 128), BF),
         rk2=((3, 2, 256, 128), BF),
         dkvd=((T, 128), BF),
-        tbf=((128, 640), F32),
         tb=((128, 640), BF),
         rt1=((64, 640), BF),
         tsm=((64, 640), BF),
@@ -140,20 +143,25 @@
         layr=((256, D), BF),
         tgr=((256, D), BF),
         gain=((8, D), F32),
-        osem=(9,),
+        i_cot=((T, D), BF),
+        i_up=((shard, FF), F32),
+        i_down=((FF, shard), F32),
+        i_qw=((LE, HD, D), F32),
+        i_ow=((LE, HD, D), F32),
+        osem=(10,),
         ssem=None,
         rsem=None,
     )
 
 
 def copies_of(dp):
-    return 80 + 12 * dp
+    return 80 + 16 * dp
 
 
 def layer_kernel(dp, *refs):
     shard = D // dp
     pr = piece_rows(dp)
-    (tok, cot, routes, wkv, up, down, qw, ow, rw, gains, gbatch, lens) = refs[:12]
+    (tok, cot_, routes, wkv, up_, down_, qw_, ow_, rw, gains, gbatch, lens) = refs[:12]
     (lay, tg, msgo, f2o, fqo, foo, sideo, kvo) = refs[12:20]
     names = list(scratch_list(dp))
     s = type("Scratch", (), dict(zip(names, refs[20:])))
@@ -218,6 +226,13 @@
         d.start()
         return d
 
+    cot, up, down, qw, ow = s.i_cot, s.i_up, s.i_down, s.i_qw, s.i_ow
+    loads = [
+        lcopy(x, y, k)
+        for k, (x, y) in enumerate(
+            ((up_, up), (down_, down), (qw_, qw), (ow_, ow), (cot_, cot))
+        )
+    ]
     bar = pltpu.get_barrier_semaphore()
     for peer in plane[1:] + zp[1:]:
         pl.semaphore_signal(bar, inc=1, device_id=peer, device_id_type=MESH)
@@ -245,12 +260,8 @@
     WD = HB // 2
     WP = (HB - WD) // 4
     part = pl.multiple_of(c * HB + WD + q * WP, WP)
-    for at, n in ((lo, WD), (part, WP)):
-        s.w2[0, own_rows, pl.ds(at, n)] = up[:, pl.ds(at, n)].astype(BF)
-        s.w2[1, own_rows, pl.ds(at, n)] = turned(down[pl.ds(at, n), :]).astype(BF)
-
-    def w2_rows(i, at, n):
-        return s.w2.at[:, pl.ds(pl.multiple_of(i * shard, shard), shard), pl.ds(at, n)]
+    def w2_rows(w, i, at, n):
+        return s.w2.at[w, pl.ds(pl.multiple_of(i * shard, shard), shard), pl.ds(at, n)]
 
     def to_all_z(ref):
         return [None] + [rcopy(ref, ref, zp[i]) for i in range(1, dp)]
@@ -260,6 +271,8 @@
     ]
     h_tok = rcopy(tok.at[pl.ds(256, 256)], s.tokx, swap)
     h_rt = rcopy(s.rts, s.rtx, swap)
+    loads[2].wait()
+    loads[3].wait()
     for i in range(LE):
         rows = pl.ds(pl.multiple_of(slot * ER + i * HD, HD), HD)
         s.eq[rows, :] = qw[i].astype(BF)
@@ -267,8 +280,15 @@
     own_eq = zrows(s.eq, slot, ER)
     own_eo = zrows(s.eo, slot, ER)
     h_eq1 = rcopy(own_eq, own_eq, near)
-    h_wp1 = to_all_z(w2_rows(z, part, WP))
-    h_wd = to_all_z(w2_rows(z, lo, WD))
+    loads[0].wait()
+    loads[1].wait()
+    for at, n in ((lo, WD), (part, WP)):
+        s.w2[0, own_rows, pl.ds(at, n)] = up[:, pl.ds(at, n)].astype(BF)
+    s.w2[1, own_rows, pl.ds(lo, HB)] = turned(down[pl.ds(lo, HB), :]).astype(BF)
+
+    h_wp1 = to_all_z(w2_rows(0, z, part, WP))
+    h_wu = to_all_z(w2_rows(0, z, lo, WD))
+    h_wd = to_all_z(w2_rows(1, z, lo, HB))
 
     def gather_far(h, ref):
         rwait(h, zrows(ref, c * 4 + qs[1], ER))
@@ -280,8 +300,8 @@
         mine = zrows(ref, c, 4 * ER)
         return rcopy(mine, mine, sib)
 
-    def w2_cols(at, n):
-        return s.w2.at[:, :, pl.ds(at, n)]
+    def w2_cols(w, at, n):
+        return s.w2.at[w, :, pl.ds(at, n)]
 
     s.wrt[0:NE, :] = rw[...]
     s.wrt[NE:32, :] = jnp.zeros((32 - NE, D), F32)
@@ -299,6 +319,7 @@
     n0 = (rms(nat0)[0] * g0).astype(BF)
     n1 = (rms(nat1)[0] * g0).astype(BF)
     s.nd[0:256, :] = n0
+    loads[4].wait()
     cot0 = mm(split, cot[0:256, :])
     s.cotd[0:256, :] = cot0.astype(BF)
 
@@ -309,7 +330,7 @@
     for p in range(2):
         s.kvb[slot, p, 0:128, :] = kv0[p * 128 : (p + 1) * 128]
         s.kvb[slot, p, 128:256, :] = kv1[p * 128 : (p + 1) * 128]
-    h_kv = [None] + [rcopy(s.kvb.at[slot], s.kvb.at[slot], chips[m]) for m in (1, 2, 3)]
+    h_kv1 = rcopy(s.kvb.at[slot], s.kvb.at[slot], near)
     h_eq2 = gather_far(h_eq1, s.eq)
 
     rwait(h_tok, s.tokx)
@@ -365,9 +386,12 @@
     s.cnt[...] = jnp.broadcast_to(jnp.sum(counts, axis=1, keepdims=True), (32, 128))
 
     half = NE * HD // 2
+    rwait(h_kv1, s.kvb.at[c * 4 + qs[1]])
+    kv_pair = s.kvb.at[pl.ds(c * 4 + a * 2, 2)]
+    h_kv2 = rcopy(kv_pair, kv_pair, far)
     h_eqs = gather_sib(h_eq2, s.eq)
-    for m in (1, 2, 3):
-        rwait(h_kv[m], s.kvb.at[c * 4 + qs[m]])
+    rwait(h_kv2, s.kvb.at[pl.ds(c * 4 + (1 - a) * 2, 2)])
+    h_eo1 = rcopy(own_eo, own_eo, near)
     h_kvs = rcopy(s.kvb.at[pl.ds(c * 4, 4)], s.kvb.at[pl.ds(c * 4, 4)], sib)
     rwait(h_eqs, zrows(s.eq, 1 - c, half))
 
@@ -393,7 +417,6 @@
 
     lax.fori_loop(0, 4, choose, 0)
 
-    h_eo1 = rcopy(own_eo, own_eo, near)
     rwait(h_kvs, s.kvb.at[pl.ds((1 - c) * 4, 4)])
     krow = lax.broadcasted_iota(jnp.int32, (256, 128), 0)
     klane = lax.broadcasted_iota(jnp.int32, (256, 128), 1)
@@ -440,16 +463,16 @@
             s.top[g0_ + p] = jnp.broadcast_to(news[p], (8, 1024))
         return 0
 
+    h_eo2 = gather_far(h_eo1, s.eo)
     lax.fori_loop(0, 3, attend, 0)
-    h_eo2 = gather_far(h_eo1, s.eo)
     for i in range(1, dp):
-        rwait(h_wp1[i], w2_rows(zfrom[i], part, WP))
-    h_wp2 = rcopy(w2_cols(part, WP), w2_cols(part, WP), near)
+        rwait(h_wp1[i], w2_rows(0, zfrom[i], part, WP))
+    h_wp2 = rcopy(w2_cols(0, part, WP), w2_cols(0, part, WP), near)
+    h_cot = rcopy(cot.at[pl.ds(256, 256)], s.cotx, swap)
     lax.fori_loop(3, 5, attend, 0)
-    rwait(h_wp2, w2_cols(c * HB + WD + qs[1] * WP, WP))
+    rwait(h_wp2, w2_cols(0, c * HB + WD + qs[1] * WP, WP))
     both_parts = pl.multiple_of(c * HB + WD + a * 2 * WP, 2 * WP)
-    h_wp3 = rcopy(w2_cols(both_parts, 2 * WP), w2_cols(both_parts, 2 * WP), far)
-    h_cot = rcopy(cot.at[pl.ds(256, 256)], s.cotx, swap)
+    h_wp3 = rcopy(w2_cols(0, both_parts, 2 * WP), w2_cols(0, both_parts, 2 * WP), far)
     lax.fori_loop(5, 7, attend, 0)
     h_eos = gather_sib(h_eo2, s.eo)
     lax.fori_loop(7, 9, attend, 0)
@@ -457,12 +480,10 @@
         inv = 1.0 / s.att[g, 64:72, :]
         s.linv[g] = inv
         s.att[g, 0:64, :] = s.att[g, 0:64, :] * inv[0:1]
+    rwait(h_wp3, w2_cols(0, pl.multiple_of(c * HB + WD + (1 - a) * 2 * WP, 2 * WP), 2 * WP))
     for i in range(1, dp):
-        rwait(h_wd[i], w2_rows(zfrom[i], lo, WD))
-    h_w2s = [rcopy(w2_cols(lo, WD), w2_cols(lo, WD), sib)]
-    rwait(h_wp3, w2_cols(pl.multiple_of(c * HB + WD + (1 - a) * 2 * WP, 2 * WP), 2 * WP))
-    rest = pl.multiple_of(lo + WD, WD)
-    h_w2s.append(rcopy(w2_cols(rest, HB - WD), w2_cols(rest, HB - WD), sib))
+        rwait(h_wu[i], w2_rows(0, zfrom[i], lo, WD))
+    h_w2s = [rcopy(w2_cols(0, lo, HB), w2_cols(0, lo, HB), sib)]
     def spread(dst, src, scale):
         def one(g, _):
             lanes = pl.ds(pl.multiple_of(g * 128, 128), 128)
@@ -487,6 +508,9 @@
         lax.fori_loop(0, 4, one, 0)
 
     spread(s.at, s.att, s.gate)
+    for i in range(1, dp):
+        rwait(h_wd[i], w2_rows(1, zfrom[i], lo, HB))
+    h_w2s.append(rcopy(w2_cols(1, lo, HB), w2_cols(1, lo, HB), sib))
     rwait(h_eos, zrows(s.eo, 1 - c, half))
     s.acc1[...] = s.tokd[...].astype(F32)
 
@@ -507,14 +531,14 @@
     s.cott[:, 0:256] = cot0.T.astype(BF)
     s.cott[:, 256:512] = cot1.T.astype(BF)
     s.acc2[...] = jnp.zeros((T, D), F32)
-    rwait(h_w2s[0], w2_cols(hi, WD))
-    rwait(h_w2s[1], w2_cols(pl.multiple_of(hi + WD, WD), HB - WD))
+    for w in range(2):
+        rwait(h_w2s[w], w2_cols(w, hi, HB))
 
     FT = 256
 
-    def feed(i, base_, keep):
-        cols = pl.ds(pl.multiple_of(base_ + i * FT, FT), FT)
-        part_cols = pl.ds(pl.multiple_of(i * FT, FT), FT)
+    def feed(i, base_, at, keep):
+        cols = pl.ds(pl.multiple_of(base_ + at + i * FT, FT), FT)
+        part_cols = pl.ds(pl.multiple_of(at + i * FT, FT), FT)
         up = mm(s.ffn[...], s.w2[0, :, cols])
         sq = up * up
         th = jnp.tanh(0.79788456 * up * (1.0 + 0.044715 * sq))
@@ -529,10 +553,6 @@
         s.acc2[...] += mm_nt(dup, s.w2[0, :, cols])
         return 0
 
-    lax.fori_loop(0, HB // FT, lambda i, _: feed(i, hi, s.gfh), 0)
-    h_f1 = [rcopy(s.gfh.at[w], s.rf1.at[w], sib) for w in range(2)]
-    lax.fori_loop(0, HB // FT, lambda i, _: feed(i, lo, s.gfl), 0)
-
     def both(x, y):
         return (x.astype(F32) + y.astype(F32)).astype(BF)
 
@@ -552,17 +572,17 @@
     place1 = pl.multiple_of(c * HB + keep1, quart)
 
     def feed_grad(w):
-        own, total, one, two, three, out = (
-            s.gfl.at[w], s.rf1.at[w], s.rfa.at[w], s.rfb.at[w], s.rfc, s.f2.at[w],
-        )
-
-        def pair(at, n):
-            total[:, pl.ds(at, n)] = both(own[:, pl.ds(at, n)], total[:, pl.ds(at, n)])
-
-        rwait(h_f1[w], total)
-        pair(give2, 2 * quart)
+        own, total, one, two, three = s.gfl.at[w], s.rf1.at[w], s.rfa, s.rfb, s.rfc
+
+        def pair(j, at):
+            cols = pl.ds(at, 2 * quart)
+            rwait(h_f1[j][w], total.at[:, cols])
+            total[:, cols] = both(own[:, cols], total[:, cols])
+
+        pair(0, give2)
         h = rcopy(total.at[:, pl.ds(give2, 2 * quart)], one, far)
-        pair(keep2, 2 * quart)
+        yield
+        pair(1, keep2)
         yield
         rwait(h, one)
         for at in (give1, keep1):
@@ -579,12 +599,16 @@
         def zpart(i):
             return total.at[pl.ds(pl.multiple_of(i * shard, shard), shard), pl.ds(keep1, quart)]
 
-        hz = [rcopy(zpart(zp[i][0]), three.at[i - 1, w], zp[i]) for i in range(1, dp)]
+        hz = [rcopy(zpart(zp[i][0]), three.at[i - 1], zp[i]) for i in range(1, dp)]
         yield
         acc = zpart(z)[...].astype(F32)
         for i in range(1, dp):
-            rwait(hz[i - 1], three.at[i - 1, w])
-            acc = acc + three[i - 1, w].astype(F32)
+            rwait(hz[i - 1], three.at[i - 1])
+            acc = acc + three[i - 1].astype(F32)
+        yield from spread_grad(w, acc)
+
+    def spread_grad(w, acc):
+        out = s.f2.at[w]
         acc = acc.astype(BF)
         out[:, pl.ds(place1, quart)] = acc
         acc = acc.astype(F32)
@@ -601,6 +625,33 @@
         rwait(h, out.at[:, pl.ds(hi, HB)])
         done.append(lcopy(out, f2o.at[w], 2 + w))
         yield
+
+    def dp_first_grad(w):
+        own, total, one, two, three = s.gfl.at[w], s.rf1.at[w], s.rga, s.rgb, s.rgc
+        hz = []
+        for j, at in ((0, give2), (1, keep2)):
+            cols = pl.ds(at, 2 * quart)
+            rwait(h_f1[j][w], total.at[:, cols])
+            total[:, cols] = both(own[:, cols], total[:, cols])
+            for i in range(1, dp):
+                mine = pl.ds(pl.multiple_of(zp[i][0] * shard, shard), shard)
+                hz.append((rcopy(total.at[mine, cols], three.at[i - 1, :, cols], zp[i]), i, cols))
+            yield
+        for h, i, cols in hz:
+            rwait(h, three.at[i - 1, :, cols])
+        acc = total[own_rows, :].astype(F32)
+        for i in range(1, dp):
+            acc = acc + three[i - 1].astype(F32)
+        s.rgs[...] = acc.astype(BF)
+        h = rcopy(s.rgs.at[:, pl.ds(give2, 2 * quart)], one, far)
+        yield
+        rwait(h, one)
+        s.rgs[:, pl.ds(keep2, 2 * quart)] = both(s.rgs[:, pl.ds(keep2, 2 * quart)], one[...])
+        h = rcopy(s.rgs.at[:, pl.ds(give1, quart)], two, near)
+        yield
+        rwait(h, two)
+        acc = s.rgs[:, pl.ds(keep1, quart)].astype(F32) + two[...].astype(F32)
+        yield from spread_grad(w, acc)
 
     def head_grad(src, total, one, two, full, part_, final, dst, sem):
         h = rcopy(zrows(src, 1 - c, half), total, sib)
@@ -627,7 +678,7 @@
         rwait(h, two)
         full[0:ER, :] = both(total[pl.ds(pl.multiple_of(q * ER, ER), ER), :], two[...])
         if dp * pr > ER:
-            full[ER:, :] = jnp.zeros((dp * pr - ER, D), BF)
+            full[ER:, :] = jnp.zeros((dp * pr - ER, full.shape[1]), BF)
         hz = [rcopy(zrows(full, zp[i][0], pr), part_.at[i - 1], zp[i]) for i in range(1, dp)]
         yield
         mine = pl.ds(pl.multiple_of(z * pr, pr), pr)
@@ -646,7 +697,24 @@
         done.append(lcopy(final.at[pl.ds(0, ER)], dst, sem))
         yield
 
-    chain = [feed_grad(0), feed_grad(1)]
+    def feed_tiles(base_, at, keep):
+        lax.fori_loop(0, HB // FT // 2, lambda i, _: feed(i, base_, at, keep), 0)
+
+    def to_sibling(at):
+        cols = pl.ds(at, 2 * quart)
+        return [rcopy(s.gfh.at[w, :, cols], s.rf1.at[w, :, cols], sib) for w in range(2)]
+
+    sib_give2 = pl.multiple_of((1 - b) * 2 * quart, 2 * quart)
+    sib_keep2 = pl.multiple_of(b * 2 * quart, 2 * quart)
+    feed_tiles(hi, sib_give2, s.gfh)
+    h_f1 = [to_sibling(sib_give2)]
+    feed_tiles(lo, give2, s.gfl)
+    chain = [feed_grad(0), dp_first_grad(1)]
+    next(chain[0])
+    next(chain[1])
+    feed_tiles(hi, sib_keep2, s.gfh)
+    h_f1.append(to_sibling(sib_keep2))
+    feed_tiles(lo, keep2, s.gfl)
     next(chain[0])
     next(chain[1])
 
@@ -721,16 +789,14 @@
     lax.fori_loop(0, 3, attend_back, 0)
     next(chain[0])
     lax.fori_loop(3, 5, attend_back, 0)
-    next(chain[1])
+    next(chain[2])
     lax.fori_loop(5, 7, attend_back, 0)
-    next(chain[2])
     next(chain[0])
     lax.fori_loop(7, 9, attend_back, 0)
-    next(chain[1])
+    next(chain[2])
     h_lay = rcopy(s.layx, s.layr, swap)
-    sent(h_kvs)
-    for m in (1, 2, 3):
-        sent(h_kv[m])
+    for h in (h_kv1, h_kv2, h_kvs):
+        sent(h)
     for dev in range(PL):
         sl = slot_of(dev)
         for side_, blk in enumerate((2 * dev, 15 - 2 * dev)):
@@ -738,24 +804,30 @@
                 s.kvb[sl, side_, p * 128 : (p + 1) * 128, :] = s.dkv[p, blk // 2, (blk % 2) * 128 : (blk % 2) * 128 + 128, :].astype(BF)
     h_k1 = rcopy(s.kvb.at[pl.ds((1 - c) * 4, 4)], s.rk1, sib)
     spread(s.at, s.att, None)
-    next(chain[0])
-    rwait(h_k1, s.rk1)
-    for i in range(4):
-        s.rk1[i] = both(s.kvb[c * 4 + i], s.rk1[i])
-    h_k2 = [None] + [rcopy(s.rk1.at[qs[m]], s.rk2.at[m - 1], chips[m]) for m in (1, 2, 3)]
-
-    next(chain[2])
     sent(sent_o)
 
-    def query_grad(i, start):
-        rows = pl.ds(pl.multiple_of(start + i * 256, 256), 256)
-        s.go[rows, :] = mm(s.at[rows, :], s.nd[...]).astype(BF)
-        return start
-
-    lax.fori_loop(0, half // 256, query_grad, (1 - c) * half)
-    chain.append(head_grad(s.go, s.rq1, s.rq2, s.rq3, s.xq, s.rq4, s.fq, fqo, 5))
-    next(chain[3])
-    lax.fori_loop(0, half // 256, lambda i, _: query_grad(i, c * half) * 0, 0)
+    def query_grad(i, cols):
+        rows = pl.ds(pl.multiple_of(i * 256, 256), 256)
+        s.go[rows, cols] = mm(s.at[rows, :], s.nd[:, cols]).astype(BF)
+        return 0
+
+    for j in range(2):
+        cols = pl.ds(j * 256, 256)
+        lax.fori_loop(0, NE * HD // 256, lambda i, _: query_grad(i, cols), 0)
+        chain.append(
+            head_grad(
+                *[x.at[:, cols] for x in (s.go, s.rq1, s.rq2, s.rq3, s.xq)],
+                s.rq4.at[:, :, cols], s.fq.at[:, cols], fqo.at[:, cols], 5 + 4 * j,
+            )
+        )
+        next(chain[3 + j])
+        if j == 0:
+            rwait(h_k1, s.rk1)
+            for i in range(4):
+                s.rk1[i] = both(s.kvb[c * 4 + i], s.rk1[i])
+            h_k2 = [None] + [
+                rcopy(s.rk1.at[qs[m]], s.rk2.at[m - 1], chips[m]) for m in (1, 2, 3)
+            ]
     s.acc2[...] = jnp.zeros((T, D), F32)
 
     def slot_sum(i, _):
@@ -774,8 +846,9 @@
     grt = mm(dlog, s.nd[...])
 
     next(chain[3])
+    next(chain[4])
+    next(chain[1])
     next(chain[0])
-    next(chain[1])
     for m in (1, 2, 3):
         rwait(h_k2[m], s.rk2.at[m - 1])
     for i in range(2):
@@ -786,18 +859,21 @@
     dn = s.acc2[...] + mm_nt(s.dkvd[...], s.wkvf[...])
     unit0, inv0 = rms(s.tokd[...].astype(F32))
     back0, gain0 = rms_back(dn, g0, unit0, inv0)
-    s.tbf[:, 0:512] = mm_tn(s.dkvd[...], s.nd[...])
+    s.tb[:, 0:512] = mm_tn(s.dkvd[...], s.nd[...]).astype(BF)
+    side = s.acc1.at[pl.ds(0, 128), pl.ds(0, 128)]
     for j in range(4):
         js = slice(j * 128, (j + 1) * 128)
-        s.tbf[j * 24 : (j + 1) * 24, 512:640] = grt[0:24, js]
-        s.tbf[96 + j : 97 + j, 512:640] = gain0[:, js]
-        s.tbf[100 + j : 101 + j, 512:640] = s.gain[1:2, js]
-    s.tbf[104:128, 512:640] = jnp.zeros((24, 128), F32)
-    s.tb[...] = s.tbf[...].astype(BF)
+        side[j * 24 : (j + 1) * 24, :] = grt[0:24, js]
+        side[96 + j : 97 + j, :] = gain0[:, js]
+        side[100 + j : 101 + j, :] = s.gain[1:2, js]
+    side[104:128, :] = jnp.zeros((24, 128), F32)
+    s.tb[:, 512:640] = side[...].astype(BF)
     h_t1 = rcopy(zrows(s.tb, 1 - c, 64), s.rt1, sib)
+    next(chain[1])
     next(chain[0])
     next(chain[2])
     next(chain[3])
+    next(chain[4])
     rwait(h_t1, s.rt1)
     s.tsm[...] = both(s.tb[pl.ds(pl.multiple_of(c * 64, 64), 64), :], s.rt1[...])
     h_t2 = [None] + [rcopy(zrows(s.tsm, qs[m], 16), s.rt2.at[m - 1], chips[m]) for m in (1, 2, 3)]
@@ -809,6 +885,8 @@
     s.acc1[0:256, :] = mm(join, top) + mm(join, rest)
     next(chain[1])
     next(chain[3])
+    next(chain[4])
+    next(chain[0])
     for m in (1, 2, 3):
         rwait(h_t2[m], s.rt2.at[m - 1])
     total = s.tsm[pl.ds(pl.multiple_of(q * 16, 16), 16), :].astype(F32)
@@ -829,6 +907,7 @@
         rcopy(zrows(s.tf, slot, 16), zrows(s.tf, slot, 16), chips[m]) for m in (1, 2, 3)
     ]
     next(chain[3])
+    next(chain[4])
     sq_t = fold(tail.astype(F32) * tail.astype(F32)) * (1.0 / dp)
 
     total = squares[0]
@@ -840,6 +919,7 @@
 
     for m in (1, 2, 3):
         rwait(h_t4[m], zrows(s.tf, c * 4 + qs[m], 16))
+    next(chain[1])
     h_t5 = rcopy(zrows(s.tf, c, 64), zrows(s.tf, c, 64), sib)
 
     for i in range(1, dp):
@@ -864,6 +944,7 @@
     done.append(lcopy(s.acc2.at[own_rows, pl.ds(0, 128)], kvo, 7))
     next(chain[2])
     next(chain[3])
+    next(chain[4])
     for i in range(1, PL):
         rwait(h_m2[i], s.mq.at[(e + PL - i) % PL])
     total = s.mq[0]
@@ -957,7 +1038,7 @@
     lay, tg, msg, f2, fq, fo, side, kvg = pl.pallas_call(
         kernel,
         out_shape=outs,
-        in_specs=[vm] * 10 + [sm] * 2,
+        in_specs=[vm, hbm, vm, vm, hbm, hbm, hbm, hbm, vm, vm, sm, sm],
         out_specs=[hbm] * len(outs),
         scratch_shapes=scr,
         compiler_params=pltpu.CompilerParams(
@@ -969,7 +1050,7 @@
         group_batch, seq_lengths,
     )
 
-    steps = min(4, shard // 16)
+    steps = 2
     rows = lambda i: (i, 0)
     middle = lambda i: (0, i, 0)
     blocks = [

time: 157 us -> 143 us (0.911)
  Pallas kernels: 156 us -> 142 us
    pallas_call x1, Pallas kernels: 146 us -> 133 us  [on_device(): pl.pallas_call(kernel, out_shape=outs, in_specs=[vm, hbm, vm, vm, hbm, hb...]
where the time goes in v4:
time: 143 us
  Pallas kernels  142 us (99%)
    pallas_call x1, Pallas kernels, on_device(): pl.pallas_call(kernel, out_shape=outs, in_specs=[vm, hbm, vm, vm, hbm, hb...  133 us
    pallas_call x1, Pallas kernels, on_device(): pl.pallas_call(update, grid=(steps,), out_shape=[jax.ShapeDtypeStruct((T,...  9.41 us

profile of v4, /device:TPU:0, one launch (start us, length us, event | category | flops | bytes accessed | tf_op | source)
XLA Modules:
  0.0 143.2 jit_solution(4858854498882187212)
XLA Ops:
  0.7 133.0 %layer.1 = (bf16[512,512]{1,0:T(8,128)(2,1)}, f32[512,512]{1,0:T(8,128)}, f32[32,128]{1,0:T(8,128)}, bf16[2,128,2048]{2,1,0:T(8,128)(2,1)}, bf16[192,512]{1,0:T(...) custom-call(bf16[512,512]{1,0:T(8,128)(2,1)} %refs_0_.1, ...), custom_call_target="tpu_custom_call" | custom-call | tf_op jit(solution)/shard_map/layer/pallas_call | solution.py:1038
  133.7 9.4 %adamw.1 = (bf16[512,512]{1,0:T(8,128)(2,1)}, f32[512,512]{1,0:T(8,128)}, s32[24]{0:T(128)}, f32[1,1]{1,0:T(1,128)}, f32[2,512]{1,0:T(2,128)}, /*index=5*/f32[2,...) custom-call(bf16[512,512]{1,0:T(8,128)(2,1)} %get-tuple-element.58.r, ...), custom_call_target="tpu_custom_call" | custom-call | tf_op jit(solution)/shard_map/adamw/pallas_call | solution.py:1070

commit v5 on v4

--- a/solution.py
+++ b/solution.py
@@ -869,14 +869,14 @@
     side[104:128, :] = jnp.zeros((24, 128), F32)
     s.tb[:, 512:640] = side[...].astype(BF)
     h_t1 = rcopy(zrows(s.tb, 1 - c, 64), s.rt1, sib)
-    next(chain[1])
-    next(chain[0])
-    next(chain[2])
     next(chain[3])
     next(chain[4])
     rwait(h_t1, s.rt1)
     s.tsm[...] = both(s.tb[pl.ds(pl.multiple_of(c * 64, 64), 64), :], s.rt1[...])
     h_t2 = [None] + [rcopy(zrows(s.tsm, qs[m], 16), s.rt2.at[m - 1], chips[m]) for m in (1, 2, 3)]
+    next(chain[1])
+    next(chain[0])
+    next(chain[2])
     grad = s.mixed[...] + back0
     sent(h_lay)
     s.layx[...] = mm(join, grad[256:512].astype(BF)).astype(BF)

time: 143 us -> 145 us (1.014)
  Pallas kernels: 142 us -> 144 us
where the time goes in v5:
time: 145 us; the launch traced here: 144 us
  Pallas kernels  144 us (99%)
    pallas_call x1, Pallas kernels, on_device(): pl.pallas_call(kernel, out_shape=outs, in_specs=[vm, hbm, vm, vm, hbm, hb...  134 us
    pallas_call x1, Pallas kernels, on_device(): pl.pallas_call(update, grid=(steps,), out_shape=[jax.ShapeDtypeStruct((T,...  9.41 us

profile of v5, /device:TPU:0, one launch (start us, length us, event | category | flops | bytes accessed | tf_op | source)
XLA Modules:
  0.0 144.5 jit_solution(7706674321710840111)
XLA Ops:
  0.7 134.2 %layer.1 = (bf16[512,512]{1,0:T(8,128)(2,1)}, f32[512,512]{1,0:T(8,128)}, f32[32,128]{1,0:T(8,128)}, bf16[2,128,2048]{2,1,0:T(8,128)(2,1)}, bf16[192,512]{1,0:T(...) custom-call(bf16[512,512]{1,0:T(8,128)(2,1)} %refs_0_.1, ...), custom_call_target="tpu_custom_call" | custom-call | tf_op jit(solution)/shard_map/layer/pallas_call | solution.py:1038
  134.9 9.4 %adamw.1 = (bf16[512,512]{1,0:T(8,128)(2,1)}, f32[512,512]{1,0:T(8,128)}, s32[24]{0:T(128)}, f32[1,1]{1,0:T(1,128)}, f32[2,512]{1,0:T(2,128)}, /*index=5*/f32[2,...) custom-call(bf16[512,512]{1,0:T(8,128)(2,1)} %get-tuple-element.58.r, ...), custom_call_target="tpu_custom_call" | custom-call | tf_op jit(solution)/shard_map/adamw/pallas_call | solution.py:1070

commit v6 on v4

--- a/solution.py
+++ b/solution.py
@@ -508,9 +508,6 @@
         lax.fori_loop(0, 4, one, 0)
 
     spread(s.at, s.att, s.gate)
-    for i in range(1, dp):
-        rwait(h_wd[i], w2_rows(1, zfrom[i], lo, HB))
-    h_w2s.append(rcopy(w2_cols(1, lo, HB), w2_cols(1, lo, HB), sib))
     rwait(h_eos, zrows(s.eo, 1 - c, half))
     s.acc1[...] = s.tokd[...].astype(F32)
 
@@ -520,6 +517,9 @@
         return 0
 
     lax.fori_loop(0, NE * HD // 256, mix, 0)
+    for i in range(1, dp):
+        rwait(h_wd[i], w2_rows(1, zfrom[i], lo, HB))
+    h_w2s.append(rcopy(w2_cols(1, lo, HB), w2_cols(1, lo, HB), sib))
     mixed = s.acc1[...]
     s.mixed[...] = mixed
     ffn = rms(mixed)[0] * g1

time: 143 us -> 145 us (1.014)
  Pallas kernels: 142 us -> 144 us
    pallas_call x1, Pallas kernels: 133 us -> 135 us  [on_device(): pl.pallas_call(kernel, out_shape=outs, in_specs=[vm, hbm, vm, vm, hbm, hb...]
where the time goes in v6:
time: 145 us
  Pallas kernels  144 us (99%)
    pallas_call x1, Pallas kernels, on_device(): pl.pallas_call(kernel, out_shape=outs, in_specs=[vm, hbm, vm, vm, hbm, hb...  135 us
    pallas_call x1, Pallas kernels, on_device(): pl.pallas_call(update, grid=(steps,), out_shape=[jax.ShapeDtypeStruct((T,...  9.41 us

profile of v6, /device:TPU:0, one launch (start us, length us, event | category | flops | bytes accessed | tf_op | source)
XLA Modules:
  0.0 145.0 jit_solution(17857261511412694655)
XLA Ops:
  0.7 134.8 %layer.1 = (bf16[512,512]{1,0:T(8,128)(2,1)}, f32[512,512]{1,0:T(8,128)}, f32[32,128]{1,0:T(8,128)}, bf16[2,128,2048]{2,1,0:T(8,128)(2,1)}, bf16[192,512]{1,0:T(...) custom-call(bf16[512,512]{1,0:T(8,128)(2,1)} %refs_0_.1, ...), custom_call_target="tpu_custom_call" | custom-call | tf_op jit(solution)/shard_map/layer/pallas_call | solution.py:1038
  135.4 9.4 %adamw.1 = (bf16[512,512]{1,0:T(8,128)(2,1)}, f32[512,512]{1,0:T(8,128)}, s32[24]{0:T(128)}, f32[1,1]{1,0:T(1,128)}, f32[2,512]{1,0:T(2,128)}, /*index=5*/f32[2,...) custom-call(bf16[512,512]{1,0:T(8,128)(2,1)} %get-tuple-element.58.r, ...), custom_call_target="tpu_custom_call" | custom-call | tf_op jit(solution)/shard_map/adamw/pallas_call | solution.py:1070
